TPU v7x, 32 devices: a whole 2x2x4 slice. The times are simulated.
32 devices in a mesh: ctx: 16 (over z, y, x), tp: 2 (over core).
Axes of the slice: x: 2, y: 2, z: 4, core: 2. Of those that a mesh axis runs over, the one named last changes fastest.
Arguments:
- queries: bfloat16 [2048, 64, 128], P(('ctx', 'tp')), may hold values from -24 to 24
- rotated_key_rows: bfloat16 [2048, 8, 128], P(('ctx', 'tp')), may hold values from -24 to 24
- unscaled_value_rows: bfloat16 [2048, 8, 128], P(('ctx', 'tp')), may hold values from -6 to 6
- key_block_scales: bfloat16 [16, 8], P('ctx', 'tp'), may hold values from 0.5 to 2
- value_block_scales: bfloat16 [16, 8], P('ctx', 'tp'), may hold values from 0.5 to 2
- doc_lengths: int32 [16], replicated, may hold values from 1 to 512, 2048 in all
Outputs:
- attended: bfloat16 [2048, 64, 128], P(('ctx', 'tp'))
Inputs may be any that keep to these rules, and one draw needn't show every extreme that they name: `doc_lengths`: they sum to 2048; the longest is exactly 512.
All inputs are finite; a program needn't handle non-finite values.
Results may differ from a plain program's by a relative error of at most 0.0035.
Values may be sent and summed in bfloat16 or wider, within the bound.
No kernel may reach another device: no remote copies, remote signals or barrier semaphores. Data moves between devices by JAX's collectives and lax.ppermute only.
A program may use at most 64 MiB of HBM per device.

v0:
```python
import math

import jax
import jax.numpy as jnp
from jax import lax
from jax.sharding import PartitionSpec as P


def passed_along(value, axis, steps):
    count = lax.axis_size(axis)
    leading, last = (max(0, -steps), min(count, count - steps))
    return lax.ppermute(value, axis, [(source, source + steps) for source in range(leading, last)])


def document_of(positions, ends):
    return jnp.sum((positions[:, None] >= ends[None, :]).astype(jnp.int32), axis=1)


def shards(
    queries,
    rotated_key_rows,
    unscaled_value_rows,
    key_block_scales,
    value_block_scales,
    doc_lengths,
):
    query_rows, key_vectors, value_vectors = (
        lax.all_to_all(queries, "tp", split_axis=1, concat_axis=0, tiled=True),
        lax.all_to_all(rotated_key_rows, "tp", split_axis=1, concat_axis=0, tiled=True),
        lax.all_to_all(unscaled_value_rows, "tp", split_axis=1, concat_axis=0, tiled=True),
    )
    tokens_here = query_rows.shape[0]
    kv_local = key_vectors.shape[1]
    heads_local = query_rows.shape[1]
    query_group = heads_local // kv_local
    head_size = query_rows.shape[2]
    block_index = tokens_here // key_block_scales.shape[0]
    key_scale = jnp.repeat(key_block_scales, block_index, axis=0)
    value_scale = jnp.repeat(value_block_scales, block_index, axis=0)
    here = lax.axis_index("ctx")
    base = here * tokens_here
    ends = jnp.cumsum(doc_lengths)
    offsets = jnp.arange(tokens_here, dtype=jnp.int32)
    q_pos = base + offsets
    q_doc = document_of(q_pos, ends)
    grouped = query_rows.reshape(tokens_here, kv_local, query_group, head_size)
    reach = min(4, lax.axis_size("ctx") // 2)

    def attend(carry, pieces, back):
        k_part, v_part, k_scl, v_scl = pieces
        k_pos = base - back * tokens_here + offsets
        k_doc = document_of(k_pos, ends)
        allowed = (
            (k_doc[None, :] == q_doc[:, None])
            & (k_pos[None, :] <= q_pos[:, None])
            & (k_pos[None, :] >= 0)
        )
        mask_four = allowed[:, None, None, :]
        top, total, summed = carry
        scores = jnp.einsum("qkgd,jkd->qkgj", grouped, k_part, preferred_element_type=jnp.float32)
        scores = scores / math.sqrt(head_size) * k_scl.astype(jnp.float32).T[None, :, None, :]
        scores = jnp.where(mask_four, scores, -1e30)
        new_top = jnp.maximum(top, jnp.max(scores, axis=3))
        factor = jnp.exp(top - new_top)
        expo = jnp.where(mask_four, jnp.exp(scores - new_top[..., None]), 0.0)
        new_total = total * factor + jnp.sum(expo, axis=3)
        weights = (expo * v_scl.astype(jnp.float32).T[None, :, None, :]).astype(jnp.bfloat16)
        added = jnp.einsum("qkgj,jkd->qkgd", weights, v_part, preferred_element_type=jnp.float32)
        return (new_top, new_total, summed * factor[..., None] + added)

    carry = (
        jnp.full((tokens_here, kv_local, query_group), -1e30, jnp.float32),
        jnp.zeros((tokens_here, kv_local, query_group), jnp.float32),
        jnp.zeros((tokens_here, kv_local, query_group, head_size), jnp.float32),
    )
    local_part = (key_vectors, value_vectors, key_scale, value_scale)
    carry = attend(carry, local_part, 0)
    moving = local_part
    for back in range(1, reach + 1):
        moving = passed_along((moving[0], moving[1], moving[2], moving[3]), "ctx", 1)
        carry = attend(carry, moving, back)
    top, total, summed = carry
    result = (
        (summed / total[..., None])
        .reshape(tokens_here, heads_local, head_size)
        .astype(jnp.bfloat16)
    )
    return lax.all_to_all(result, "tp", split_axis=0, concat_axis=1, tiled=True)


def solution(mesh):
    return jax.shard_map(
        shards,
        mesh=mesh,
        in_specs=(
            P(("ctx", "tp"), None, None),
            P(("ctx", "tp"), None, None),
            P(("ctx", "tp"), None, None),
            P("ctx", "tp"),
            P("ctx", "tp"),
            P(),
        ),
        out_specs=P(("ctx", "tp"), None, None),
        check_vma=False,
    )
```

profile of v0, /device:TPU:9, one launch (start us, length us, event | category | flops | bytes accessed | tf_op | source)
XLA Modules:
  0.0 101.7 jit_solution(1131820641784648389)
XLA Ops:
  0.7 3.1 %collective-permute-start.1 = (bf16[128,4]{0,1:T(4,128)(2,1)S(1)}, bf16[128,4]{0,1:T(4,128)(2,1)S(1)}, u32[]{:S(2)}, u32[]{:S(2)}) collective-permute-start(bf16[128,4]{0,1:T(4,128)(2,1)S(1)} %reshape.501), channel_id=1, source_target_pairs={{0,2},{2,4},{4,6},{6,8},{8,10},{10,12},{12,14},{14,16},{16,18},{18... | collective-permute-start | bytes 3080 | tf_op jit(solution)/shard_map/ppermute | solution.py:12
  4.8 4.4 %all_to_all.69 = bf16[64,8,128]{2,0,1:T(8,128)(2,1)S(1)} all-to-all(bf16[64,8,128]{2,0,1:T(8,128)(2,1)S(1)} %copy.42), channel_id=1, replica_groups=mesh['ctx'=16,'tp'=2] {'tp'}, dimensions={1} | all-to-all | bytes 262144 | tf_op jit(solution)/shard_map/all_to_all | solution.py:29
  9.2 3.1 %collective-permute-start = (bf16[128,4,128]{2,0,1:T(8,128)(2,1)S(1)}, bf16[128,4,128]{2,0,1:T(8,128)(2,1)S(1)}, u32[]{:S(2)}, u32[]{:S(2)}) collective-permute-start(bf16[128,4,128]{2,0,1:T(8,128)(2,1)S(1)} %bitcast.194), channel_id=1, source_target_pairs={{0,2},{2,4},{4,6},{6,8},{8,10},{10,12},{12,14},{14,16},{16,18},{18... | collective-permute-start | bytes 393224 | tf_op jit(solution)/shard_map/ppermute | solution.py:12
  13.9 4.0 %all-to-all-start.2 = ((bf16[64,8,128]{2,0,1:T(8,128)(2,1)}), bf16[64,8,128]{2,0,1:T(8,128)(2,1)S(1)}, u32[]{:S(2)}, u32[]{:S(2)}) async-start(bf16[64,8,128]{2,0,1:T(8,128)(2,1)} %copy.46), calls=%async_computation.2 | async-start | bytes 262144 | tf_op jit(solution)/shard_map/all_to_all | solution.py:30
  17.9 2.9 %copy.44 = bf16[64,64,128]{2,0,1:T(8,128)(2,1)} copy(bf16[64,64,128]{2,1,0:T(8,128)(2,1)} %param.6) | data formatting | bytes 2097152 | tf_op args[0]
  20.8 3.6 %all-to-all-start.1 = ((bf16[64,64,128]{2,0,1:T(8,128)(2,1)}), bf16[64,64,128]{2,0,1:T(8,128)(2,1)S(1)}, u32[]{:S(2)}, u32[]{:S(2)}) async-start(bf16[64,64,128]{2,0,1:T(8,128)(2,1)} %copy.44), calls=%async_computation.1 | async-start | bytes 2097152 | tf_op jit(solution)/shard_map/all_to_all | solution.py:28
  24.4 3.1 %collective-permute-start.3 = (bf16[128,4,128]{2,0,1:T(8,128)(2,1)S(1)}, bf16[128,4,128]{2,0,1:T(8,128)(2,1)S(1)}, u32[]{:S(2)}, u32[]{:S(2)}) collective-permute-start(bf16[128,4,128]{2,0,1:T(8,128)(2,1)S(1)} %bitcast.198), channel_id=1, source_target_pairs={{0,2},{2,4},{4,6},{6,8},{8,10},{10,12},{12,14},{14,16},{16,18},{18... | collective-permute-start | bytes 393224 | tf_op jit(solution)/shard_map/ppermute | solution.py:12
  27.7 3.1 %collective-permute-start.2 = (bf16[128,4]{0,1:T(4,128)(2,1)S(1)}, bf16[128,4]{0,1:T(4,128)(2,1)S(1)}, u32[]{:S(2)}, u32[]{:S(2)}) collective-permute-start(bf16[128,4]{0,1:T(4,128)(2,1)S(1)} %reshape.502), channel_id=1, source_target_pairs={{0,2},{2,4},{4,6},{6,8},{8,10},{10,12},{12,14},{14,16},{16,18},{18... | collective-permute-start | bytes 3080 | tf_op jit(solution)/shard_map/ppermute | solution.py:12
  32.1 3.1 %collective-permute-start.5 = (bf16[128,4]{0,1:T(4,128)(2,1)S(1)}, bf16[128,4]{0,1:T(4,128)(2,1)S(1)}, u32[]{:S(2)}, u32[]{:S(2)}) collective-permute-start(bf16[128,4]{0,1:T(4,128)(2,1)S(1)} %collective-permute-done.1), channel_id=1, source_target_pairs={{0,2},{2,4},{4,6},{6,8},{8,10},{10,12},{12,14},{14,16},{16,18},{18... | collective-permute-start | bytes 3080 | tf_op jit(solution)/shard_map/ppermute | solution.py:12
  35.3 3.1 %collective-permute-start.6 = (bf16[128,4]{0,1:T(4,128)(2,1)S(1)}, bf16[128,4]{0,1:T(4,128)(2,1)S(1)}, u32[]{:S(2)}, u32[]{:S(2)}) collective-permute-start(bf16[128,4]{0,1:T(4,128)(2,1)S(1)} %collective-permute-done.2), channel_id=1, source_target_pairs={{0,2},{2,4},{4,6},{6,8},{8,10},{10,12},{12,14},{14,16},{16,18},{18... | collective-permute-start | bytes 3080 | tf_op jit(solution)/shard_map/ppermute | solution.py:12
  38.4 3.1 %collective-permute-start.9 = (bf16[128,4]{0,1:T(4,128)(2,1)S(1)}, bf16[128,4]{0,1:T(4,128)(2,1)S(1)}, u32[]{:S(2)}, u32[]{:S(2)}) collective-permute-start(bf16[128,4]{0,1:T(4,128)(2,1)S(1)} %collective-permute-done.5), channel_id=1, source_target_pairs={{0,2},{2,4},{4,6},{6,8},{8,10},{10,12},{12,14},{14,16},{16,18},{18... | collective-permute-start | bytes 3080 | tf_op jit(solution)/shard_map/ppermute | solution.py:12
  41.6 3.1 %collective-permute-start.10 = (bf16[128,4]{0,1:T(4,128)(2,1)S(1)}, bf16[128,4]{0,1:T(4,128)(2,1)S(1)}, u32[]{:S(2)}, u32[]{:S(2)}) collective-permute-start(bf16[128,4]{0,1:T(4,128)(2,1)S(1)} %collective-permute-done.6), channel_id=1, source_target_pairs={{0,2},{2,4},{4,6},{6,8},{8,10},{10,12},{12,14},{14,16},{16,18},{18... | collective-permute-start | bytes 3080 | tf_op jit(solution)/shard_map/ppermute | solution.py:12
  44.7 3.1 %collective-permute-start.13 = (bf16[128,4]{0,1:T(4,128)(2,1)S(1)}, bf16[128,4]{0,1:T(4,128)(2,1)S(1)}, u32[]{:S(2)}, u32[]{:S(2)}) collective-permute-start(bf16[128,4]{0,1:T(4,128)(2,1)S(1)} %collective-permute-done.9), channel_id=1, source_target_pairs={{0,2},{2,4},{4,6},{6,8},{8,10},{10,12},{12,14},{14,16},{16,18},{18... | collective-permute-start | bytes 3080 | tf_op jit(solution)/shard_map/ppermute | solution.py:12
  47.9 3.1 %collective-permute-start.14 = (bf16[128,4]{0,1:T(4,128)(2,1)S(1)}, bf16[128,4]{0,1:T(4,128)(2,1)S(1)}, u32[]{:S(2)}, u32[]{:S(2)}) collective-permute-start(bf16[128,4]{0,1:T(4,128)(2,1)S(1)} %collective-permute-done.10), channel_id=1, source_target_pairs={{0,2},{2,4},{4,6},{6,8},{8,10},{10,12},{12,14},{14,16},{16,18},{18... | collective-permute-start | bytes 3080 | tf_op jit(solution)/shard_map/ppermute | solution.py:12
  51.0 3.0 %collective-permute-done.14 = bf16[128,4]{0,1:T(4,128)(2,1)S(1)} collective-permute-done((bf16[128,4]{0,1:T(4,128)(2,1)S(1)}, bf16[128,4]{0,1:T(4,128)(2,1)S(1)}, u32[]{:S(2)}, u32[]{:S(2)}) %collective-permute-start.14) | collective-permute-done | bytes 1056 | tf_op jit(solution)/shard_map/ppermute | solution.py:12
  54.1 1.9 %collective-permute-start.4 = (bf16[128,4,128]{2,0,1:T(8,128)(2,1)S(1)}, bf16[128,4,128]{2,0,1:T(8,128)(2,1)S(1)}, u32[]{:S(2)}, u32[]{:S(2)}) collective-permute-start(bf16[128,4,128]{2,0,1:T(8,128)(2,1)S(1)} %collective-permute-done), channel_id=1, source_target_pairs={{0,2},{2,4},{4,6},{6,8},{8,10},{10,12},{12,14},{14,16},{16,18},{18... | collective-permute-start | bytes 393224 | tf_op jit(solution)/shard_map/ppermute | solution.py:12
  56.0 3.3 %collective-permute-start.7 = (bf16[128,4,128]{2,0,1:T(8,128)(2,1)S(1)}, bf16[128,4,128]{2,0,1:T(8,128)(2,1)S(1)}, u32[]{:S(2)}, u32[]{:S(2)}) collective-permute-start(bf16[128,4,128]{2,0,1:T(8,128)(2,1)S(1)} %collective-permute-done.3), channel_id=1, source_target_pairs={{0,2},{2,4},{4,6},{6,8},{8,10},{10,12},{12,14},{14,16},{16,18},{18... | collective-permute-start | bytes 393224 | tf_op jit(solution)/shard_map/ppermute | solution.py:12
  61.6 1.9 %collective-permute-start.8 = (bf16[128,4,128]{2,0,1:T(8,128)(2,1)S(1)}, bf16[128,4,128]{2,0,1:T(8,128)(2,1)S(1)}, u32[]{:S(2)}, u32[]{:S(2)}) collective-permute-start(bf16[128,4,128]{2,0,1:T(8,128)(2,1)S(1)} %collective-permute-done.4), channel_id=1, source_target_pairs={{0,2},{2,4},{4,6},{6,8},{8,10},{10,12},{12,14},{14,16},{16,18},{18... | collective-permute-start | bytes 393224 | tf_op jit(solution)/shard_map/ppermute | solution.py:12
  63.5 3.6 %collective-permute-start.11 = (bf16[128,4,128]{2,0,1:T(8,128)(2,1)S(1)}, bf16[128,4,128]{2,0,1:T(8,128)(2,1)S(1)}, u32[]{:S(2)}, u32[]{:S(2)}) collective-permute-start(bf16[128,4,128]{2,0,1:T(8,128)(2,1)S(1)} %collective-permute-done.7), channel_id=1, source_target_pairs={{0,2},{2,4},{4,6},{6,8},{8,10},{10,12},{12,14},{14,16},{16,18},{18... | collective-permute-start | bytes 393224 | tf_op jit(solution)/shard_map/ppermute | solution.py:12
  69.2 1.9 %collective-permute-start.12 = (bf16[128,4,128]{2,0,1:T(8,128)(2,1)S(1)}, bf16[128,4,128]{2,0,1:T(8,128)(2,1)S(1)}, u32[]{:S(2)}, u32[]{:S(2)}) collective-permute-start(bf16[128,4,128]{2,0,1:T(8,128)(2,1)S(1)} %collective-permute-done.8), channel_id=1, source_target_pairs={{0,2},{2,4},{4,6},{6,8},{8,10},{10,12},{12,14},{14,16},{16,18},{18... | collective-permute-start | bytes 393224 | tf_op jit(solution)/shard_map/ppermute | solution.py:12
  71.2 3.6 %collective-permute-start.15 = (bf16[128,4,128]{2,0,1:T(8,128)(2,1)S(1)}, bf16[128,4,128]{2,0,1:T(8,128)(2,1)S(1)}, u32[]{:S(2)}, u32[]{:S(2)}) collective-permute-start(bf16[128,4,128]{2,0,1:T(8,128)(2,1)S(1)} %collective-permute-done.11), channel_id=1, source_target_pairs={{0,2},{2,4},{4,6},{6,8},{8,10},{10,12},{12,14},{14,16},{16,18},{18... | collective-permute-start | bytes 393224 | tf_op jit(solution)/shard_map/ppermute | solution.py:12
  75.3 2.9 %collective-permute-done.12 = bf16[128,4,128]{2,0,1:T(8,128)(2,1)S(1)} collective-permute-done((bf16[128,4,128]{2,0,1:T(8,128)(2,1)S(1)}, bf16[128,4,128]{2,0,1:T(8,128)(2,1)S(1)}, u32[]{:S(2)}, u32[]{:S(2)}) %collective-permute-start.12) | collective-permute-done | bytes 131104 | tf_op jit(solution)/shard_map/ppermute | solution.py:12
  85.4 4.5 %fusion.1 = bf16[128,4,8,128]{3,0,2,1:T(8,128)(2,1)S(1)} fusion(f32[4,128,8,128]{3,1,2,0:T(8,128)S(1)} %fusion.19, f32[4,128,8,128]{3,1,2,0:T(8,128)S(1)} %fusion.18, f32[4,128,8,128]{3,1,2,0:T(8,128)S(1)} %fusion.17, f32[4,128,8,128]{3,1,2,0:T(8,128)S(1)} %fusion.16, f32[4,128,128,8]{2,1,3,0:T(8,128)S(1)} %get-tuple-element.27, ...), kind=kOutput, calls=%fused_computation.2 | convolution fusion | flops 143130624 | bytes 11800576 | tf_op jit(solution)/shard_map/qkgj,jkd->qkgd/dot_general | solution.py:68
  90.6 10.0 %all_to_all.70 = bf16[128,32,128]{2,1,0:T(8,128)(2,1)S(1)} all-to-all(bf16[128,32,128]{2,1,0:T(8,128)(2,1)S(1)} %copy.53), channel_id=1, replica_groups=mesh['ctx'=16,'tp'=2] {'tp'}, dimensions={0} | all-to-all | bytes 2097152 | tf_op jit(solution)/shard_map/all_to_all | solution.py:88
  (68 shorter events, 18.5 us)
Async XLA Ops:
  0.7 31.4 %collective-permute-start.1 = (bf16[128,4]{0,1:T(4,128)(2,1)S(1)}, bf16[128,4]{0,1:T(4,128)(2,1)S(1)}, u32[]{:S(2)}, u32[]{:S(2)}) collective-permute-start(bf16[128,4]{0,1:T(4,128)(2,1)S(1)} %reshape.501), channel_id=1, source_target_pairs={{0,2},{2,4},{4,6},{6,8},{8,10},{10,12},{12,14},{14,16},{16,18},{18... | collective-permute-start | bytes 3080 | tf_op jit(solution)/shard_map/ppermute | solution.py:12
  9.2 44.9 %collective-permute-start = (bf16[128,4,128]{2,0,1:T(8,128)(2,1)S(1)}, bf16[128,4,128]{2,0,1:T(8,128)(2,1)S(1)}, u32[]{:S(2)}, u32[]{:S(2)}) collective-permute-start(bf16[128,4,128]{2,0,1:T(8,128)(2,1)S(1)} %bitcast.194), channel_id=1, source_target_pairs={{0,2},{2,4},{4,6},{6,8},{8,10},{10,12},{12,14},{14,16},{16,18},{18... | collective-permute-start | bytes 393224 | tf_op jit(solution)/shard_map/ppermute | solution.py:12
  13.9 6.9 %all-to-all-start.2 = ((bf16[64,8,128]{2,0,1:T(8,128)(2,1)}), bf16[64,8,128]{2,0,1:T(8,128)(2,1)S(1)}, u32[]{:S(2)}, u32[]{:S(2)}) async-start(bf16[64,8,128]{2,0,1:T(8,128)(2,1)} %copy.46), calls=%async_computation.2 | async-start | bytes 262144 | tf_op jit(solution)/shard_map/all_to_all | solution.py:30
  17.9 9.7 %copy-start.2 = (bf16[1,4]{1,0:T(2,128)(2,1)S(1)}, bf16[1,4]{1,0:T(2,128)(2,1)}, u32[]{:S(2)}) copy-start(bf16[1,4]{1,0:T(2,128)(2,1)} %param.10) | copy-start | bytes 28
  17.9 12.9 %copy-start.1 = (bf16[1,4]{1,0:T(2,128)(2,1)S(1)}, bf16[1,4]{1,0:T(2,128)(2,1)}, u32[]{:S(2)}) copy-start(bf16[1,4]{1,0:T(2,128)(2,1)} %param.9) | copy-start | bytes 28
  17.9 13.0 %copy-start = (s32[16]{0:T(128)S(1)}, s32[16]{0:T(128)}, u32[]{:S(2)}) copy-start(s32[16]{0:T(128)} %param.11) | copy-start | bytes 196
  20.8 10.3 %all-to-all-start.1 = ((bf16[64,64,128]{2,0,1:T(8,128)(2,1)}), bf16[64,64,128]{2,0,1:T(8,128)(2,1)S(1)}, u32[]{:S(2)}, u32[]{:S(2)}) async-start(bf16[64,64,128]{2,0,1:T(8,128)(2,1)} %copy.44), calls=%async_computation.1 | async-start | bytes 2097152 | tf_op jit(solution)/shard_map/all_to_all | solution.py:28
  24.4 31.6 %collective-permute-start.3 = (bf16[128,4,128]{2,0,1:T(8,128)(2,1)S(1)}, bf16[128,4,128]{2,0,1:T(8,128)(2,1)S(1)}, u32[]{:S(2)}, u32[]{:S(2)}) collective-permute-start(bf16[128,4,128]{2,0,1:T(8,128)(2,1)S(1)} %bitcast.198), channel_id=1, source_target_pairs={{0,2},{2,4},{4,6},{6,8},{8,10},{10,12},{12,14},{14,16},{16,18},{18... | collective-permute-start | bytes 393224 | tf_op jit(solution)/shard_map/ppermute | solution.py:12
  27.7 7.6 %collective-permute-start.2 = (bf16[128,4]{0,1:T(4,128)(2,1)S(1)}, bf16[128,4]{0,1:T(4,128)(2,1)S(1)}, u32[]{:S(2)}, u32[]{:S(2)}) collective-permute-start(bf16[128,4]{0,1:T(4,128)(2,1)S(1)} %reshape.502), channel_id=1, source_target_pairs={{0,2},{2,4},{4,6},{6,8},{8,10},{10,12},{12,14},{14,16},{16,18},{18... | collective-permute-start | bytes 3080 | tf_op jit(solution)/shard_map/ppermute | solution.py:12
  32.1 6.3 %collective-permute-start.5 = (bf16[128,4]{0,1:T(4,128)(2,1)S(1)}, bf16[128,4]{0,1:T(4,128)(2,1)S(1)}, u32[]{:S(2)}, u32[]{:S(2)}) collective-permute-start(bf16[128,4]{0,1:T(4,128)(2,1)S(1)} %collective-permute-done.1), channel_id=1, source_target_pairs={{0,2},{2,4},{4,6},{6,8},{8,10},{10,12},{12,14},{14,16},{16,18},{18... | collective-permute-start | bytes 3080 | tf_op jit(solution)/shard_map/ppermute | solution.py:12
  35.3 6.3 %collective-permute-start.6 = (bf16[128,4]{0,1:T(4,128)(2,1)S(1)}, bf16[128,4]{0,1:T(4,128)(2,1)S(1)}, u32[]{:S(2)}, u32[]{:S(2)}) collective-permute-start(bf16[128,4]{0,1:T(4,128)(2,1)S(1)} %collective-permute-done.2), channel_id=1, source_target_pairs={{0,2},{2,4},{4,6},{6,8},{8,10},{10,12},{12,14},{14,16},{16,18},{18... | collective-permute-start | bytes 3080 | tf_op jit(solution)/shard_map/ppermute | solution.py:12
  38.4 6.3 %collective-permute-start.9 = (bf16[128,4]{0,1:T(4,128)(2,1)S(1)}, bf16[128,4]{0,1:T(4,128)(2,1)S(1)}, u32[]{:S(2)}, u32[]{:S(2)}) collective-permute-start(bf16[128,4]{0,1:T(4,128)(2,1)S(1)} %collective-permute-done.5), channel_id=1, source_target_pairs={{0,2},{2,4},{4,6},{6,8},{8,10},{10,12},{12,14},{14,16},{16,18},{18... | collective-permute-start | bytes 3080 | tf_op jit(solution)/shard_map/ppermute | solution.py:12
  41.6 6.3 %collective-permute-start.10 = (bf16[128,4]{0,1:T(4,128)(2,1)S(1)}, bf16[128,4]{0,1:T(4,128)(2,1)S(1)}, u32[]{:S(2)}, u32[]{:S(2)}) collective-permute-start(bf16[128,4]{0,1:T(4,128)(2,1)S(1)} %collective-permute-done.6), channel_id=1, source_target_pairs={{0,2},{2,4},{4,6},{6,8},{8,10},{10,12},{12,14},{14,16},{16,18},{18... | collective-permute-start | bytes 3080 | tf_op jit(solution)/shard_map/ppermute | solution.py:12
  44.7 6.3 %collective-permute-start.13 = (bf16[128,4]{0,1:T(4,128)(2,1)S(1)}, bf16[128,4]{0,1:T(4,128)(2,1)S(1)}, u32[]{:S(2)}, u32[]{:S(2)}) collective-permute-start(bf16[128,4]{0,1:T(4,128)(2,1)S(1)} %collective-permute-done.9), channel_id=1, source_target_pairs={{0,2},{2,4},{4,6},{6,8},{8,10},{10,12},{12,14},{14,16},{16,18},{18... | collective-permute-start | bytes 3080 | tf_op jit(solution)/shard_map/ppermute | solution.py:12
  47.9 6.2 %collective-permute-start.14 = (bf16[128,4]{0,1:T(4,128)(2,1)S(1)}, bf16[128,4]{0,1:T(4,128)(2,1)S(1)}, u32[]{:S(2)}, u32[]{:S(2)}) collective-permute-start(bf16[128,4]{0,1:T(4,128)(2,1)S(1)} %collective-permute-done.10), channel_id=1, source_target_pairs={{0,2},{2,4},{4,6},{6,8},{8,10},{10,12},{12,14},{14,16},{16,18},{18... | collective-permute-start | bytes 3080 | tf_op jit(solution)/shard_map/ppermute | solution.py:12
  54.1 7.5 %collective-permute-start.4 = (bf16[128,4,128]{2,0,1:T(8,128)(2,1)S(1)}, bf16[128,4,128]{2,0,1:T(8,128)(2,1)S(1)}, u32[]{:S(2)}, u32[]{:S(2)}) collective-permute-start(bf16[128,4,128]{2,0,1:T(8,128)(2,1)S(1)} %collective-permute-done), channel_id=1, source_target_pairs={{0,2},{2,4},{4,6},{6,8},{8,10},{10,12},{12,14},{14,16},{16,18},{18... | collective-permute-start | bytes 393224 | tf_op jit(solution)/shard_map/ppermute | solution.py:12
  56.0 7.5 %collective-permute-start.7 = (bf16[128,4,128]{2,0,1:T(8,128)(2,1)S(1)}, bf16[128,4,128]{2,0,1:T(8,128)(2,1)S(1)}, u32[]{:S(2)}, u32[]{:S(2)}) collective-permute-start(bf16[128,4,128]{2,0,1:T(8,128)(2,1)S(1)} %collective-permute-done.3), channel_id=1, source_target_pairs={{0,2},{2,4},{4,6},{6,8},{8,10},{10,12},{12,14},{14,16},{16,18},{18... | collective-permute-start | bytes 393224 | tf_op jit(solution)/shard_map/ppermute | solution.py:12
  61.6 7.6 %collective-permute-start.8 = (bf16[128,4,128]{2,0,1:T(8,128)(2,1)S(1)}, bf16[128,4,128]{2,0,1:T(8,128)(2,1)S(1)}, u32[]{:S(2)}, u32[]{:S(2)}) collective-permute-start(bf16[128,4,128]{2,0,1:T(8,128)(2,1)S(1)} %collective-permute-done.4), channel_id=1, source_target_pairs={{0,2},{2,4},{4,6},{6,8},{8,10},{10,12},{12,14},{14,16},{16,18},{18... | collective-permute-start | bytes 393224 | tf_op jit(solution)/shard_map/ppermute | solution.py:12
  63.5 7.6 %collective-permute-start.11 = (bf16[128,4,128]{2,0,1:T(8,128)(2,1)S(1)}, bf16[128,4,128]{2,0,1:T(8,128)(2,1)S(1)}, u32[]{:S(2)}, u32[]{:S(2)}) collective-permute-start(bf16[128,4,128]{2,0,1:T(8,128)(2,1)S(1)} %collective-permute-done.7), channel_id=1, source_target_pairs={{0,2},{2,4},{4,6},{6,8},{8,10},{10,12},{12,14},{14,16},{16,18},{18... | collective-permute-start | bytes 393224 | tf_op jit(solution)/shard_map/ppermute | solution.py:12
  69.2 8.9 %collective-permute-start.12 = (bf16[128,4,128]{2,0,1:T(8,128)(2,1)S(1)}, bf16[128,4,128]{2,0,1:T(8,128)(2,1)S(1)}, u32[]{:S(2)}, u32[]{:S(2)}) collective-permute-start(bf16[128,4,128]{2,0,1:T(8,128)(2,1)S(1)} %collective-permute-done.8), channel_id=1, source_target_pairs={{0,2},{2,4},{4,6},{6,8},{8,10},{10,12},{12,14},{14,16},{16,18},{18... | collective-permute-start | bytes 393224 | tf_op jit(solution)/shard_map/ppermute | solution.py:12
  71.2 14.3 %collective-permute-start.15 = (bf16[128,4,128]{2,0,1:T(8,128)(2,1)S(1)}, bf16[128,4,128]{2,0,1:T(8,128)(2,1)S(1)}, u32[]{:S(2)}, u32[]{:S(2)}) collective-permute-start(bf16[128,4,128]{2,0,1:T(8,128)(2,1)S(1)} %collective-permute-done.11), channel_id=1, source_target_pairs={{0,2},{2,4},{4,6},{6,8},{8,10},{10,12},{12,14},{14,16},{16,18},{18... | collective-permute-start | bytes 393224 | tf_op jit(solution)/shard_map/ppermute | solution.py:12
where the time goes:
time: 103 us; the launch traced here: 102 us
  starting transfers between devices  55 us (53%)
  blocking collectives  14.4 us (14%)
  matrix products  10.4 us (10%)
  waiting for transfers between devices  9.42 us (9%)
  local copies, waits for them, and re-layouts  8.2 us (8%)
  other arithmetic  3.77 us (4%)
    ppermute x16, starting transfers between devices, passed_along(): lax.ppermute(value, axis, [(source, source + steps) for source in range(l...  47.4 us
    all_to_all x1, blocking collectives, shards(): return lax.all_to_all(result, 'tp', split_axis=0, concat_axis=1, tiled=True)  9.95 us
    ppermute x16, waiting for transfers between devices, passed_along(): lax.ppermute(value, axis, [(source, source + steps) for source in range(l...  9.42 us
    dot_general x5, matrix products, attend(): jnp.einsum('qkgj,jkd->qkgd', weights, v_part, preferred_element_type=jnp....  8.13 us
    unnamed x9, local copies, waits for them, and re-layouts  5.41 us
    all_to_all x1, blocking collectives, shards(): lax.all_to_all(rotated_key_rows, 'tp', split_axis=1, concat_axis=0, tiled...  4.44 us
    all_to_all x1, starting transfers between devices, shards(): lax.all_to_all(unscaled_value_rows, 'tp', split_axis=1, concat_axis=0, ti...  4 us
    all_to_all x1, starting transfers between devices, shards(): lax.all_to_all(queries, 'tp', split_axis=1, concat_axis=0, tiled=True)  3.59 us
  transfers between devices with their start and end apart: 18, of which 4 were waited for; matrix products, arithmetic and copies ran while one was open for 15% of the time, Pallas kernels for 0%

commit v1 on v0

v1 whole, which is shorter than its diff:
```python
import functools
import math

import jax
import jax.numpy as jnp
from jax import lax
from jax.experimental import pallas as pl
from jax.experimental.pallas import tpu as pltpu
from jax.sharding import PartitionSpec as P

NEG = -1e30
VMEM = pltpu.MemorySpace.VMEM
SMEM = pltpu.MemorySpace.SMEM


def pack_kernel(k_ref, v_ref, s_ref, out_ref, rows_ref):
    tokens, heads, width = k_ref.shape
    for part, ref in enumerate((k_ref, v_ref)):
        rows_ref[part] = ref[...].astype(jnp.float32).reshape(tokens * heads, width)
        for head in range(heads):
            start = (part * heads + head) * tokens
            out_ref[start : start + tokens, :] = rows_ref[part, pl.ds(head, tokens, stride=heads), :].astype(
                out_ref.dtype
            )
    out_ref[2 * heads * tokens :, :] = s_ref[...]


def pack(keys, values, scales):
    tokens, heads, width = keys.shape
    return pl.pallas_call(
        pack_kernel,
        out_shape=jax.ShapeDtypeStruct((2 * heads * tokens + scales.shape[0], width), keys.dtype),
        in_specs=[pl.BlockSpec(memory_space=VMEM)] * 3,
        out_specs=pl.BlockSpec(memory_space=VMEM),
        scratch_shapes=[pltpu.VMEM((2, tokens * heads, width), jnp.float32)],
        compiler_params=pltpu.CompilerParams(vmem_limit_bytes=8 * 2**20),
        name="pack",
    )(keys, values, scales)


def attend_kernel(count, heads, group, place_ref, length_ref, q_ref, *refs):
    mine, sibling = refs[:count], refs[count : 2 * count]
    out_ref, bias_ref = refs[2 * count :]
    tokens, step_heads, width = q_ref.shape
    rows = tokens * group
    block = 2 * tokens
    core = place_ref[1]
    step = pl.program_id(0)

    @pl.when(step == 0)
    def _():
        position = place_ref[0] + lax.broadcasted_iota(jnp.int32, (rows, width), 0) // group

        def later(i, carry):
            start, end = carry
            end = end + length_ref[i]
            return jnp.where(position >= end, end, start), end

        start, _ = lax.fori_loop(0, length_ref.shape[0], later, (jnp.zeros_like(position), jnp.int32(0)))
        lane = lax.broadcasted_iota(jnp.int32, (rows, width), 1)
        half = jnp.where(lane < tokens, core, 1 - core) * tokens + jnp.where(lane < tokens, lane, lane - tokens)
        for b in range(count):
            key = place_ref[2 + b] + half
            allowed = (key >= start) & (key <= position)
            bias_ref[:, b * block : (b + 1) * block] = jnp.where(allowed, 0.0, NEG)

    kv_local = heads // 2
    first = core == 0
    scale_rows = []
    for b in range(count):
        low = 2 * heads * tokens
        a = mine[b][low : low + 16, :].astype(jnp.float32)
        z = sibling[b][low : low + 16, :].astype(jnp.float32)
        scale_rows.append((jnp.where(first, a, z), jnp.where(first, z, a)))

    def pick(b, which, head):
        lower, upper = scale_rows[b]
        both = jnp.concatenate([lower[which * kv_local : which * kv_local + kv_local], upper[which * kv_local : which * kv_local + kv_local]], axis=0)
        row = lax.broadcasted_iota(jnp.int32, both.shape, 0)
        return jnp.sum(jnp.where(row == head, both, 0.0), axis=0, keepdims=True)

    for sub in range(step_heads // group):
        head = step * (step_heads // group) + sub
        q = q_ref[:, sub * group : (sub + 1) * group, :].reshape(rows, width)
        at_k = pl.multiple_of(head * tokens, tokens)
        at_v = pl.multiple_of((heads + head) * tokens, tokens)
        keys = jnp.concatenate(
            [ref[pl.ds(at_k, tokens), :] for b in range(count) for ref in (mine[b], sibling[b])], axis=0
        )
        values = jnp.concatenate(
            [ref[pl.ds(at_v, tokens), :] for b in range(count) for ref in (mine[b], sibling[b])], axis=0
        )
        k_scale = jnp.concatenate([pick(b, 0, head) for b in range(count)], axis=1)
        k_scale = k_scale * (math.log2(math.e) / math.sqrt(width))
        v_scale = jnp.concatenate([pick(b, 1, head) for b in range(count)], axis=1)
        scores = lax.dot_general(q, keys, (((1,), (1,)), ((), ())), preferred_element_type=jnp.float32)
        scores = scores * k_scale + bias_ref[...]
        top = jnp.max(scores, axis=1, keepdims=True)
        expo = jnp.exp2(scores - top)
        total = jnp.sum(expo, axis=1, keepdims=True)
        weights = (expo * v_scale).astype(jnp.bfloat16)
        summed = jnp.dot(weights, values, preferred_element_type=jnp.float32)
        out = (summed / total).astype(out_ref.dtype)
        out_ref[:, sub * group : (sub + 1) * group, :] = out.reshape(tokens, group, width)


def attend(queries, place, lengths, mine, sibling, heads):
    tokens, q_heads, width = queries.shape
    group = q_heads // heads
    count = len(mine)
    per_step = 2 * group
    whole = pl.BlockSpec(memory_space=VMEM)
    return pl.pallas_call(
        functools.partial(attend_kernel, count, heads, group),
        out_shape=jax.ShapeDtypeStruct(queries.shape, queries.dtype),
        grid=(q_heads // per_step,),
        in_specs=[
            pl.BlockSpec(memory_space=SMEM),
            pl.BlockSpec(memory_space=SMEM),
            pl.BlockSpec((tokens, per_step, width), lambda i: (0, i, 0)),
        ]
        + [whole] * (2 * count),
        out_specs=pl.BlockSpec((tokens, per_step, width), lambda i: (0, i, 0)),
        scratch_shapes=[pltpu.VMEM((tokens * group, count * 2 * tokens), jnp.float32)],
        compiler_params=pltpu.CompilerParams(vmem_limit_bytes=32 * 2**20),
        cost_estimate=pl.CostEstimate(
            flops=4 * tokens * q_heads * count * 2 * tokens * width,
            bytes_accessed=4 * tokens * q_heads * width,
            transcendentals=tokens * q_heads * count * 2 * tokens,
        ),
        name="attend",
    )(place, lengths, queries, *mine, *sibling)


def shards(queries, keys, values, key_scales, value_scales, lengths):
    tokens, heads, width = keys.shape
    ranks = lax.axis_size("ctx")
    c, t = lax.axis_index("ctx"), lax.axis_index("tp")
    block = tokens * lax.axis_size("tp")
    scales = jnp.concatenate([key_scales[0], value_scales[0]])
    scales = jnp.broadcast_to(scales[:, None], (scales.shape[0], width))
    scales = jnp.pad(scales, ((0, 16 - scales.shape[0]), (0, 0)))
    own = pack(keys, values, scales)

    def send(value, target):
        pairs = [(source, target(source)) for source in range(ranks)]
        return lax.ppermute(value, "ctx", [(i, j) for i, j in pairs if 0 <= j < ranks])

    def swap(value):
        return lax.ppermute(value, "tp", [(0, 1), (1, 0)])

    k = c % 4
    from_z = send(own, lambda i: i + 4)
    from_d = send(own, lambda i: i + (3 if i % 4 in (0, 2) else 1))
    to_x = jnp.where(k % 2 == 0, own, from_z)
    to_y = jnp.where(k < 2, own, from_z)
    from_x = send(to_x, lambda i: i ^ 1)
    from_y = send(to_y, lambda i: i ^ 2)
    mine = [own, from_z, from_d, from_x, from_y]
    back = [0, 4, jnp.where(k % 2 == 0, 1, 3), jnp.where(k % 2 == 0, 3, 1), 2]
    sibling = [swap(part) for part in mine]
    place = jnp.stack([c * block + t * tokens, t] + [(c - b) * block for b in back]).astype(jnp.int32)
    return attend(queries, place, lengths, mine, sibling, heads)


def solution(mesh):
    both = P(("ctx", "tp"), None, None)
    return jax.shard_map(
        shards,
        mesh=mesh,
        in_specs=(both, both, both, P("ctx", "tp"), P("ctx", "tp"), P()),
        out_specs=both,
        check_vma=False,
    )
```

time: 103 us -> 37 us (0.36); the launches traced: 102 us -> 36.8 us
  starting transfers between devices: 55 us -> 16.1 us
  blocking collectives: 14.4 us -> 0 us
  matrix products: 10.4 us -> 0 us
  Pallas kernels: 0 us -> 8.98 us
  local copies, waits for them, and re-layouts: 8.2 us -> 2.65 us
  other arithmetic: 3.77 us -> 0.12 us
    ppermute x16 -> x9, starting transfers between devices: 47.4 us -> 16.1 us  [the longest x4 9.93 us: send(): lax.ppermute(value, 'ctx', [(i, j) for i, j in pairs if 0 <= j < ranks])]
    all_to_all x2 -> x0, blocking collectives: 14.4 us -> none  [the longest x1 9.95 us: shards(): return lax.all_to_all(result, 'tp', split_axis=0, concat_axis=1, tiled=True)]
    dot_general x10 -> x0, matrix products: 10.4 us -> none  [the longest x5 8.13 us: attend(): jnp.einsum('qkgj,jkd->qkgd', weights, v_part, preferred_element_type=jnp....]
    pallas_call x0 -> x2, Pallas kernels: none -> 8.98 us  [the longest x1 8.86 us: attend(): pl.pallas_call(functools.partial(attend_kernel, count, heads, group), out...]
    all_to_all x2 -> x0, starting transfers between devices: 7.59 us -> none  [the longest x1 4 us: shards(): lax.all_to_all(unscaled_value_rows, 'tp', split_axis=1, concat_axis=0, ti...]
    reduce_sum x6 -> x0, other arithmetic: 3.15 us -> none  [the longest x5 3.06 us: attend(): new_total = total * factor + jnp.sum(expo, axis=3)]
    unnamed x9 -> x12, local copies, waits for them, and re-layouts: 5.41 us -> 2.49 us
    all_to_all x4 -> x0, local copies, waits for them, and re-layouts: 1.23 us -> none  [the longest x1 1.12 us: shards(): return lax.all_to_all(result, 'tp', split_axis=0, concat_axis=1, tiled=True)]
  transfers between devices with their start and end apart: 18 -> 9, of which waited for: 4 -> 5; matrix products, arithmetic and copies ran while one was open for 15% -> 0% of each run, Pallas kernels for 0% -> 0%
where the time goes in v1:
time: 37 us; the launch traced here: 36.8 us
  starting transfers between devices  16.1 us (44%)
  Pallas kernels  8.98 us (24%)
  waiting for transfers between devices  8.79 us (24%)
  local copies, waits for them, and re-layouts  2.65 us (7%)
    ppermute x4, starting transfers between devices, send(): lax.ppermute(value, 'ctx', [(i, j) for i, j in pairs if 0 <= j < ranks])  9.93 us
    pallas_call x1, Pallas kernels, attend(): pl.pallas_call(functools.partial(attend_kernel, count, heads, group), out...  8.86 us
    ppermute x4, waiting for transfers between devices, send(): lax.ppermute(value, 'ctx', [(i, j) for i, j in pairs if 0 <= j < ranks])  7.21 us
    ppermute x5, starting transfers between devices, swap(): return lax.ppermute(value, 'tp', [(0, 1), (1, 0)])  6.21 us
    unnamed x12, local copies, waits for them, and re-layouts  2.49 us
    ppermute x5, waiting for transfers between devices, swap(): return lax.ppermute(value, 'tp', [(0, 1), (1, 0)])  1.57 us
  transfers between devices with their start and end apart: 9, of which 5 were waited for; matrix products, arithmetic and copies ran while one was open for 0% of the time, Pallas kernels for 0%

profile of v1, /device:TPU:9, one launch (start us, length us, event | category | flops | bytes accessed | tf_op | source)
XLA Modules:
  0.0 36.8 jit_solution(15570641036661383850)
XLA Ops:
  0.0 0.7 %copy-done.4 = bf16[1,4]{1,0:T(2,128)(2,1)S(1)} copy-done((bf16[1,4]{1,0:T(2,128)(2,1)S(1)}, bf16[1,4]{1,0:T(2,128)(2,1)}, u32[]{:S(2)}) %copy-start.4) | copy-done | bytes 32
  0.7 0.0 copy-done.5
  0.7 0.1 fusion
  0.7 0.1 pad.7.s_ref
  0.8 0.9 %copy-done = bf16[64,8,128]{2,1,0:T(8,128)(2,1)S(1)} copy-done((bf16[64,8,128]{2,1,0:T(8,128)(2,1)S(1)}, bf16[64,8,128]{2,1,0:T(8,128)(2,1)}, u32[]{:S(2)}) %copy-start) | copy-done | bytes 131096
  1.7 0.9 %copy-done.1 = bf16[64,8,128]{2,1,0:T(8,128)(2,1)S(1)} copy-done((bf16[64,8,128]{2,1,0:T(8,128)(2,1)S(1)}, bf16[64,8,128]{2,1,0:T(8,128)(2,1)}, u32[]{:S(2)}) %copy-start.1) | copy-done | bytes 131096
  2.6 0.1 pack.1.refs_0_
  2.8 3.3 %collective-permute-start = (bf16[1040,128]{1,0:T(8,128)(2,1)S(1)}, bf16[1040,128]{1,0:T(8,128)(2,1)S(1)}, u32[]{:S(2)}, u32[]{:S(2)}) collective-permute-start(bf16[1040,128]{1,0:T(8,128)(2,1)S(1)} %pack.1.refs_0_), channel_id=1, source_target_pairs={{0,8},{2,10},{4,12},{6,14},{8,16},{10,18},{12,20},{14,22},{16,24},... | collective-permute-start | bytes 798728 | tf_op jit(solution)/shard_map/ppermute | solution.py:147
  6.1 4.1 %collective-permute-start.1 = (bf16[1040,128]{1,0:T(8,128)(2,1)S(1)}, bf16[1040,128]{1,0:T(8,128)(2,1)S(1)}, u32[]{:S(2)}, u32[]{:S(2)}) collective-permute-start(bf16[1040,128]{1,0:T(8,128)(2,1)S(1)} %pack.1.refs_0_), channel_id=1, source_target_pairs={{0,6},{2,4},{4,10},{6,8},{8,14},{10,12},{12,18},{14,16},{16,22},{1... | collective-permute-start | bytes 798728 | tf_op jit(solution)/shard_map/ppermute | solution.py:147
  10.2 1.8 %collective-permute-done.refs_1_ = bf16[1040,128]{1,0:T(8,128)(2,1)S(1)} collective-permute-done((bf16[1040,128]{1,0:T(8,128)(2,1)S(1)}, bf16[1040,128]{1,0:T(8,128)(2,1)S(1)}, u32[]{:S(2)}, u32[]{:S(2)}) %collective-permute-start) | collective-permute-done | bytes 266272 | tf_op jit(solution)/shard_map/ppermute | solution.py:147
  12.1 1.3 %collective-permute-start.3 = (bf16[1040,128]{1,0:T(8,128)(2,1)S(1)}, bf16[1040,128]{1,0:T(8,128)(2,1)S(1)}, u32[]{:S(2)}, u32[]{:S(2)}) collective-permute-start(bf16[1040,128]{1,0:T(8,128)(2,1)S(1)} %get-tuple-element.5), channel_id=1, source_target_pairs={{0,4},{2,6},{4,0},{6,2},{8,12},{10,14},{12,8},{14,10},{16,20},{18,... | collective-permute-start | bytes 798728 | tf_op jit(solution)/shard_map/ppermute | solution.py:147
  13.4 1.2 %collective-permute-start.2 = (bf16[1040,128]{1,0:T(8,128)(2,1)S(1)}, bf16[1040,128]{1,0:T(8,128)(2,1)S(1)}, u32[]{:S(2)}, u32[]{:S(2)}) collective-permute-start(bf16[1040,128]{1,0:T(8,128)(2,1)S(1)} %get-tuple-element.6), channel_id=1, source_target_pairs={{0,2},{2,0},{4,6},{6,4},{8,10},{10,8},{12,14},{14,12},{16,18},{18,... | collective-permute-start | bytes 798728 | tf_op jit(solution)/shard_map/ppermute | solution.py:147
  14.6 3.3 %collective-permute-start.4 = (bf16[1040,128]{1,0:T(8,128)(2,1)S(1)}, bf16[1040,128]{1,0:T(8,128)(2,1)S(1)}, u32[]{:S(2)}, u32[]{:S(2)}) collective-permute-start(bf16[1040,128]{1,0:T(8,128)(2,1)S(1)} %pack.1.refs_0_), channel_id=1, source_target_pairs={{0,1},{1,0},{2,3},{3,2},{4,5},{5,4},{6,7},{7,6},{8,9},{9,8},{10,11... | collective-permute-start | bytes 798728 | tf_op jit(solution)/shard_map/ppermute | solution.py:150
  17.9 0.0 collective-permute-start.5
  17.9 1.8 %collective-permute-done.1.refs_2_ = bf16[1040,128]{1,0:T(8,128)(2,1)S(1)} collective-permute-done((bf16[1040,128]{1,0:T(8,128)(2,1)S(1)}, bf16[1040,128]{1,0:T(8,128)(2,1)S(1)}, u32[]{:S(2)}, u32[]{:S(2)}) %collective-permute-start.1) | collective-permute-done | bytes 266272 | tf_op jit(solution)/shard_map/ppermute | solution.py:147
  19.7 1.7 %collective-permute-start.6 = (bf16[1040,128]{1,0:T(8,128)(2,1)S(1)}, bf16[1040,128]{1,0:T(8,128)(2,1)S(1)}, u32[]{:S(2)}, u32[]{:S(2)}) collective-permute-start(bf16[1040,128]{1,0:T(8,128)(2,1)S(1)} %collective-permute-done.1.refs_2_), channel_id=1, source_target_pairs={{0,1},{1,0},{2,3},{3,2},{4,5},{5,4},{6,7},{7,6},{8,9},{9,8},{10,11... | collective-permute-start | bytes 798728 | tf_op jit(solution)/shard_map/ppermute | solution.py:150
  21.3 3.6 %collective-permute-done.3.refs_4_ = bf16[1040,128]{1,0:T(8,128)(2,1)S(1)} collective-permute-done((bf16[1040,128]{1,0:T(8,128)(2,1)S(1)}, bf16[1040,128]{1,0:T(8,128)(2,1)S(1)}, u32[]{:S(2)}, u32[]{:S(2)}) %collective-permute-start.3) | collective-permute-done | bytes 266272 | tf_op jit(solution)/shard_map/ppermute | solution.py:147
  24.9 1.3 %collective-permute-start.8 = (bf16[1040,128]{1,0:T(8,128)(2,1)S(1)}, bf16[1040,128]{1,0:T(8,128)(2,1)S(1)}, u32[]{:S(2)}, u32[]{:S(2)}) collective-permute-start(bf16[1040,128]{1,0:T(8,128)(2,1)S(1)} %collective-permute-done.3.refs_4_), channel_id=1, source_target_pairs={{0,1},{1,0},{2,3},{3,2},{4,5},{5,4},{6,7},{7,6},{8,9},{9,8},{10,11... | collective-permute-start | bytes 798728 | tf_op jit(solution)/shard_map/ppermute | solution.py:150
  26.2 0.0 collective-permute-done.2.refs_3_
  26.2 0.0 collective-permute-start.7
  26.2 0.1 stack.31.place_ref
  26.3 1.4 %collective-permute-done.8.refs_9_ = bf16[1040,128]{1,0:T(8,128)(2,1)S(1)} collective-permute-done((bf16[1040,128]{1,0:T(8,128)(2,1)S(1)}, bf16[1040,128]{1,0:T(8,128)(2,1)S(1)}, u32[]{:S(2)}, u32[]{:S(2)}) %collective-permute-start.8) | collective-permute-done | bytes 266272 | tf_op jit(solution)/shard_map/ppermute | solution.py:150
  27.7 0.2 collective-permute-done.7.refs_8_
  27.9 8.9 %attend.1 = bf16[64,64,128]{2,1,0:T(8,128)(2,1)} custom-call(s32[7]{0:T(128)S(1)} %stack.31.place_ref, s32[16]{0:T(128)S(1)} %copy-done.3, bf16[64,64,128]{2,1,0:T(8,128)(2,1)S(1)} %copy-done.2, bf16[1040,128]{1,0:T(8,128)(2,1)S(1)} %pack.1.refs_0_, bf16[1040,128]{1,0:T(8,128)(2,1)S(1)} %collective-permute-done.refs_1_, ...), custom_call_target="tpu_custom_call" | custom-call | flops 1342177280 | bytes 2097152 | tf_op jit(solution)/shard_map/attend/pallas_call | solution.py:113
  (12 shorter events, 0.1 us)
Async XLA Ops:
  0.0 0.7 %copy-start.4 = (bf16[1,4]{1,0:T(2,128)(2,1)S(1)}, bf16[1,4]{1,0:T(2,128)(2,1)}, u32[]{:S(2)}) copy-start(bf16[1,4]{1,0:T(2,128)(2,1)} %param.10) | copy-start | bytes 28
  0.0 0.7 %copy-start.5 = (bf16[1,4]{1,0:T(2,128)(2,1)S(1)}, bf16[1,4]{1,0:T(2,128)(2,1)}, u32[]{:S(2)}) copy-start(bf16[1,4]{1,0:T(2,128)(2,1)} %param.9) | copy-start | bytes 28
  0.8 0.9 %copy-start = (bf16[64,8,128]{2,1,0:T(8,128)(2,1)S(1)}, bf16[64,8,128]{2,1,0:T(8,128)(2,1)}, u32[]{:S(2)}) copy-start(bf16[64,8,128]{2,1,0:T(8,128)(2,1)} %k_ref.1) | copy-start | bytes 393220
  1.7 0.9 %copy-start.1 = (bf16[64,8,128]{2,1,0:T(8,128)(2,1)S(1)}, bf16[64,8,128]{2,1,0:T(8,128)(2,1)}, u32[]{:S(2)}) copy-start(bf16[64,8,128]{2,1,0:T(8,128)(2,1)} %v_ref.1) | copy-start | bytes 393220
  2.6 25.3 %copy-start.2 = (bf16[64,64,128]{2,1,0:T(8,128)(2,1)S(1)}, bf16[64,64,128]{2,1,0:T(8,128)(2,1)}, u32[]{:S(2)}) copy-start(bf16[64,64,128]{2,1,0:T(8,128)(2,1)} %q_ref.1) | copy-start | bytes 3145732
  2.8 9.3 %collective-permute-start = (bf16[1040,128]{1,0:T(8,128)(2,1)S(1)}, bf16[1040,128]{1,0:T(8,128)(2,1)S(1)}, u32[]{:S(2)}, u32[]{:S(2)}) collective-permute-start(bf16[1040,128]{1,0:T(8,128)(2,1)S(1)} %pack.1.refs_0_), channel_id=1, source_target_pairs={{0,8},{2,10},{4,12},{6,14},{8,16},{10,18},{12,20},{14,22},{16,24},... | collective-permute-start | bytes 798728 | tf_op jit(solution)/shard_map/ppermute | solution.py:147
  6.1 13.6 %collective-permute-start.1 = (bf16[1040,128]{1,0:T(8,128)(2,1)S(1)}, bf16[1040,128]{1,0:T(8,128)(2,1)S(1)}, u32[]{:S(2)}, u32[]{:S(2)}) collective-permute-start(bf16[1040,128]{1,0:T(8,128)(2,1)S(1)} %pack.1.refs_0_), channel_id=1, source_target_pairs={{0,6},{2,4},{4,10},{6,8},{8,14},{10,12},{12,18},{14,16},{16,22},{1... | collective-permute-start | bytes 798728 | tf_op jit(solution)/shard_map/ppermute | solution.py:147
  12.1 12.8 %collective-permute-start.3 = (bf16[1040,128]{1,0:T(8,128)(2,1)S(1)}, bf16[1040,128]{1,0:T(8,128)(2,1)S(1)}, u32[]{:S(2)}, u32[]{:S(2)}) collective-permute-start(bf16[1040,128]{1,0:T(8,128)(2,1)S(1)} %get-tuple-element.5), channel_id=1, source_target_pairs={{0,4},{2,6},{4,0},{6,2},{8,12},{10,14},{12,8},{14,10},{16,20},{18,... | collective-permute-start | bytes 798728 | tf_op jit(solution)/shard_map/ppermute | solution.py:147
  13.4 12.8 %collective-permute-start.2 = (bf16[1040,128]{1,0:T(8,128)(2,1)S(1)}, bf16[1040,128]{1,0:T(8,128)(2,1)S(1)}, u32[]{:S(2)}, u32[]{:S(2)}) collective-permute-start(bf16[1040,128]{1,0:T(8,128)(2,1)S(1)} %get-tuple-element.6), channel_id=1, source_target_pairs={{0,2},{2,0},{4,6},{6,4},{8,10},{10,8},{12,14},{14,12},{16,18},{18,... | collective-permute-start | bytes 798728 | tf_op jit(solution)/shard_map/ppermute | solution.py:147
  14.6 11.7 %collective-permute-start.4 = (bf16[1040,128]{1,0:T(8,128)(2,1)S(1)}, bf16[1040,128]{1,0:T(8,128)(2,1)S(1)}, u32[]{:S(2)}, u32[]{:S(2)}) collective-permute-start(bf16[1040,128]{1,0:T(8,128)(2,1)S(1)} %pack.1.refs_0_), channel_id=1, source_target_pairs={{0,1},{1,0},{2,3},{3,2},{4,5},{5,4},{6,7},{7,6},{8,9},{9,8},{10,11... | collective-permute-start | bytes 798728 | tf_op jit(solution)/shard_map/ppermute | solution.py:150
  17.9 8.4 %collective-permute-start.5 = (bf16[1040,128]{1,0:T(8,128)(2,1)S(1)}, bf16[1040,128]{1,0:T(8,128)(2,1)S(1)}, u32[]{:S(2)}, u32[]{:S(2)}) collective-permute-start(bf16[1040,128]{1,0:T(8,128)(2,1)S(1)} %collective-permute-done.refs_1_), channel_id=1, source_target_pairs={{0,1},{1,0},{2,3},{3,2},{4,5},{5,4},{6,7},{7,6},{8,9},{9,8},{10,11... | collective-permute-start | bytes 798728 | tf_op jit(solution)/shard_map/ppermute | solution.py:150
  19.7 6.6 %collective-permute-start.6 = (bf16[1040,128]{1,0:T(8,128)(2,1)S(1)}, bf16[1040,128]{1,0:T(8,128)(2,1)S(1)}, u32[]{:S(2)}, u32[]{:S(2)}) collective-permute-start(bf16[1040,128]{1,0:T(8,128)(2,1)S(1)} %collective-permute-done.1.refs_2_), channel_id=1, source_target_pairs={{0,1},{1,0},{2,3},{3,2},{4,5},{5,4},{6,7},{7,6},{8,9},{9,8},{10,11... | collective-permute-start | bytes 798728 | tf_op jit(solution)/shard_map/ppermute | solution.py:150
  24.9 2.8 %collective-permute-start.8 = (bf16[1040,128]{1,0:T(8,128)(2,1)S(1)}, bf16[1040,128]{1,0:T(8,128)(2,1)S(1)}, u32[]{:S(2)}, u32[]{:S(2)}) collective-permute-start(bf16[1040,128]{1,0:T(8,128)(2,1)S(1)} %collective-permute-done.3.refs_4_), channel_id=1, source_target_pairs={{0,1},{1,0},{2,3},{3,2},{4,5},{5,4},{6,7},{7,6},{8,9},{9,8},{10,11... | collective-permute-start | bytes 798728 | tf_op jit(solution)/shard_map/ppermute | solution.py:150
  26.2 1.7 %collective-permute-start.7 = (bf16[1040,128]{1,0:T(8,128)(2,1)S(1)}, bf16[1040,128]{1,0:T(8,128)(2,1)}, u32[]{:S(2)}, u32[]{:S(2)}) collective-permute-start(bf16[1040,128]{1,0:T(8,128)(2,1)S(1)} %collective-permute-done.2.refs_3_), channel_id=1, source_target_pairs={{0,1},{1,0},{2,3},{3,2},{4,5},{5,4},{6,7},{7,6},{8,9},{9,8},{10,11... | collective-permute-start | bytes 798728 | tf_op jit(solution)/shard_map/ppermute | solution.py:150
  26.2 1.7 %copy-start.3 = (s32[16]{0:T(128)S(1)}, s32[16]{0:T(128)}, u32[]{:S(2)}) copy-start(s32[16]{0:T(128)} %length_ref.1) | copy-start | bytes 196

commit v2 on v1

v2 whole, which is shorter than its diff:
```python
import functools
import math

import jax
import jax.numpy as jnp
from jax import lax
from jax.experimental import pallas as pl
from jax.experimental.pallas import tpu as pltpu
from jax.sharding import PartitionSpec as P

NEG = -1e30
VMEM = pltpu.MemorySpace.VMEM
SMEM = pltpu.MemorySpace.SMEM
HBM = pltpu.MemorySpace.HBM
F32 = jnp.float32
BF16 = jnp.bfloat16
WHOLE = pl.BlockSpec(memory_space=VMEM)
SCALE_ROWS = 16
CHUNK = 256


def pack_kernel(k_ref, v_ref, ks_ref, vs_ref, out_ref, rows_ref):
    tokens, heads, width = k_ref.shape
    for part, ref in enumerate((k_ref, v_ref)):
        rows_ref[part] = ref[...].astype(F32).reshape(tokens * heads, width)
        for head in range(heads):
            start = (part * heads + head) * tokens
            rows = rows_ref[part, pl.ds(head, tokens, stride=heads), :]
            out_ref[start : start + tokens, :] = rows.astype(out_ref.dtype)
    held = ks_ref.shape[1]
    row = lax.broadcasted_iota(jnp.int32, (SCALE_ROWS, held), 0)
    col = lax.broadcasted_iota(jnp.int32, (SCALE_ROWS, held), 1)
    k_scale = jnp.broadcast_to(ks_ref[...].astype(F32), row.shape)
    v_scale = jnp.broadcast_to(vs_ref[...].astype(F32), row.shape)
    both = jnp.where(row == col, k_scale, 0.0) + jnp.where(row == col + held, v_scale, 0.0)
    both = jnp.broadcast_to(jnp.sum(both, axis=1, keepdims=True), (SCALE_ROWS, width))
    out_ref[2 * heads * tokens :, :] = both.astype(out_ref.dtype)


def pack(keys, values, key_scales, value_scales):
    tokens, heads, width = keys.shape
    args = [pltpu.with_memory_space_constraint(x, HBM) for x in (keys, values, key_scales, value_scales)]
    return pl.pallas_call(
        pack_kernel,
        out_shape=jax.ShapeDtypeStruct((2 * heads * tokens + SCALE_ROWS, width), keys.dtype),
        grid=(1,),
        in_specs=[pl.BlockSpec(x.shape, lambda i, n=x.ndim: (0,) * n) for x in (keys, values, key_scales, value_scales)],
        out_specs=WHOLE,
        scratch_shapes=[pltpu.VMEM((2, tokens * heads, width), F32)],
        compiler_params=pltpu.CompilerParams(vmem_limit_bytes=8 * 2**20),
        name="pack",
    )(*args)


def scales_of(mine, sibling, heads, tokens, first):
    low = 2 * heads * tokens
    out = []
    for m, s in zip(mine, sibling):
        a, z = m[low:, :].astype(F32), s[low:, :].astype(F32)
        a, z = jnp.where(a > 0, a, 1.0), jnp.where(z > 0, z, 1.0)
        out.append((jnp.where(first, a, z), jnp.where(first, z, a)))
    return out


def attend_blocks(get_q, put, mask, mine, sibling, scale, heads, tokens, group, width, old):
    count = len(mine)
    block = 2 * tokens
    rows = tokens * group
    local = heads // 2
    chunk = min(CHUNK, rows)
    row_token = lax.broadcasted_iota(jnp.int32, (rows, width), 0) // group
    one_hot = jnp.where(row_token == lax.broadcasted_iota(jnp.int32, (rows, width), 1), 1.0, 0.0).astype(BF16)
    of_key = lax.broadcasted_iota(jnp.int32, (block * count, width), 0) // block
    ones = jnp.where(of_key == lax.broadcasted_iota(jnp.int32, (block * count, width), 1), 1.0, 0.0).astype(BF16)
    units = [(h, slice(r, r + chunk)) for h in range(heads) for r in range(0, rows, chunk)]
    ready = {}

    def stacked(at):
        return jnp.concatenate([r[at : at + tokens, :] for b in range(count) for r in (mine[b], sibling[b])], axis=0)

    def wide(x):
        return jnp.concatenate([x] * (chunk // width), axis=1)

    def prepared(h):
        if h not in ready:
            keys = jnp.concatenate([stacked(h * tokens), mask], axis=1)
            q = jnp.concatenate([get_q(h), one_hot], axis=1)
            part, at = h // local, h % local
            ks = [wide(s[part][at : at + 1, :] * (math.log2(math.e) / math.sqrt(width))) for s in scale]
            vs = [wide(s[part][local + at : local + at + 1, :]) for s in scale]
            ready[h] = keys, q, ks, [jnp.log2(v) for v in vs], [1.0 / v for v in vs]
        return ready[h]

    def scores_of(h, cs):
        keys, q = prepared(h)[:2]
        return lax.dot_general(keys, q[cs], (((1,), (1,)), ((), ())), preferred_element_type=F32)

    def softmax(h, cs, scores):
        ks, lv = prepared(h)[2:4]
        parts = [scores[b * block : (b + 1) * block] * ks[b] for b in range(count)]
        top = functools.reduce(jnp.maximum, [jnp.max(p, axis=0, keepdims=True) for p in parts])
        factor = None
        if old is not None:
            before = old[0][h : h + 1, cs]
            top = jnp.maximum(top, before)
            factor = jnp.exp2(before - top)
        weights = [jnp.exp2(parts[b] - (top - lv[b])).astype(BF16) for b in range(count)]
        return jnp.concatenate(weights, axis=0), top, factor

    def finish(h, cs, weights, top, factor):
        iv = prepared(h)[4]
        values = jnp.concatenate([stacked((heads + h) * tokens), ones], axis=1)
        acc = lax.dot_general(values, weights, (((0,), (0,)), ((), ())), preferred_element_type=F32)
        total = functools.reduce(jnp.add, [acc[width + b : width + b + 1] * iv[b] for b in range(count)])
        acc = acc[:width]
        if factor is not None:
            total = total + old[1][h : h + 1, cs] * factor
            acc = acc + old[2][h, :, cs] * factor
        put(h, cs, acc, top, total)

    scores = scores_of(*units[0])
    waiting = None
    for i, (h, cs) in enumerate(units):
        following = scores_of(*units[i + 1]) if i + 1 < len(units) else None
        done = softmax(h, cs, scores)
        if waiting is not None:
            finish(*waiting)
        waiting = (h, cs) + done
        scores = following
    finish(*waiting)


def early_kernel(count, late, heads, group, place_ref, length_ref, q_ref, *refs):
    mine, sibling = refs[:count], refs[count : 2 * count]
    acc_ref, top_ref, sum_ref, qh_ref, mask_ref, q_buf, q_sem = refs[2 * count :]
    tokens, _, width = q_ref.shape
    rows, block, pair = tokens * group, 2 * tokens, 2 * group
    copies = [
        pltpu.make_async_copy(q_ref.at[:, pl.ds(g * pair, pair), :], q_buf.at[g], q_sem.at[g]) for g in range(heads // 2)
    ]
    for copy in copies:
        copy.start()
    core = place_ref[1]
    position = place_ref[0] + lax.broadcasted_iota(jnp.int32, (8, width), 1)

    def later(i, carry):
        start, end = carry
        end = end + length_ref[i]
        return jnp.where(position >= end, end, start), end

    start, _ = lax.fori_loop(0, length_ref.shape[0], later, (jnp.zeros_like(position), jnp.int32(0)))
    start, position = start[:1], position[:1]
    i = lax.broadcasted_iota(jnp.int32, (block, width), 0)
    offset = jnp.where(i < tokens, core * tokens + i, (1 - core) * tokens + i - tokens)

    def mask(b):
        key = place_ref[2 + b] + offset
        return jnp.where((key >= start) & (key <= position), 0.0, NEG).astype(BF16)

    for b in range(late):
        mask_ref[b * block : (b + 1) * block, :] = mask(count + b)
    here = jnp.concatenate([mask(b) for b in range(count)], axis=0)
    scale = scales_of(mine, sibling, heads, tokens, core == 0)

    def get_q(h):
        if h % 2 == 0:
            copies[h // 2].wait()
        q = q_buf[h // 2][:, (h % 2) * group : (h % 2 + 1) * group, :].reshape(rows, width)
        qh_ref[h] = q
        return q

    def put(h, cs, acc, top, total):
        acc_ref[h, :, cs] = acc
        top_ref[h : h + 1, cs] = top
        sum_ref[h : h + 1, cs] = total

    attend_blocks(get_q, put, here, mine, sibling, scale, heads, tokens, group, width, None)


def last_kernel(count, heads, group, qh_ref, mask_ref, acc_ref, top_ref, sum_ref, *refs):
    mine, sibling = refs[:count], refs[count : 2 * count]
    out_ref, o_buf, o_sem = refs[2 * count :]
    _, rows, width = qh_ref.shape
    tokens, pair = rows // group, 2 * group
    scale = scales_of(mine, sibling, heads, tokens, lax.axis_index("tp") == 0)
    copies = []

    def put(h, cs, acc, top, total):
        out = (acc / total).T.astype(BF16)
        span = slice(cs.start // group, cs.stop // group)
        o_buf[h // 2, span, (h % 2) * group : (h % 2 + 1) * group, :] = out.reshape(span.stop - span.start, group, width)
        if h % 2 == 1 and cs.stop == rows:
            g = h // 2
            copies.append(pltpu.make_async_copy(o_buf.at[g], out_ref.at[:, pl.ds(g * pair, pair), :], o_sem.at[g]))
            copies[-1].start()

    attend_blocks(
        lambda h: qh_ref[h], put, mask_ref[...], mine, sibling, scale, heads, tokens, group, width, (top_ref, sum_ref, acc_ref)
    )
    for copy in copies:
        copy.wait()


def cost(tokens, q_heads, width, blocks):
    work = tokens * q_heads * blocks * 2 * tokens
    return pl.CostEstimate(flops=4 * work * width, bytes_accessed=2 * tokens * q_heads * width, transcendentals=work)


def early(queries, place, lengths, mine, sibling, late, heads):
    tokens, q_heads, width = queries.shape
    group, count = q_heads // heads, len(mine)
    rows = tokens * group
    shape = jax.ShapeDtypeStruct
    return pl.pallas_call(
        functools.partial(early_kernel, count, late, heads, group),
        out_shape=[
            shape((heads, width, rows), F32),
            shape((heads, rows), F32),
            shape((heads, rows), F32),
            shape((heads, rows, width), BF16),
            shape((late * 2 * tokens, width), BF16),
        ],
        in_specs=[pl.BlockSpec(memory_space=SMEM)] * 2 + [pl.BlockSpec(memory_space=HBM)] + [WHOLE] * (2 * count),
        out_specs=[WHOLE] * 5,
        scratch_shapes=[
            pltpu.VMEM((heads // 2, tokens, 2 * group, width), BF16),
            pltpu.SemaphoreType.DMA((heads // 2,)),
        ],
        compiler_params=pltpu.CompilerParams(vmem_limit_bytes=24 * 2**20),
        cost_estimate=cost(tokens, q_heads, width, count),
        name="early",
    )(place, lengths, pltpu.with_memory_space_constraint(queries, HBM), *mine, *sibling)


def last(state, mine, sibling, heads):
    acc, top, total, qh, mask = state
    _, rows, width = qh.shape
    count = len(mine)
    tokens = mask.shape[0] // (2 * count)
    group = rows // tokens
    return pl.pallas_call(
        functools.partial(last_kernel, count, heads, group),
        out_shape=jax.ShapeDtypeStruct((tokens, heads * group, width), BF16),
        in_specs=[WHOLE] * (5 + 2 * count),
        out_specs=pl.BlockSpec(memory_space=HBM),
        scratch_shapes=[
            pltpu.VMEM((heads // 2, tokens, 2 * group, width), BF16),
            pltpu.SemaphoreType.DMA((heads // 2,)),
        ],
        compiler_params=pltpu.CompilerParams(vmem_limit_bytes=24 * 2**20),
        cost_estimate=cost(tokens, heads * group, width, count),
        name="last",
    )(qh, mask, acc, top, total, *mine, *sibling)


def shards(queries, keys, values, key_scales, value_scales, lengths):
    tokens, heads, _ = keys.shape
    ranks = lax.axis_size("ctx")
    c, t = lax.axis_index("ctx"), lax.axis_index("tp")
    block = tokens * lax.axis_size("tp")
    own = pack(keys, values, key_scales, value_scales)

    def send(value, target):
        pairs = [(source, target(source)) for source in range(ranks)]
        return lax.ppermute(value, "ctx", [(i, j) for i, j in pairs if 0 <= j < ranks])

    def swap(value):
        return lax.ppermute(value, "tp", [(0, 1), (1, 0)])

    k = c % 4
    from_z = send(own, lambda i: (i + 4) % ranks)
    from_d = send(own, lambda i: i + (3 if i % 2 == 0 else 1))
    to_x = jnp.where(k % 2 == 0, own, from_z)
    to_y = jnp.where(k < 2, own, from_z)
    from_x = send(to_x, lambda i: i ^ 1)
    from_y = send(to_y, lambda i: i ^ 2)
    mine = [own, from_z, from_d, from_x, from_y]
    even = k % 2 == 0
    back = [0, 4, jnp.where(even, 1, 3), jnp.where(even, 3, 1), 2]
    sibling = [swap(part) for part in mine]
    place = jnp.stack([c * block + t * tokens, t] + [(c - b) * block for b in back]).astype(jnp.int32)
    state = early(queries, place, lengths, mine[:3], sibling[:3], 2, heads)
    return last(state, mine[3:], sibling[3:], heads)


def solution(mesh):
    both = P(("ctx", "tp"), None, None)
    return jax.shard_map(
        shards,
        mesh=mesh,
        in_specs=(both, both, both, P("ctx", "tp"), P("ctx", "tp"), P()),
        out_specs=both,
        check_vma=False,
    )
```

time: 37 us -> 31.3 us (0.85)
  waiting for transfers between devices: 8.79 us -> 6.66 us
  local copies, waits for them, and re-layouts: 2.65 us -> 0.73 us
  starting transfers between devices: 16.1 us -> 15.3 us
  Pallas kernels: 8.98 us -> 8.29 us
    ppermute x4, starting transfers between devices: 9.93 us -> 7.93 us  [send(): lax.ppermute(value, 'ctx', [(i, j) for i, j in pairs if 0 <= j < ranks])]
    unnamed x12 -> x2, local copies, waits for them, and re-layouts: 2.49 us -> 0.65 us
    pallas_call x1 -> x2, Pallas kernels: 8.86 us -> 7.2 us  [the longest x1 4.72 us: early(): pl.pallas_call(functools.partial(early_kernel, count, late, heads, group)...]
    ppermute x5, waiting for transfers between devices: 1.57 us -> 0.01 us  [swap(): return lax.ppermute(value, 'tp', [(0, 1), (1, 0)])]
    ppermute x5, starting transfers between devices: 6.21 us -> 7.41 us  [swap(): return lax.ppermute(value, 'tp', [(0, 1), (1, 0)])]
    pallas_call x1, Pallas kernels: 0.12 us -> 1.09 us  [pack(): pl.pallas_call(pack_kernel, out_shape=jax.ShapeDtypeStruct((2 * heads * t...]
    ppermute x4, waiting for transfers between devices: 7.21 us -> 6.65 us  [send(): lax.ppermute(value, 'ctx', [(i, j) for i, j in pairs if 0 <= j < ranks])]
  transfers between devices with their start and end apart: 9 -> 9, of which waited for: 5 -> 4; matrix products, arithmetic and copies ran while one was open for 0% -> 0% of each run, Pallas kernels for 0% -> 15%
where the time goes in v2:
time: 31.3 us; the launch traced here: 31.2 us
  starting transfers between devices  15.3 us (49%)
  Pallas kernels  8.29 us (26%)
  waiting for transfers between devices  6.66 us (21%)
  local copies, waits for them, and re-layouts  0.73 us (2%)
    ppermute x4, starting transfers between devices, send(): lax.ppermute(value, 'ctx', [(i, j) for i, j in pairs if 0 <= j < ranks])  7.93 us
    ppermute x5, starting transfers between devices, swap(): return lax.ppermute(value, 'tp', [(0, 1), (1, 0)])  7.41 us
    ppermute x4, waiting for transfers between devices, send(): lax.ppermute(value, 'ctx', [(i, j) for i, j in pairs if 0 <= j < ranks])  6.65 us
    pallas_call x1, Pallas kernels, early(): pl.pallas_call(functools.partial(early_kernel, count, late, heads, group)...  4.72 us
    pallas_call x1, Pallas kernels, last(): pl.pallas_call(functools.partial(last_kernel, count, heads, group), out_s...  2.49 us
    pallas_call x1, Pallas kernels, pack(): pl.pallas_call(pack_kernel, out_shape=jax.ShapeDtypeStruct((2 * heads * t...  1.09 us
    unnamed x2, local copies, waits for them, and re-layouts  0.65 us
  transfers between devices with their start and end apart: 9, of which 4 were waited for; matrix products, arithmetic and copies ran while one was open for 0% of the time, Pallas kernels for 15%

profile of v2, /device:TPU:9, one launch (start us, length us, event | category | flops | bytes accessed | tf_op | source)
XLA Modules:
  0.0 31.2 jit_solution(1023536540668980932)
XLA Ops:
  0.0 1.1 %pack.1.refs_0_ = bf16[1040,128]{1,0:T(8,128)(2,1)S(1)} custom-call(bf16[64,8,128]{2,1,0:T(8,128)(2,1)} %k_ref.1, bf16[64,8,128]{2,1,0:T(8,128)(2,1)} %v_ref.1, bf16[1,4]{1,0:T(2,128)(2,1)} %ks_ref.1, bf16[1,4]{1,0:T(2,128)(2,1)} %vs_ref.1), custom_call_target="tpu_custom_call" | custom-call | tf_op jit(solution)/shard_map/pack/pallas_call | solution.py:43
  1.1 1.3 %collective-permute-start = (bf16[1040,128]{1,0:T(8,128)(2,1)S(1)}, bf16[1040,128]{1,0:T(8,128)(2,1)S(1)}, u32[]{:S(2)}, u32[]{:S(2)}) collective-permute-start(bf16[1040,128]{1,0:T(8,128)(2,1)S(1)} %pack.1.refs_0_), channel_id=1, source_target_pairs={{0,8},{2,10},{4,12},{6,14},{8,16},{10,18},{12,20},{14,22},{16,24},... | collective-permute-start | bytes 798728 | tf_op jit(solution)/shard_map/ppermute | solution.py:265
  2.4 4.1 %collective-permute-start.1 = (bf16[1040,128]{1,0:T(8,128)(2,1)S(1)}, bf16[1040,128]{1,0:T(8,128)(2,1)S(1)}, u32[]{:S(2)}, u32[]{:S(2)}) collective-permute-start(bf16[1040,128]{1,0:T(8,128)(2,1)S(1)} %pack.1.refs_0_), channel_id=1, source_target_pairs={{0,6},{2,4},{4,10},{6,8},{8,14},{10,12},{12,18},{14,16},{16,22},{1... | collective-permute-start | bytes 798728 | tf_op jit(solution)/shard_map/ppermute | solution.py:265
  6.5 1.9 %collective-permute-done.refs_1_ = bf16[1040,128]{1,0:T(8,128)(2,1)S(1)} collective-permute-done((bf16[1040,128]{1,0:T(8,128)(2,1)S(1)}, bf16[1040,128]{1,0:T(8,128)(2,1)S(1)}, u32[]{:S(2)}, u32[]{:S(2)}) %collective-permute-start) | collective-permute-done | bytes 266272 | tf_op jit(solution)/shard_map/ppermute | solution.py:265
  8.5 1.3 %collective-permute-start.5 = (bf16[1040,128]{1,0:T(8,128)(2,1)S(1)}, bf16[1040,128]{1,0:T(8,128)(2,1)S(1)}, u32[]{:S(2)}, u32[]{:S(2)}) collective-permute-start(bf16[1040,128]{1,0:T(8,128)(2,1)S(1)} %get-tuple-element.16), channel_id=1, source_target_pairs={{0,2},{2,0},{4,6},{6,4},{8,10},{10,8},{12,14},{14,12},{16,18},{18,... | collective-permute-start | bytes 798728 | tf_op jit(solution)/shard_map/ppermute | solution.py:265
  9.7 1.2 %collective-permute-start.6 = (bf16[1040,128]{1,0:T(8,128)(2,1)S(1)}, bf16[1040,128]{1,0:T(8,128)(2,1)S(1)}, u32[]{:S(2)}, u32[]{:S(2)}) collective-permute-start(bf16[1040,128]{1,0:T(8,128)(2,1)S(1)} %get-tuple-element.15), channel_id=1, source_target_pairs={{0,4},{2,6},{4,0},{6,2},{8,12},{10,14},{12,8},{14,10},{16,20},{18,... | collective-permute-start | bytes 798728 | tf_op jit(solution)/shard_map/ppermute | solution.py:265
  11.0 3.3 %collective-permute-start.2 = (bf16[1040,128]{1,0:T(8,128)(2,1)S(1)}, bf16[1040,128]{1,0:T(8,128)(2,1)S(1)}, u32[]{:S(2)}, u32[]{:S(2)}) collective-permute-start(bf16[1040,128]{1,0:T(8,128)(2,1)S(1)} %pack.1.refs_0_), channel_id=1, source_target_pairs={{0,1},{1,0},{2,3},{3,2},{4,5},{5,4},{6,7},{7,6},{8,9},{9,8},{10,11... | collective-permute-start | bytes 798728 | tf_op jit(solution)/shard_map/ppermute | solution.py:268
  14.2 0.0 collective-permute-start.3
  14.2 1.8 %collective-permute-done.1.refs_2_ = bf16[1040,128]{1,0:T(8,128)(2,1)S(1)} collective-permute-done((bf16[1040,128]{1,0:T(8,128)(2,1)S(1)}, bf16[1040,128]{1,0:T(8,128)(2,1)S(1)}, u32[]{:S(2)}, u32[]{:S(2)}) %collective-permute-start.1) | collective-permute-done | bytes 266272 | tf_op jit(solution)/shard_map/ppermute | solution.py:265
  16.0 1.7 %collective-permute-start.4 = (bf16[1040,128]{1,0:T(8,128)(2,1)S(1)}, bf16[1040,128]{1,0:T(8,128)(2,1)S(1)}, u32[]{:S(2)}, u32[]{:S(2)}) collective-permute-start(bf16[1040,128]{1,0:T(8,128)(2,1)S(1)} %collective-permute-done.1.refs_2_), channel_id=1, source_target_pairs={{0,1},{1,0},{2,3},{3,2},{4,5},{5,4},{6,7},{7,6},{8,9},{9,8},{10,11... | collective-permute-start | bytes 798728 | tf_op jit(solution)/shard_map/ppermute | solution.py:268
  17.7 0.2 collective-permute-done.5.refs_0_
  17.9 1.9 %collective-permute-start.7 = (bf16[1040,128]{1,0:T(8,128)(2,1)S(1)}, bf16[1040,128]{1,0:T(8,128)(2,1)S(1)}, u32[]{:S(2)}, u32[]{:S(2)}) collective-permute-start(bf16[1040,128]{1,0:T(8,128)(2,1)S(1)} %collective-permute-done.5.refs_0_), channel_id=1, source_target_pairs={{0,1},{1,0},{2,3},{3,2},{4,5},{5,4},{6,7},{7,6},{8,9},{9,8},{10,11... | collective-permute-start | bytes 798728 | tf_op jit(solution)/shard_map/ppermute | solution.py:268
  19.8 2.8 %collective-permute-done.6.refs_1_ = bf16[1040,128]{1,0:T(8,128)(2,1)S(1)} collective-permute-done((bf16[1040,128]{1,0:T(8,128)(2,1)S(1)}, bf16[1040,128]{1,0:T(8,128)(2,1)S(1)}, u32[]{:S(2)}, u32[]{:S(2)}) %collective-permute-start.6) | collective-permute-done | bytes 266272 | tf_op jit(solution)/shard_map/ppermute | solution.py:265
  22.5 0.6 %collective-permute-start.8 = (bf16[1040,128]{1,0:T(8,128)(2,1)S(1)}, bf16[1040,128]{1,0:T(8,128)(2,1)S(1)}, u32[]{:S(2)}, u32[]{:S(2)}) collective-permute-start(bf16[1040,128]{1,0:T(8,128)(2,1)S(1)} %collective-permute-done.6.refs_1_), channel_id=1, source_target_pairs={{0,1},{1,0},{2,3},{3,2},{4,5},{5,4},{6,7},{7,6},{8,9},{9,8},{10,11... | collective-permute-start | bytes 798728 | tf_op jit(solution)/shard_map/ppermute | solution.py:268
  23.2 0.1 stack.31.place_ref
  23.3 0.0 collective-permute-done.2.refs_3_
  23.3 0.0 collective-permute-done.3.refs_4_
  23.3 0.0 collective-permute-done.4.refs_5_
  23.3 0.0 copy-start
  23.3 0.6 %copy-done = s32[16]{0:T(128)S(1)} copy-done((s32[16]{0:T(128)S(1)}, s32[16]{0:T(128)}, u32[]{:S(2)}) %copy-start) | copy-done | bytes 88
  23.9 4.7 %early.1 = (f32[8,128,512]{2,1,0:T(8,128)S(1)}, f32[8,512]{1,0:T(8,128)S(1)}, f32[8,512]{1,0:T(8,128)S(1)}, bf16[8,512,128]{2,1,0:T(8,128)(2,1)S(1)}, bf16[256,128]{1,0:T(8,128)(2,1)S(1)}) custom-call(s32[7]{0:T(128)S(1)} %stack.31.place_ref, s32[16]{0:T(128)S(1)} %copy-done, bf16[64,64,128]{2,1,0:T(8,128)(2,1)} %q_ref.1, ...), custom_call_target="tpu_custom_call" | custom-call | flops 805306368 | bytes 1048576 | tf_op jit(solution)/shard_map/early/pallas_call | solution.py:214
  28.7 0.0 collective-permute-done.7.refs_2_
  28.7 0.0 collective-permute-done.8.refs_3_
  28.7 2.5 %last.1 = bf16[64,64,128]{2,1,0:T(8,128)(2,1)} custom-call(bf16[8,512,128]{2,1,0:T(8,128)(2,1)S(1)} %get-tuple-element.10.qh_ref, bf16[256,128]{1,0:T(8,128)(2,1)S(1)} %get-tuple-element.11.mask_ref, f32[8,128,512]{2,1,0:T(8,128)S(1)} %get-tuple-element.12.acc_ref, f32[8,512]{1,0:T(8,128)S(1)} %get-tuple-element.13.top_ref, ...), custom_call_target="tpu_custom_call" | custom-call | flops 536870912 | bytes 1048576 | tf_op jit(solution)/shard_map/last/pallas_call | solution.py:241
  (1 shorter events, 0.0 us)
Async XLA Ops:
  1.1 7.3 %collective-permute-start = (bf16[1040,128]{1,0:T(8,128)(2,1)S(1)}, bf16[1040,128]{1,0:T(8,128)(2,1)S(1)}, u32[]{:S(2)}, u32[]{:S(2)}) collective-permute-start(bf16[1040,128]{1,0:T(8,128)(2,1)S(1)} %pack.1.refs_0_), channel_id=1, source_target_pairs={{0,8},{2,10},{4,12},{6,14},{8,16},{10,18},{12,20},{14,22},{16,24},... | collective-permute-start | bytes 798728 | tf_op jit(solution)/shard_map/ppermute | solution.py:265
  2.4 13.6 %collective-permute-start.1 = (bf16[1040,128]{1,0:T(8,128)(2,1)S(1)}, bf16[1040,128]{1,0:T(8,128)(2,1)S(1)}, u32[]{:S(2)}, u32[]{:S(2)}) collective-permute-start(bf16[1040,128]{1,0:T(8,128)(2,1)S(1)} %pack.1.refs_0_), channel_id=1, source_target_pairs={{0,6},{2,4},{4,10},{6,8},{8,14},{10,12},{12,18},{14,16},{16,22},{1... | collective-permute-start | bytes 798728 | tf_op jit(solution)/shard_map/ppermute | solution.py:265
  8.5 9.5 %collective-permute-start.5 = (bf16[1040,128]{1,0:T(8,128)(2,1)S(1)}, bf16[1040,128]{1,0:T(8,128)(2,1)S(1)}, u32[]{:S(2)}, u32[]{:S(2)}) collective-permute-start(bf16[1040,128]{1,0:T(8,128)(2,1)S(1)} %get-tuple-element.16), channel_id=1, source_target_pairs={{0,2},{2,0},{4,6},{6,4},{8,10},{10,8},{12,14},{14,12},{16,18},{18,... | collective-permute-start | bytes 798728 | tf_op jit(solution)/shard_map/ppermute | solution.py:265
  9.7 12.8 %collective-permute-start.6 = (bf16[1040,128]{1,0:T(8,128)(2,1)S(1)}, bf16[1040,128]{1,0:T(8,128)(2,1)S(1)}, u32[]{:S(2)}, u32[]{:S(2)}) collective-permute-start(bf16[1040,128]{1,0:T(8,128)(2,1)S(1)} %get-tuple-element.15), channel_id=1, source_target_pairs={{0,4},{2,6},{4,0},{6,2},{8,12},{10,14},{12,8},{14,10},{16,20},{18,... | collective-permute-start | bytes 798728 | tf_op jit(solution)/shard_map/ppermute | solution.py:265
  11.0 12.3 %collective-permute-start.2 = (bf16[1040,128]{1,0:T(8,128)(2,1)S(1)}, bf16[1040,128]{1,0:T(8,128)(2,1)S(1)}, u32[]{:S(2)}, u32[]{:S(2)}) collective-permute-start(bf16[1040,128]{1,0:T(8,128)(2,1)S(1)} %pack.1.refs_0_), channel_id=1, source_target_pairs={{0,1},{1,0},{2,3},{3,2},{4,5},{5,4},{6,7},{7,6},{8,9},{9,8},{10,11... | collective-permute-start | bytes 798728 | tf_op jit(solution)/shard_map/ppermute | solution.py:268
  14.2 9.0 %collective-permute-start.3 = (bf16[1040,128]{1,0:T(8,128)(2,1)S(1)}, bf16[1040,128]{1,0:T(8,128)(2,1)S(1)}, u32[]{:S(2)}, u32[]{:S(2)}) collective-permute-start(bf16[1040,128]{1,0:T(8,128)(2,1)S(1)} %collective-permute-done.refs_1_), channel_id=1, source_target_pairs={{0,1},{1,0},{2,3},{3,2},{4,5},{5,4},{6,7},{7,6},{8,9},{9,8},{10,11... | collective-permute-start | bytes 798728 | tf_op jit(solution)/shard_map/ppermute | solution.py:268
  16.0 7.2 %collective-permute-start.4 = (bf16[1040,128]{1,0:T(8,128)(2,1)S(1)}, bf16[1040,128]{1,0:T(8,128)(2,1)S(1)}, u32[]{:S(2)}, u32[]{:S(2)}) collective-permute-start(bf16[1040,128]{1,0:T(8,128)(2,1)S(1)} %collective-permute-done.1.refs_2_), channel_id=1, source_target_pairs={{0,1},{1,0},{2,3},{3,2},{4,5},{5,4},{6,7},{7,6},{8,9},{9,8},{10,11... | collective-permute-start | bytes 798728 | tf_op jit(solution)/shard_map/ppermute | solution.py:268
  17.9 10.7 %collective-permute-start.7 = (bf16[1040,128]{1,0:T(8,128)(2,1)S(1)}, bf16[1040,128]{1,0:T(8,128)(2,1)S(1)}, u32[]{:S(2)}, u32[]{:S(2)}) collective-permute-start(bf16[1040,128]{1,0:T(8,128)(2,1)S(1)} %collective-permute-done.5.refs_0_), channel_id=1, source_target_pairs={{0,1},{1,0},{2,3},{3,2},{4,5},{5,4},{6,7},{7,6},{8,9},{9,8},{10,11... | collective-permute-start | bytes 798728 | tf_op jit(solution)/shard_map/ppermute | solution.py:268
  22.5 6.1 %collective-permute-start.8 = (bf16[1040,128]{1,0:T(8,128)(2,1)S(1)}, bf16[1040,128]{1,0:T(8,128)(2,1)S(1)}, u32[]{:S(2)}, u32[]{:S(2)}) collective-permute-start(bf16[1040,128]{1,0:T(8,128)(2,1)S(1)} %collective-permute-done.6.refs_1_), channel_id=1, source_target_pairs={{0,1},{1,0},{2,3},{3,2},{4,5},{5,4},{6,7},{7,6},{8,9},{9,8},{10,11... | collective-permute-start | bytes 798728 | tf_op jit(solution)/shard_map/ppermute | solution.py:268
  23.3 0.7 %copy-start = (s32[16]{0:T(128)S(1)}, s32[16]{0:T(128)}, u32[]{:S(2)}) copy-start(s32[16]{0:T(128)} %length_ref.1) | copy-start | bytes 196

commit v3 on v2

--- a/solution.py
+++ b/solution.py
@@ -132,7 +132,8 @@
 
 def early_kernel(count, late, heads, group, place_ref, length_ref, q_ref, *refs):
     mine, sibling = refs[:count], refs[count : 2 * count]
-    acc_ref, top_ref, sum_ref, qh_ref, mask_ref, q_buf, q_sem = refs[2 * count :]
+    acc_ref, top_ref, sum_ref, qh_ref = refs[2 * count : 2 * count + 4]
+    masks, (q_buf, q_sem) = refs[2 * count + 4 : -2], refs[-2:]
     tokens, _, width = q_ref.shape
     rows, block, pair = tokens * group, 2 * tokens, 2 * group
     copies = [
@@ -158,7 +159,7 @@
         return jnp.where((key >= start) & (key <= position), 0.0, NEG).astype(BF16)
 
     for b in range(late):
-        mask_ref[b * block : (b + 1) * block, :] = mask(count + b)
+        masks[b][...] = mask(count + b)
     here = jnp.concatenate([mask(b) for b in range(count)], axis=0)
     scale = scales_of(mine, sibling, heads, tokens, core == 0)
 
@@ -177,12 +178,30 @@
     attend_blocks(get_q, put, here, mine, sibling, scale, heads, tokens, group, width, None)
 
 
-def last_kernel(count, heads, group, qh_ref, mask_ref, acc_ref, top_ref, sum_ref, *refs):
+def middle_kernel(count, heads, group, qh_ref, mask_ref, acc_ref, top_ref, sum_ref, *refs):
     mine, sibling = refs[:count], refs[count : 2 * count]
-    out_ref, o_buf, o_sem = refs[2 * count :]
+    acc_out, top_out, sum_out = refs[2 * count :]
+    _, rows, width = qh_ref.shape
+    tokens = rows // group
+    scale = scales_of(mine, sibling, heads, tokens, lax.axis_index("tp") == 0)
+
+    def put(h, cs, acc, top, total):
+        acc_out[h, :, cs] = acc
+        top_out[h : h + 1, cs] = top
+        sum_out[h : h + 1, cs] = total
+
+    attend_blocks(
+        lambda h: qh_ref[h], put, mask_ref[...], mine, sibling, scale, heads, tokens, group, width, (top_ref, sum_ref, acc_ref)
+    )
+
+
+def last_kernel(count, heads, group, qh_ref, acc_ref, top_ref, sum_ref, *refs):
+    masks, mine, sibling = refs[:count], refs[count : 2 * count], refs[2 * count : 3 * count]
+    out_ref, o_buf, o_sem = refs[3 * count :]
     _, rows, width = qh_ref.shape
     tokens, pair = rows // group, 2 * group
     scale = scales_of(mine, sibling, heads, tokens, lax.axis_index("tp") == 0)
+    mask = jnp.concatenate([ref[...] for ref in masks], axis=0)
     copies = []
 
     def put(h, cs, acc, top, total):
@@ -195,7 +214,7 @@
             copies[-1].start()
 
     attend_blocks(
-        lambda h: qh_ref[h], put, mask_ref[...], mine, sibling, scale, heads, tokens, group, width, (top_ref, sum_ref, acc_ref)
+        lambda h: qh_ref[h], put, mask, mine, sibling, scale, heads, tokens, group, width, (top_ref, sum_ref, acc_ref)
     )
     for copy in copies:
         copy.wait()
@@ -218,10 +237,10 @@
             shape((heads, rows), F32),
             shape((heads, rows), F32),
             shape((heads, rows, width), BF16),
-            shape((late * 2 * tokens, width), BF16),
-        ],
+        ]
+        + [shape((2 * tokens, width), BF16)] * late,
         in_specs=[pl.BlockSpec(memory_space=SMEM)] * 2 + [pl.BlockSpec(memory_space=HBM)] + [WHOLE] * (2 * count),
-        out_specs=[WHOLE] * 5,
+        out_specs=[WHOLE] * (4 + late),
         scratch_shapes=[
             pltpu.VMEM((heads // 2, tokens, 2 * group, width), BF16),
             pltpu.SemaphoreType.DMA((heads // 2,)),
@@ -232,16 +251,29 @@
     )(place, lengths, pltpu.with_memory_space_constraint(queries, HBM), *mine, *sibling)
 
 
-def last(state, mine, sibling, heads):
-    acc, top, total, qh, mask = state
-    _, rows, width = qh.shape
-    count = len(mine)
-    tokens = mask.shape[0] // (2 * count)
+def middle(state, qh, mask, mine, sibling):
+    heads, rows, width = qh.shape
+    tokens = mask.shape[0] // 2
+    group = rows // tokens
+    return pl.pallas_call(
+        functools.partial(middle_kernel, 1, heads, group),
+        out_shape=[jax.ShapeDtypeStruct(x.shape, x.dtype) for x in state],
+        in_specs=[WHOLE] * 7,
+        out_specs=[WHOLE] * 3,
+        compiler_params=pltpu.CompilerParams(vmem_limit_bytes=24 * 2**20),
+        cost_estimate=cost(tokens, heads * group, width, 1),
+        name="middle",
+    )(qh, mask, *state, mine, sibling)
+
+
+def last(state, qh, masks, mine, sibling):
+    heads, rows, width = qh.shape
+    count, tokens = len(mine), masks[0].shape[0] // 2
     group = rows // tokens
     return pl.pallas_call(
         functools.partial(last_kernel, count, heads, group),
         out_shape=jax.ShapeDtypeStruct((tokens, heads * group, width), BF16),
-        in_specs=[WHOLE] * (5 + 2 * count),
+        in_specs=[WHOLE] * (4 + 3 * count),
         out_specs=pl.BlockSpec(memory_space=HBM),
         scratch_shapes=[
             pltpu.VMEM((heads // 2, tokens, 2 * group, width), BF16),
@@ -250,7 +282,7 @@
         compiler_params=pltpu.CompilerParams(vmem_limit_bytes=24 * 2**20),
         cost_estimate=cost(tokens, heads * group, width, count),
         name="last",
-    )(qh, mask, acc, top, total, *mine, *sibling)
+    )(qh, *state, *masks, *mine, *sibling)
 
 
 def shards(queries, keys, values, key_scales, value_scales, lengths):
@@ -274,13 +306,19 @@
     to_y = jnp.where(k < 2, own, from_z)
     from_x = send(to_x, lambda i: i ^ 1)
     from_y = send(to_y, lambda i: i ^ 2)
-    mine = [own, from_z, from_d, from_x, from_y]
     even = k % 2 == 0
     back = [0, 4, jnp.where(even, 1, 3), jnp.where(even, 3, 1), 2]
-    sibling = [swap(part) for part in mine]
     place = jnp.stack([c * block + t * tokens, t] + [(c - b) * block for b in back]).astype(jnp.int32)
-    state = early(queries, place, lengths, mine[:3], sibling[:3], 2, heads)
-    return last(state, mine[3:], sibling[3:], heads)
+
+    acc, top, total, qh, mask_d, mask_x, mask_y = early(
+        queries, place, lengths, [own, from_z], [swap(own), swap(from_z)], 3, heads
+    )
+    from_d, top = lax.optimization_barrier((from_d, top))
+    beside_d = swap(from_d)
+    from_x, from_y, top, beside_d = lax.optimization_barrier((from_x, from_y, top, beside_d))
+    beside = [swap(from_x), swap(from_y)]
+    state = middle((acc, top, total), qh, mask_d, from_d, beside_d)
+    return last(state, qh, [mask_x, mask_y], [from_x, from_y], beside)
 
 
 def solution(mesh):

time: 31.3 us -> 28.1 us (0.90)
  waiting for transfers between devices: 6.66 us -> 4.37 us
  starting transfers between devices: 15.3 us -> 13.1 us
  Pallas kernels: 8.29 us -> 9.62 us
    ppermute x5, starting transfers between devices: 7.41 us -> 3.99 us  [swap(): return lax.ppermute(value, 'tp', [(0, 1), (1, 0)])]
    ppermute x4, waiting for transfers between devices: 6.65 us -> 4.36 us  [send(): lax.ppermute(value, 'ctx', [(i, j) for i, j in pairs if 0 <= j < ranks])]
    pallas_call x0 -> x1, Pallas kernels: none -> 1.95 us  [middle(): pl.pallas_call(functools.partial(middle_kernel, 1, heads, group), out_sha...]
    ppermute x4, starting transfers between devices: 7.93 us -> 9.07 us  [send(): lax.ppermute(value, 'ctx', [(i, j) for i, j in pairs if 0 <= j < ranks])]
    pallas_call x1, Pallas kernels: 4.72 us -> 4.01 us  [early(): pl.pallas_call(functools.partial(early_kernel, count, late, heads, group)...]
  transfers between devices with their start and end apart: 9 -> 9, of which waited for: 4 -> 2; matrix products, arithmetic and copies ran while one was open for 0% -> 0% of each run, Pallas kernels for 15% -> 21%
where the time goes in v3:
time: 28.1 us; the launch traced here: 27.9 us
  starting transfers between devices  13.1 us (47%)
  Pallas kernels  9.62 us (34%)
  waiting for transfers between devices  4.37 us (16%)
  local copies, waits for them, and re-layouts  0.74 us (3%)
    ppermute x4, starting transfers between devices, send(): lax.ppermute(value, 'ctx', [(i, j) for i, j in pairs if 0 <= j < ranks])  9.07 us
    ppermute x4, waiting for transfers between devices, send(): lax.ppermute(value, 'ctx', [(i, j) for i, j in pairs if 0 <= j < ranks])  4.36 us
    pallas_call x1, Pallas kernels, early(): pl.pallas_call(functools.partial(early_kernel, count, late, heads, group)...  4.01 us
    ppermute x5, starting transfers between devices, swap(): return lax.ppermute(value, 'tp', [(0, 1), (1, 0)])  3.99 us
    pallas_call x1, Pallas kernels, last(): pl.pallas_call(functools.partial(last_kernel, count, heads, group), out_s...  2.58 us
    pallas_call x1, Pallas kernels, middle(): pl.pallas_call(functools.partial(middle_kernel, 1, heads, group), out_sha...  1.95 us
    pallas_call x1, Pallas kernels, pack(): pl.pallas_call(pack_kernel, out_shape=jax.ShapeDtypeStruct((2 * heads * t...  1.09 us
    unnamed x2, local copies, waits for them, and re-layouts  0.65 us
  transfers between devices with their start and end apart: 9, of which 2 were waited for; matrix products, arithmetic and copies ran while one was open for 0% of the time, Pallas kernels for 21%

profile of v3, /device:TPU:9, one launch (start us, length us, event | category | flops | bytes accessed | tf_op | source)
XLA Modules:
  0.0 27.9 jit_solution(17886221247821119734)
XLA Ops:
  0.0 1.1 %pack.1.refs_0_ = bf16[1040,128]{1,0:T(8,128)(2,1)S(1)} custom-call(bf16[64,8,128]{2,1,0:T(8,128)(2,1)} %k_ref.1, bf16[64,8,128]{2,1,0:T(8,128)(2,1)} %v_ref.1, bf16[1,4]{1,0:T(2,128)(2,1)} %ks_ref.1, bf16[1,4]{1,0:T(2,128)(2,1)} %vs_ref.1), custom_call_target="tpu_custom_call" | custom-call | tf_op jit(solution)/shard_map/pack/pallas_call | solution.py:43
  1.1 1.3 %collective-permute-start = (bf16[1040,128]{1,0:T(8,128)(2,1)S(1)}, bf16[1040,128]{1,0:T(8,128)(2,1)S(1)}, u32[]{:S(2)}, u32[]{:S(2)}) collective-permute-start(bf16[1040,128]{1,0:T(8,128)(2,1)S(1)} %pack.1.refs_0_), channel_id=1, source_target_pairs={{0,8},{2,10},{4,12},{6,14},{8,16},{10,18},{12,20},{14,22},{16,24},... | collective-permute-start | bytes 798728 | tf_op jit(solution)/shard_map/ppermute | solution.py:297
  2.4 4.1 %collective-permute-start.5 = (bf16[1040,128]{1,0:T(8,128)(2,1)S(1)}, bf16[1040,128]{1,0:T(8,128)(2,1)S(1)}, u32[]{:S(2)}, u32[]{:S(2)}) collective-permute-start(bf16[1040,128]{1,0:T(8,128)(2,1)S(1)} %pack.1.refs_0_), channel_id=1, source_target_pairs={{0,6},{2,4},{4,10},{6,8},{8,14},{10,12},{12,18},{14,16},{16,22},{1... | collective-permute-start | bytes 798728 | tf_op jit(solution)/shard_map/ppermute | solution.py:297
  6.5 1.3 %collective-permute-start.1 = (bf16[1040,128]{1,0:T(8,128)(2,1)S(1)}, bf16[1040,128]{1,0:T(8,128)(2,1)S(1)}, u32[]{:S(2)}, u32[]{:S(2)}) collective-permute-start(bf16[1040,128]{1,0:T(8,128)(2,1)S(1)} %pack.1.refs_0_), channel_id=1, source_target_pairs={{0,1},{1,0},{2,3},{3,2},{4,5},{5,4},{6,7},{7,6},{8,9},{9,8},{10,11... | collective-permute-start | bytes 798728 | tf_op jit(solution)/shard_map/ppermute | solution.py:300
  7.8 0.1 stack.31.place_ref
  7.9 0.5 %collective-permute-done.refs_1_ = bf16[1040,128]{1,0:T(8,128)(2,1)S(1)} collective-permute-done((bf16[1040,128]{1,0:T(8,128)(2,1)S(1)}, bf16[1040,128]{1,0:T(8,128)(2,1)S(1)}, u32[]{:S(2)}, u32[]{:S(2)}) %collective-permute-start) | collective-permute-done | bytes 266272 | tf_op jit(solution)/shard_map/ppermute | solution.py:297
  8.4 1.5 %collective-permute-start.2 = (bf16[1040,128]{1,0:T(8,128)(2,1)S(1)}, bf16[1040,128]{1,0:T(8,128)(2,1)S(1)}, u32[]{:S(2)}, u32[]{:S(2)}) collective-permute-start(bf16[1040,128]{1,0:T(8,128)(2,1)S(1)} %collective-permute-done.refs_1_), channel_id=1, source_target_pairs={{0,1},{1,0},{2,3},{3,2},{4,5},{5,4},{6,7},{7,6},{8,9},{9,8},{10,11... | collective-permute-start | bytes 798728 | tf_op jit(solution)/shard_map/ppermute | solution.py:300
  10.0 2.5 %collective-permute-start.4 = (bf16[1040,128]{1,0:T(8,128)(2,1)S(1)}, bf16[1040,128]{1,0:T(8,128)(2,1)S(1)}, u32[]{:S(2)}, u32[]{:S(2)}) collective-permute-start(bf16[1040,128]{1,0:T(8,128)(2,1)S(1)} %get-tuple-element.37), channel_id=1, source_target_pairs={{0,4},{2,6},{4,0},{6,2},{8,12},{10,14},{12,8},{14,10},{16,20},{18,... | collective-permute-start | bytes 798728 | tf_op jit(solution)/shard_map/ppermute | solution.py:297
  12.5 1.2 %collective-permute-start.3 = (bf16[1040,128]{1,0:T(8,128)(2,1)S(1)}, bf16[1040,128]{1,0:T(8,128)(2,1)S(1)}, u32[]{:S(2)}, u32[]{:S(2)}) collective-permute-start(bf16[1040,128]{1,0:T(8,128)(2,1)S(1)} %get-tuple-element.38), channel_id=1, source_target_pairs={{0,2},{2,0},{4,6},{6,4},{8,10},{10,8},{12,14},{14,12},{16,18},{18,... | collective-permute-start | bytes 798728 | tf_op jit(solution)/shard_map/ppermute | solution.py:297
  13.7 0.0 collective-permute-done.1.refs_2_
  13.7 0.0 collective-permute-done.2.refs_3_
  13.7 0.7 %copy-done = s32[16]{0:T(128)S(1)} copy-done((s32[16]{0:T(128)S(1)}, s32[16]{0:T(128)}, u32[]{:S(2)}) %copy-start) | copy-done | bytes 88
  14.3 4.0 %early.1 = (f32[8,128,512]{2,1,0:T(8,128)S(1)}, f32[8,512]{1,0:T(8,128)S(1)}, f32[8,512]{1,0:T(8,128)S(1)}, bf16[8,512,128]{2,1,0:T(8,128)(2,1)S(1)}, bf16[128,1...) custom-call(s32[7]{0:T(128)S(1)} %stack.31.place_ref, s32[16]{0:T(128)S(1)} %copy-done, ...), custom_call_target="tpu_custom_call" | custom-call | flops 536870912 | bytes 1048576 | tf_op jit(solution)/shard_map/early/pallas_call | solution.py:233
  18.4 0.0 collective-permute-done.5.refs_0_
  18.4 0.6 %collective-permute-start.6 = (bf16[1040,128]{1,0:T(8,128)(2,1)S(1)}, bf16[1040,128]{1,0:T(8,128)(2,1)S(1)}, u32[]{:S(2)}, u32[]{:S(2)}) collective-permute-start(bf16[1040,128]{1,0:T(8,128)(2,1)S(1)} %collective-permute-done.5.refs_0_), channel_id=1, source_target_pairs={{0,1},{1,0},{2,3},{3,2},{4,5},{5,4},{6,7},{7,6},{8,9},{9,8},{10,11... | collective-permute-start | bytes 798728 | tf_op jit(solution)/shard_map/ppermute | solution.py:300
  19.0 3.8 %collective-permute-done.4.refs_3_ = bf16[1040,128]{1,0:T(8,128)(2,1)S(1)} collective-permute-done((bf16[1040,128]{1,0:T(8,128)(2,1)S(1)}, bf16[1040,128]{1,0:T(8,128)(2,1)S(1)}, u32[]{:S(2)}, u32[]{:S(2)}) %collective-permute-start.4) | collective-permute-done | bytes 266272 | tf_op jit(solution)/shard_map/ppermute | solution.py:297
  22.8 0.0 collective-permute-done.3.refs_2_
  22.8 0.0 collective-permute-done.6.refs_1_
  22.8 0.4 %collective-permute-start.7 = (bf16[1040,128]{1,0:T(8,128)(2,1)S(1)}, bf16[1040,128]{1,0:T(8,128)(2,1)S(1)}, u32[]{:S(2)}, u32[]{:S(2)}) collective-permute-start(bf16[1040,128]{1,0:T(8,128)(2,1)S(1)} %collective-permute-done.3.refs_2_), channel_id=1, source_target_pairs={{0,1},{1,0},{2,3},{3,2},{4,5},{5,4},{6,7},{7,6},{8,9},{9,8},{10,11... | collective-permute-start | bytes 798728 | tf_op jit(solution)/shard_map/ppermute | solution.py:300
  23.3 0.1 collective-permute-start.8
  23.4 1.9 %middle.1 = (f32[8,128,512]{2,1,0:T(8,128)S(1)}, f32[8,512]{1,0:T(8,128)S(1)}, f32[8,512]{1,0:T(8,128)S(1)}) custom-call(bf16[8,512,128]{2,1,0:T(8,128)(2,1)S(1)} %get-tuple-element.21.qh_ref, bf16[128,128]{1,0:T(8,128)(2,1)S(1)} %get-tuple-element.22.mask_ref, f32[8,128,512]{2,1,0:T(8,128)S(1)} %get-tuple-element.23.acc_ref, ...), custom_call_target="tpu_custom_call" | custom-call | flops 268435456 | bytes 1048576 | tf_op jit(solution)/shard_map/middle/pallas_call | solution.py:258
  25.3 0.0 collective-permute-done.7.refs_4_
  25.3 0.0 collective-permute-done.8.refs_5_
  25.3 2.6 %last.1 = bf16[64,64,128]{2,1,0:T(8,128)(2,1)} custom-call(bf16[8,512,128]{2,1,0:T(8,128)(2,1)S(1)} %get-tuple-element.21.qh_ref, f32[8,128,512]{2,1,0:T(8,128)S(1)} %get-tuple-element.30.acc_ref, f32[8,512]{1,0:T(8,128)S(1)} %get-tuple-element.31.top_ref, f32[8,512]{1,0:T(8,128)S(1)} %get-tuple-element.32.sum_ref, ...), custom_call_target="tpu_custom_call" | custom-call | flops 536870912 | bytes 1048576 | tf_op jit(solution)/shard_map/last/pallas_call | solution.py:273
  (2 shorter events, 0.0 us)
Async XLA Ops:
  1.1 7.3 %collective-permute-start = (bf16[1040,128]{1,0:T(8,128)(2,1)S(1)}, bf16[1040,128]{1,0:T(8,128)(2,1)S(1)}, u32[]{:S(2)}, u32[]{:S(2)}) collective-permute-start(bf16[1040,128]{1,0:T(8,128)(2,1)S(1)} %pack.1.refs_0_), channel_id=1, source_target_pairs={{0,8},{2,10},{4,12},{6,14},{8,16},{10,18},{12,20},{14,22},{16,24},... | collective-permute-start | bytes 798728 | tf_op jit(solution)/shard_map/ppermute | solution.py:297
  2.4 15.9 %collective-permute-start.5 = (bf16[1040,128]{1,0:T(8,128)(2,1)S(1)}, bf16[1040,128]{1,0:T(8,128)(2,1)S(1)}, u32[]{:S(2)}, u32[]{:S(2)}) collective-permute-start(bf16[1040,128]{1,0:T(8,128)(2,1)S(1)} %pack.1.refs_0_), channel_id=1, source_target_pairs={{0,6},{2,4},{4,10},{6,8},{8,14},{10,12},{12,18},{14,16},{16,22},{1... | collective-permute-start | bytes 798728 | tf_op jit(solution)/shard_map/ppermute | solution.py:297
  6.5 7.2 %collective-permute-start.1 = (bf16[1040,128]{1,0:T(8,128)(2,1)S(1)}, bf16[1040,128]{1,0:T(8,128)(2,1)S(1)}, u32[]{:S(2)}, u32[]{:S(2)}) collective-permute-start(bf16[1040,128]{1,0:T(8,128)(2,1)S(1)} %pack.1.refs_0_), channel_id=1, source_target_pairs={{0,1},{1,0},{2,3},{3,2},{4,5},{5,4},{6,7},{7,6},{8,9},{9,8},{10,11... | collective-permute-start | bytes 798728 | tf_op jit(solution)/shard_map/ppermute | solution.py:300
  8.4 5.3 %collective-permute-start.2 = (bf16[1040,128]{1,0:T(8,128)(2,1)S(1)}, bf16[1040,128]{1,0:T(8,128)(2,1)S(1)}, u32[]{:S(2)}, u32[]{:S(2)}) collective-permute-start(bf16[1040,128]{1,0:T(8,128)(2,1)S(1)} %collective-permute-done.refs_1_), channel_id=1, source_target_pairs={{0,1},{1,0},{2,3},{3,2},{4,5},{5,4},{6,7},{7,6},{8,9},{9,8},{10,11... | collective-permute-start | bytes 798728 | tf_op jit(solution)/shard_map/ppermute | solution.py:300
  10.0 12.8 %collective-permute-start.4 = (bf16[1040,128]{1,0:T(8,128)(2,1)S(1)}, bf16[1040,128]{1,0:T(8,128)(2,1)S(1)}, u32[]{:S(2)}, u32[]{:S(2)}) collective-permute-start(bf16[1040,128]{1,0:T(8,128)(2,1)S(1)} %get-tuple-element.37), channel_id=1, source_target_pairs={{0,4},{2,6},{4,0},{6,2},{8,12},{10,14},{12,8},{14,10},{16,20},{18,... | collective-permute-start | bytes 798728 | tf_op jit(solution)/shard_map/ppermute | solution.py:297
  12.5 10.4 %collective-permute-start.3 = (bf16[1040,128]{1,0:T(8,128)(2,1)S(1)}, bf16[1040,128]{1,0:T(8,128)(2,1)S(1)}, u32[]{:S(2)}, u32[]{:S(2)}) collective-permute-start(bf16[1040,128]{1,0:T(8,128)(2,1)S(1)} %get-tuple-element.38), channel_id=1, source_target_pairs={{0,2},{2,0},{4,6},{6,4},{8,10},{10,8},{12,14},{14,12},{16,18},{18,... | collective-permute-start | bytes 798728 | tf_op jit(solution)/shard_map/ppermute | solution.py:297
  13.7 0.7 %copy-start = (s32[16]{0:T(128)S(1)}, s32[16]{0:T(128)}, u32[]{:S(2)}) copy-start(s32[16]{0:T(128)} %length_ref.1) | copy-start | bytes 196
  18.4 4.5 %collective-permute-start.6 = (bf16[1040,128]{1,0:T(8,128)(2,1)S(1)}, bf16[1040,128]{1,0:T(8,128)(2,1)S(1)}, u32[]{:S(2)}, u32[]{:S(2)}) collective-permute-start(bf16[1040,128]{1,0:T(8,128)(2,1)S(1)} %collective-permute-done.5.refs_0_), channel_id=1, source_target_pairs={{0,1},{1,0},{2,3},{3,2},{4,5},{5,4},{6,7},{7,6},{8,9},{9,8},{10,11... | collective-permute-start | bytes 798728 | tf_op jit(solution)/shard_map/ppermute | solution.py:300
  22.8 2.5 %collective-permute-start.7 = (bf16[1040,128]{1,0:T(8,128)(2,1)S(1)}, bf16[1040,128]{1,0:T(8,128)(2,1)S(1)}, u32[]{:S(2)}, u32[]{:S(2)}) collective-permute-start(bf16[1040,128]{1,0:T(8,128)(2,1)S(1)} %collective-permute-done.3.refs_2_), channel_id=1, source_target_pairs={{0,1},{1,0},{2,3},{3,2},{4,5},{5,4},{6,7},{7,6},{8,9},{9,8},{10,11... | collective-permute-start | bytes 798728 | tf_op jit(solution)/shard_map/ppermute | solution.py:300
  23.3 2.1 %collective-permute-start.8 = (bf16[1040,128]{1,0:T(8,128)(2,1)S(1)}, bf16[1040,128]{1,0:T(8,128)(2,1)S(1)}, u32[]{:S(2)}, u32[]{:S(2)}) collective-permute-start(bf16[1040,128]{1,0:T(8,128)(2,1)S(1)} %collective-permute-done.4.refs_3_), channel_id=1, source_target_pairs={{0,1},{1,0},{2,3},{3,2},{4,5},{5,4},{6,7},{7,6},{8,9},{9,8},{10,11... | collective-permute-start | bytes 798728 | tf_op jit(solution)/shard_map/ppermute | solution.py:300

commit v4 on v3

--- a/solution.py
+++ b/solution.py
@@ -10,13 +10,13 @@
 
 NEG = -1e30
 VMEM = pltpu.MemorySpace.VMEM
-SMEM = pltpu.MemorySpace.SMEM
 HBM = pltpu.MemorySpace.HBM
 F32 = jnp.float32
 BF16 = jnp.bfloat16
 WHOLE = pl.BlockSpec(memory_space=VMEM)
 SCALE_ROWS = 16
 CHUNK = 256
+GATHERED = 2
 
 
 def pack_kernel(k_ref, v_ref, ks_ref, vs_ref, out_ref, rows_ref):
@@ -130,60 +130,62 @@
     finish(*waiting)
 
 
-def early_kernel(count, late, heads, group, place_ref, length_ref, q_ref, *refs):
-    mine, sibling = refs[:count], refs[count : 2 * count]
-    acc_ref, top_ref, sum_ref, qh_ref = refs[2 * count : 2 * count + 4]
-    masks, (q_buf, q_sem) = refs[2 * count + 4 : -2], refs[-2:]
+def prepare_kernel(heads, group, length_hbm, q_ref, qh_ref, *refs):
+    masks, (length_ref, length_sem, q_buf, q_sem) = refs[:-4], refs[-4:]
     tokens, _, width = q_ref.shape
     rows, block, pair = tokens * group, 2 * tokens, 2 * group
     copies = [
         pltpu.make_async_copy(q_ref.at[:, pl.ds(g * pair, pair), :], q_buf.at[g], q_sem.at[g]) for g in range(heads // 2)
     ]
+    lengths = pltpu.make_async_copy(length_hbm, length_ref, length_sem)
+    lengths.start()
     for copy in copies:
         copy.start()
-    core = place_ref[1]
-    position = place_ref[0] + lax.broadcasted_iota(jnp.int32, (8, width), 1)
+    chip, core = lax.axis_index("ctx"), lax.axis_index("tp")
+    even = chip % 2 == 0
+    position = chip * block + core * tokens + lax.broadcasted_iota(jnp.int32, (8, width), 1)
 
     def later(i, carry):
         start, end = carry
         end = end + length_ref[i]
         return jnp.where(position >= end, end, start), end
 
+    lengths.wait()
     start, _ = lax.fori_loop(0, length_ref.shape[0], later, (jnp.zeros_like(position), jnp.int32(0)))
     start, position = start[:1], position[:1]
     i = lax.broadcasted_iota(jnp.int32, (block, width), 0)
     offset = jnp.where(i < tokens, core * tokens + i, (1 - core) * tokens + i - tokens)
-
-    def mask(b):
-        key = place_ref[2 + b] + offset
-        return jnp.where((key >= start) & (key <= position), 0.0, NEG).astype(BF16)
-
-    for b in range(late):
-        masks[b][...] = mask(count + b)
-    here = jnp.concatenate([mask(b) for b in range(count)], axis=0)
-    scale = scales_of(mine, sibling, heads, tokens, core == 0)
-
-    def get_q(h):
+    for b, back in enumerate((0, 4, jnp.where(even, 1, 3), jnp.where(even, 3, 1), 2)):
+        key = (chip - back) * block + (i if b == GATHERED else offset)
+        masks[b][...] = jnp.where((key >= start) & (key <= position), 0.0, NEG).astype(BF16)
+    for h in range(heads):
         if h % 2 == 0:
             copies[h // 2].wait()
-        q = q_buf[h // 2][:, (h % 2) * group : (h % 2 + 1) * group, :].reshape(rows, width)
-        qh_ref[h] = q
-        return q
+        qh_ref[h] = q_buf[h // 2][:, (h % 2) * group : (h % 2 + 1) * group, :].reshape(rows, width)
+
+
+def early_kernel(count, heads, group, qh_ref, *refs):
+    masks, mine, sibling = refs[:count], refs[count : 2 * count], refs[2 * count : 3 * count]
+    acc_ref, top_ref, sum_ref = refs[3 * count :]
+    _, rows, width = qh_ref.shape
+    tokens = rows // group
+    scale = scales_of(mine, sibling, heads, tokens, lax.axis_index("tp") == 0)
+    mask = jnp.concatenate([ref[...] for ref in masks], axis=0)
 
     def put(h, cs, acc, top, total):
         acc_ref[h, :, cs] = acc
         top_ref[h : h + 1, cs] = top
         sum_ref[h : h + 1, cs] = total
 
-    attend_blocks(get_q, put, here, mine, sibling, scale, heads, tokens, group, width, None)
-
-
-def middle_kernel(count, heads, group, qh_ref, mask_ref, acc_ref, top_ref, sum_ref, *refs):
-    mine, sibling = refs[:count], refs[count : 2 * count]
-    acc_out, top_out, sum_out = refs[2 * count :]
+    attend_blocks(lambda h: qh_ref[h], put, mask, mine, sibling, scale, heads, tokens, group, width, None)
+
+
+def middle_kernel(heads, group, qh_ref, mask_ref, acc_ref, top_ref, sum_ref, both_ref, acc_out, top_out, sum_out):
     _, rows, width = qh_ref.shape
     tokens = rows // group
-    scale = scales_of(mine, sibling, heads, tokens, lax.axis_index("tp") == 0)
+    size = both_ref.shape[0] // 2
+    mine, sibling = [both_ref.at[:size]], [both_ref.at[size:]]
+    scale = scales_of(mine, sibling, heads, tokens, True)
 
     def put(h, cs, acc, top, total):
         acc_out[h, :, cs] = acc
@@ -225,45 +227,56 @@
     return pl.CostEstimate(flops=4 * work * width, bytes_accessed=2 * tokens * q_heads * width, transcendentals=work)
 
 
-def early(queries, place, lengths, mine, sibling, late, heads):
+def prepare(queries, lengths, heads, blocks=5):
     tokens, q_heads, width = queries.shape
-    group, count = q_heads // heads, len(mine)
-    rows = tokens * group
-    shape = jax.ShapeDtypeStruct
-    return pl.pallas_call(
-        functools.partial(early_kernel, count, late, heads, group),
-        out_shape=[
-            shape((heads, width, rows), F32),
-            shape((heads, rows), F32),
-            shape((heads, rows), F32),
-            shape((heads, rows, width), BF16),
-        ]
-        + [shape((2 * tokens, width), BF16)] * late,
-        in_specs=[pl.BlockSpec(memory_space=SMEM)] * 2 + [pl.BlockSpec(memory_space=HBM)] + [WHOLE] * (2 * count),
-        out_specs=[WHOLE] * (4 + late),
+    group = q_heads // heads
+    out = [((heads, tokens * group, width), BF16)] + [((2 * tokens, width), BF16)] * blocks
+    qh, *masks = pl.pallas_call(
+        functools.partial(prepare_kernel, heads, group),
+        out_shape=[jax.ShapeDtypeStruct(*x) for x in out],
+        in_specs=[pl.BlockSpec(memory_space=HBM)] * 2,
+        out_specs=[WHOLE] * (1 + blocks),
         scratch_shapes=[
+            pltpu.SMEM(lengths.shape, lengths.dtype),
+            pltpu.SemaphoreType.DMA,
             pltpu.VMEM((heads // 2, tokens, 2 * group, width), BF16),
             pltpu.SemaphoreType.DMA((heads // 2,)),
         ],
         compiler_params=pltpu.CompilerParams(vmem_limit_bytes=24 * 2**20),
-        cost_estimate=cost(tokens, q_heads, width, count),
+        name="prepare",
+    )(*(pltpu.with_memory_space_constraint(x, HBM) for x in (lengths, queries)))
+    return qh, masks
+
+
+def early(qh, masks, mine, sibling):
+    heads, rows, width = qh.shape
+    count, tokens = len(mine), masks[0].shape[0] // 2
+    group = rows // tokens
+    shape = jax.ShapeDtypeStruct
+    return pl.pallas_call(
+        functools.partial(early_kernel, count, heads, group),
+        out_shape=[shape((heads, width, rows), F32), shape((heads, rows), F32), shape((heads, rows), F32)],
+        in_specs=[WHOLE] * (1 + 3 * count),
+        out_specs=[WHOLE] * 3,
+        compiler_params=pltpu.CompilerParams(vmem_limit_bytes=24 * 2**20),
+        cost_estimate=cost(tokens, heads * group, width, count),
         name="early",
-    )(place, lengths, pltpu.with_memory_space_constraint(queries, HBM), *mine, *sibling)
-
-
-def middle(state, qh, mask, mine, sibling):
+    )(qh, *masks, *mine, *sibling)
+
+
+def middle(state, qh, mask, both):
     heads, rows, width = qh.shape
     tokens = mask.shape[0] // 2
     group = rows // tokens
     return pl.pallas_call(
-        functools.partial(middle_kernel, 1, heads, group),
+        functools.partial(middle_kernel, heads, group),
         out_shape=[jax.ShapeDtypeStruct(x.shape, x.dtype) for x in state],
-        in_specs=[WHOLE] * 7,
+        in_specs=[WHOLE] * 6,
         out_specs=[WHOLE] * 3,
         compiler_params=pltpu.CompilerParams(vmem_limit_bytes=24 * 2**20),
         cost_estimate=cost(tokens, heads * group, width, 1),
         name="middle",
-    )(qh, mask, *state, mine, sibling)
+    )(qh, mask, *state, both)
 
 
 def last(state, qh, masks, mine, sibling):
@@ -288,8 +301,7 @@
 def shards(queries, keys, values, key_scales, value_scales, lengths):
     tokens, heads, _ = keys.shape
     ranks = lax.axis_size("ctx")
-    c, t = lax.axis_index("ctx"), lax.axis_index("tp")
-    block = tokens * lax.axis_size("tp")
+    c = lax.axis_index("ctx")
     own = pack(keys, values, key_scales, value_scales)
 
     def send(value, target):
@@ -300,25 +312,19 @@
         return lax.ppermute(value, "tp", [(0, 1), (1, 0)])
 
     k = c % 4
+    even = k % 2 == 0
     from_z = send(own, lambda i: (i + 4) % ranks)
     from_d = send(own, lambda i: i + (3 if i % 2 == 0 else 1))
-    to_x = jnp.where(k % 2 == 0, own, from_z)
-    to_y = jnp.where(k < 2, own, from_z)
-    from_x = send(to_x, lambda i: i ^ 1)
-    from_y = send(to_y, lambda i: i ^ 2)
-    even = k % 2 == 0
-    back = [0, 4, jnp.where(even, 1, 3), jnp.where(even, 3, 1), 2]
-    place = jnp.stack([c * block + t * tokens, t] + [(c - b) * block for b in back]).astype(jnp.int32)
-
-    acc, top, total, qh, mask_d, mask_x, mask_y = early(
-        queries, place, lengths, [own, from_z], [swap(own), swap(from_z)], 3, heads
-    )
+    qh, masks = prepare(queries, lengths, heads)
+    from_z, masks[0] = lax.optimization_barrier((from_z, masks[0]))
+    from_x = send(jnp.where(even, own, from_z), lambda i: i ^ 1)
+    from_y = send(jnp.where(k < 2, own, from_z), lambda i: i ^ 2)
+    acc, top, total = early(qh, masks[:2], [own, from_z], [swap(own), swap(from_z)])
     from_d, top = lax.optimization_barrier((from_d, top))
-    beside_d = swap(from_d)
-    from_x, from_y, top, beside_d = lax.optimization_barrier((from_x, from_y, top, beside_d))
-    beside = [swap(from_x), swap(from_y)]
-    state = middle((acc, top, total), qh, mask_d, from_d, beside_d)
-    return last(state, qh, [mask_x, mask_y], [from_x, from_y], beside)
+    both_d = lax.all_gather(from_d, "tp", axis=0, tiled=True)
+    acc, top, total = middle((acc, top, total), qh, masks[GATHERED], both_d)
+    from_x, from_y, top = lax.optimization_barrier((from_x, from_y, top))
+    return last((acc, top, total), qh, masks[3:], [from_x, from_y], [swap(from_x), swap(from_y)])
 
 
 def solution(mesh):

time: 28.1 us -> 27.5 us (0.979)
  blocking collectives: 0 us -> 3.51 us
  starting transfers between devices: 13.1 us -> 11.7 us
  Pallas kernels: 9.62 us -> 8.42 us
  waiting for transfers between devices: 4.37 us -> 3.6 us
  local copies, waits for them, and re-layouts: 0.74 us -> 0 us
    all_gather x0 -> x1, blocking collectives: none -> 3.51 us  [shards(): both_d = lax.all_gather(from_d, 'tp', axis=0, tiled=True)]
    ppermute x4, waiting for transfers between devices: 4.36 us -> 2.15 us  [send(): lax.ppermute(value, 'ctx', [(i, j) for i, j in pairs if 0 <= j < ranks])]
    ppermute x5 -> x4, waiting for transfers between devices: 0.01 us -> 1.45 us  [swap(): return lax.ppermute(value, 'tp', [(0, 1), (1, 0)])]
    ppermute x5 -> x4, starting transfers between devices: 3.99 us -> 2.65 us  [swap(): return lax.ppermute(value, 'tp', [(0, 1), (1, 0)])]
    pallas_call x2 -> x3, Pallas kernels: 5.96 us -> 4.79 us  [the longest x1 1.94 us: middle(): pl.pallas_call(functools.partial(middle_kernel, heads, group), out_shape=...]
    unnamed x2 -> x0, local copies, waits for them, and re-layouts: 0.65 us -> none
  transfers between devices with their start and end apart: 9 -> 8, of which waited for: 2 -> 4; matrix products, arithmetic and copies ran while one was open for 0% -> 0% of each run, Pallas kernels for 21% -> 17%
where the time goes in v4:
time: 27.5 us; the launch traced here: 27.4 us
  starting transfers between devices  11.7 us (43%)
  Pallas kernels  8.42 us (31%)
  waiting for transfers between devices  3.6 us (13%)
  blocking collectives  3.51 us (13%)
    ppermute x4, starting transfers between devices, send(): lax.ppermute(value, 'ctx', [(i, j) for i, j in pairs if 0 <= j < ranks])  9.07 us
    all_gather x1, blocking collectives, shards(): both_d = lax.all_gather(from_d, 'tp', axis=0, tiled=True)  3.51 us
    ppermute x4, starting transfers between devices, swap(): return lax.ppermute(value, 'tp', [(0, 1), (1, 0)])  2.65 us
    pallas_call x1, Pallas kernels, last(): pl.pallas_call(functools.partial(last_kernel, count, heads, group), out_s...  2.55 us
    ppermute x4, waiting for transfers between devices, send(): lax.ppermute(value, 'ctx', [(i, j) for i, j in pairs if 0 <= j < ranks])  2.15 us
    pallas_call x1, Pallas kernels, middle(): pl.pallas_call(functools.partial(middle_kernel, heads, group), out_shape=...  1.94 us
    pallas_call x1, Pallas kernels, early(): pl.pallas_call(functools.partial(early_kernel, count, heads, group), out_...  1.56 us
    ppermute x4, waiting for transfers between devices, swap(): return lax.ppermute(value, 'tp', [(0, 1), (1, 0)])  1.45 us
  transfers between devices with their start and end apart: 8, of which 4 were waited for; matrix products, arithmetic and copies ran while one was open for 0% of the time, Pallas kernels for 17%

profile of v4, /device:TPU:9, one launch (start us, length us, event | category | flops | bytes accessed | tf_op | source)
XLA Modules:
  0.0 27.4 jit_solution(12586599107633850208)
XLA Ops:
  0.0 1.1 %pack.1.refs_2_ = bf16[1040,128]{1,0:T(8,128)(2,1)S(1)} custom-call(bf16[64,8,128]{2,1,0:T(8,128)(2,1)} %k_ref.1, bf16[64,8,128]{2,1,0:T(8,128)(2,1)} %v_ref.1, bf16[1,4]{1,0:T(2,128)(2,1)} %ks_ref.1, bf16[1,4]{1,0:T(2,128)(2,1)} %vs_ref.1), custom_call_target="tpu_custom_call" | custom-call | tf_op jit(solution)/shard_map/pack/pallas_call | solution.py:43
  1.1 1.3 %collective-permute-start = (bf16[1040,128]{1,0:T(8,128)(2,1)S(1)}, bf16[1040,128]{1,0:T(8,128)(2,1)S(1)}, u32[]{:S(2)}, u32[]{:S(2)}) collective-permute-start(bf16[1040,128]{1,0:T(8,128)(2,1)S(1)} %pack.1.refs_2_), channel_id=1, source_target_pairs={{0,8},{2,10},{4,12},{6,14},{8,16},{10,18},{12,20},{14,22},{16,24},... | collective-permute-start | bytes 798728 | tf_op jit(solution)/shard_map/ppermute | solution.py:309
  2.4 4.1 %collective-permute-start.3 = (bf16[1040,128]{1,0:T(8,128)(2,1)S(1)}, bf16[1040,128]{1,0:T(8,128)(2,1)S(1)}, u32[]{:S(2)}, u32[]{:S(2)}) collective-permute-start(bf16[1040,128]{1,0:T(8,128)(2,1)S(1)} %pack.1.refs_2_), channel_id=1, source_target_pairs={{0,6},{2,4},{4,10},{6,8},{8,14},{10,12},{12,18},{14,16},{16,22},{1... | collective-permute-start | bytes 798728 | tf_op jit(solution)/shard_map/ppermute | solution.py:309
  6.5 1.3 %collective-permute-start.1 = (bf16[1040,128]{1,0:T(8,128)(2,1)S(1)}, bf16[1040,128]{1,0:T(8,128)(2,1)S(1)}, u32[]{:S(2)}, u32[]{:S(2)}) collective-permute-start(bf16[1040,128]{1,0:T(8,128)(2,1)S(1)} %pack.1.refs_2_), channel_id=1, source_target_pairs={{0,1},{1,0},{2,3},{3,2},{4,5},{5,4},{6,7},{7,6},{8,9},{9,8},{10,11... | collective-permute-start | bytes 798728 | tf_op jit(solution)/shard_map/ppermute | solution.py:312
  7.8 1.3 %prepare.1 = (bf16[8,512,128]{2,1,0:T(8,128)(2,1)S(1)}, bf16[128,128]{1,0:T(8,128)(2,1)S(1)}, bf16[128,128]{1,0:T(8,128)(2,1)S(1)}, bf16[128,128]{1,0:T(8,128)(2...) custom-call(s32[16]{0:T(128)} %length_hbm.1, bf16[64,64,128]{2,1,0:T(8,128)(2,1)} %q_ref.1), custom_call_target="tpu_custom_call" | custom-call | tf_op jit(solution)/shard_map/prepare/pallas_call | solution.py:234
  9.1 0.0 collective-permute-done.refs_3_
  9.1 0.8 %collective-permute-start.2 = (bf16[1040,128]{1,0:T(8,128)(2,1)S(1)}, bf16[1040,128]{1,0:T(8,128)(2,1)S(1)}, u32[]{:S(2)}, u32[]{:S(2)}) collective-permute-start(bf16[1040,128]{1,0:T(8,128)(2,1)S(1)} %collective-permute-done.refs_3_), channel_id=1, source_target_pairs={{0,1},{1,0},{2,3},{3,2},{4,5},{5,4},{6,7},{7,6},{8,9},{9,8},{10,11... | collective-permute-start | bytes 798728 | tf_op jit(solution)/shard_map/ppermute | solution.py:312
  10.0 2.5 %collective-permute-start.5 = (bf16[1040,128]{1,0:T(8,128)(2,1)S(1)}, bf16[1040,128]{1,0:T(8,128)(2,1)S(1)}, u32[]{:S(2)}, u32[]{:S(2)}) collective-permute-start(bf16[1040,128]{1,0:T(8,128)(2,1)S(1)} %get-tuple-element.43), channel_id=1, source_target_pairs={{0,4},{2,6},{4,0},{6,2},{8,12},{10,14},{12,8},{14,10},{16,20},{18,... | collective-permute-start | bytes 798728 | tf_op jit(solution)/shard_map/ppermute | solution.py:309
  12.5 1.2 %collective-permute-start.4 = (bf16[1040,128]{1,0:T(8,128)(2,1)S(1)}, bf16[1040,128]{1,0:T(8,128)(2,1)S(1)}, u32[]{:S(2)}, u32[]{:S(2)}) collective-permute-start(bf16[1040,128]{1,0:T(8,128)(2,1)S(1)} %get-tuple-element.44), channel_id=1, source_target_pairs={{0,2},{2,0},{4,6},{6,4},{8,10},{10,8},{12,14},{14,12},{16,18},{18,... | collective-permute-start | bytes 798728 | tf_op jit(solution)/shard_map/ppermute | solution.py:309
  13.7 0.0 collective-permute-done.1.refs_4_
  13.7 0.0 collective-permute-done.2.refs_5_
  13.7 1.6 %early.1 = (f32[8,128,512]{2,1,0:T(8,128)S(1)}, f32[8,512]{1,0:T(8,128)S(1)}, f32[8,512]{1,0:T(8,128)S(1)}) custom-call(bf16[8,512,128]{2,1,0:T(8,128)(2,1)S(1)} %get-tuple-element.24.qh_ref, bf16[128,128]{1,0:T(8,128)(2,1)S(1)} %get-tuple-element.27.refs_0_, bf16[128,128]{1,0:T(8,128)(2,1)S(1)} %get-tuple-element.28.refs_1_, ...), custom_call_target="tpu_custom_call" | custom-call | flops 536870912 | bytes 1048576 | tf_op jit(solution)/shard_map/early/pallas_call | solution.py:256
  15.2 0.8 %collective-permute-done.3 = bf16[1040,128]{1,0:T(8,128)(2,1)S(1)} collective-permute-done((bf16[1040,128]{1,0:T(8,128)(2,1)S(1)}, bf16[1040,128]{1,0:T(8,128)(2,1)S(1)}, u32[]{:S(2)}, u32[]{:S(2)}) %collective-permute-start.3) | collective-permute-done | bytes 266272 | tf_op jit(solution)/shard_map/ppermute | solution.py:309
  16.0 3.5 %all_gather.3.both_ref = bf16[2080,128]{1,0:T(8,128)(2,1)S(1)} all-gather(bf16[1040,128]{1,0:T(8,128)(2,1)S(1)} %collective-permute-done.3), channel_id=1, replica_groups=mesh['ctx'=16,'tp'=2] {'tp'}, dimensions={0}, use_global_device_ids=true | all-gather | bytes 798720 | tf_op jit(solution)/shard_map/all_gather | solution.py:324
  19.5 1.9 %middle.1 = (f32[8,128,512]{2,1,0:T(8,128)S(1)}, f32[8,512]{1,0:T(8,128)S(1)}, f32[8,512]{1,0:T(8,128)S(1)}) custom-call(bf16[8,512,128]{2,1,0:T(8,128)(2,1)S(1)} %get-tuple-element.24.qh_ref, bf16[128,128]{1,0:T(8,128)(2,1)S(1)} %get-tuple-element.25.mask_ref, f32[8,128,512]{2,1,0:T(8,128)S(1)} %get-tuple-element.30.acc_ref, ...), custom_call_target="tpu_custom_call" | custom-call | flops 268435456 | bytes 1048576 | tf_op jit(solution)/shard_map/middle/pallas_call | solution.py:271
  21.5 1.4 %collective-permute-done.5.refs_3_ = bf16[1040,128]{1,0:T(8,128)(2,1)S(1)} collective-permute-done((bf16[1040,128]{1,0:T(8,128)(2,1)S(1)}, bf16[1040,128]{1,0:T(8,128)(2,1)S(1)}, u32[]{:S(2)}, u32[]{:S(2)}) %collective-permute-start.5) | collective-permute-done | bytes 266272 | tf_op jit(solution)/shard_map/ppermute | solution.py:309
  22.8 0.0 collective-permute-done.4.refs_2_
  22.8 0.4 %collective-permute-start.6 = (bf16[1040,128]{1,0:T(8,128)(2,1)S(1)}, bf16[1040,128]{1,0:T(8,128)(2,1)S(1)}, u32[]{:S(2)}, u32[]{:S(2)}) collective-permute-start(bf16[1040,128]{1,0:T(8,128)(2,1)S(1)} %collective-permute-done.4.refs_2_), channel_id=1, source_target_pairs={{0,1},{1,0},{2,3},{3,2},{4,5},{5,4},{6,7},{7,6},{8,9},{9,8},{10,11... | collective-permute-start | bytes 798728 | tf_op jit(solution)/shard_map/ppermute | solution.py:312
  23.3 0.1 collective-permute-start.7
  23.4 1.1 %collective-permute-done.6.refs_4_ = bf16[1040,128]{1,0:T(8,128)(2,1)S(1)} collective-permute-done((bf16[1040,128]{1,0:T(8,128)(2,1)S(1)}, bf16[1040,128]{1,0:T(8,128)(2,1)S(1)}, u32[]{:S(2)}, u32[]{:S(2)}) %collective-permute-start.6) | collective-permute-done | bytes 266272 | tf_op jit(solution)/shard_map/ppermute | solution.py:312
  24.4 0.4 %collective-permute-done.7.refs_5_ = bf16[1040,128]{1,0:T(8,128)(2,1)S(1)} collective-permute-done((bf16[1040,128]{1,0:T(8,128)(2,1)S(1)}, bf16[1040,128]{1,0:T(8,128)(2,1)S(1)}, u32[]{:S(2)}, u32[]{:S(2)}) %collective-permute-start.7) | collective-permute-done | bytes 266272 | tf_op jit(solution)/shard_map/ppermute | solution.py:312
  24.8 2.5 %last.1 = bf16[64,64,128]{2,1,0:T(8,128)(2,1)} custom-call(bf16[8,512,128]{2,1,0:T(8,128)(2,1)S(1)} %get-tuple-element.24.qh_ref, f32[8,128,512]{2,1,0:T(8,128)S(1)} %get-tuple-element.35.acc_ref, f32[8,512]{1,0:T(8,128)S(1)} %get-tuple-element.37.top_ref, f32[8,512]{1,0:T(8,128)S(1)} %get-tuple-element.38.sum_ref, ...), custom_call_target="tpu_custom_call" | custom-call | flops 536870912 | bytes 1048576 | tf_op jit(solution)/shard_map/last/pallas_call | solution.py:286
  (1 shorter events, 0.0 us)
Async XLA Ops:
  1.1 8.0 %collective-permute-start = (bf16[1040,128]{1,0:T(8,128)(2,1)S(1)}, bf16[1040,128]{1,0:T(8,128)(2,1)S(1)}, u32[]{:S(2)}, u32[]{:S(2)}) collective-permute-start(bf16[1040,128]{1,0:T(8,128)(2,1)S(1)} %pack.1.refs_2_), channel_id=1, source_target_pairs={{0,8},{2,10},{4,12},{6,14},{8,16},{10,18},{12,20},{14,22},{16,24},... | collective-permute-start | bytes 798728 | tf_op jit(solution)/shard_map/ppermute | solution.py:309
  2.4 13.6 %collective-permute-start.3 = (bf16[1040,128]{1,0:T(8,128)(2,1)S(1)}, bf16[1040,128]{1,0:T(8,128)(2,1)S(1)}, u32[]{:S(2)}, u32[]{:S(2)}) collective-permute-start(bf16[1040,128]{1,0:T(8,128)(2,1)S(1)} %pack.1.refs_2_), channel_id=1, source_target_pairs={{0,6},{2,4},{4,10},{6,8},{8,14},{10,12},{12,18},{14,16},{16,22},{1... | collective-permute-start | bytes 798728 | tf_op jit(solution)/shard_map/ppermute | solution.py:309
  6.5 7.2 %collective-permute-start.1 = (bf16[1040,128]{1,0:T(8,128)(2,1)S(1)}, bf16[1040,128]{1,0:T(8,128)(2,1)S(1)}, u32[]{:S(2)}, u32[]{:S(2)}) collective-permute-start(bf16[1040,128]{1,0:T(8,128)(2,1)S(1)} %pack.1.refs_2_), channel_id=1, source_target_pairs={{0,1},{1,0},{2,3},{3,2},{4,5},{5,4},{6,7},{7,6},{8,9},{9,8},{10,11... | collective-permute-start | bytes 798728 | tf_op jit(solution)/shard_map/ppermute | solution.py:312
  9.1 4.6 %collective-permute-start.2 = (bf16[1040,128]{1,0:T(8,128)(2,1)S(1)}, bf16[1040,128]{1,0:T(8,128)(2,1)S(1)}, u32[]{:S(2)}, u32[]{:S(2)}) collective-permute-start(bf16[1040,128]{1,0:T(8,128)(2,1)S(1)} %collective-permute-done.refs_3_), channel_id=1, source_target_pairs={{0,1},{1,0},{2,3},{3,2},{4,5},{5,4},{6,7},{7,6},{8,9},{9,8},{10,11... | collective-permute-start | bytes 798728 | tf_op jit(solution)/shard_map/ppermute | solution.py:312
  10.0 12.8 %collective-permute-start.5 = (bf16[1040,128]{1,0:T(8,128)(2,1)S(1)}, bf16[1040,128]{1,0:T(8,128)(2,1)S(1)}, u32[]{:S(2)}, u32[]{:S(2)}) collective-permute-start(bf16[1040,128]{1,0:T(8,128)(2,1)S(1)} %get-tuple-element.43), channel_id=1, source_target_pairs={{0,4},{2,6},{4,0},{6,2},{8,12},{10,14},{12,8},{14,10},{16,20},{18,... | collective-permute-start | bytes 798728 | tf_op jit(solution)/shard_map/ppermute | solution.py:309
  12.5 10.4 %collective-permute-start.4 = (bf16[1040,128]{1,0:T(8,128)(2,1)S(1)}, bf16[1040,128]{1,0:T(8,128)(2,1)S(1)}, u32[]{:S(2)}, u32[]{:S(2)}) collective-permute-start(bf16[1040,128]{1,0:T(8,128)(2,1)S(1)} %get-tuple-element.44), channel_id=1, source_target_pairs={{0,2},{2,0},{4,6},{6,4},{8,10},{10,8},{12,14},{14,12},{16,18},{18,... | collective-permute-start | bytes 798728 | tf_op jit(solution)/shard_map/ppermute | solution.py:309
  22.8 1.6 %collective-permute-start.6 = (bf16[1040,128]{1,0:T(8,128)(2,1)S(1)}, bf16[1040,128]{1,0:T(8,128)(2,1)S(1)}, u32[]{:S(2)}, u32[]{:S(2)}) collective-permute-start(bf16[1040,128]{1,0:T(8,128)(2,1)S(1)} %collective-permute-done.4.refs_2_), channel_id=1, source_target_pairs={{0,1},{1,0},{2,3},{3,2},{4,5},{5,4},{6,7},{7,6},{8,9},{9,8},{10,11... | collective-permute-start | bytes 798728 | tf_op jit(solution)/shard_map/ppermute | solution.py:312
  23.3 1.5 %collective-permute-start.7 = (bf16[1040,128]{1,0:T(8,128)(2,1)S(1)}, bf16[1040,128]{1,0:T(8,128)(2,1)S(1)}, u32[]{:S(2)}, u32[]{:S(2)}) collective-permute-start(bf16[1040,128]{1,0:T(8,128)(2,1)S(1)} %collective-permute-done.5.refs_3_), channel_id=1, source_target_pairs={{0,1},{1,0},{2,3},{3,2},{4,5},{5,4},{6,7},{7,6},{8,9},{9,8},{10,11... | collective-permute-start | bytes 798728 | tf_op jit(solution)/shard_map/ppermute | solution.py:312

commit v5 on v4

--- a/solution.py
+++ b/solution.py
@@ -207,7 +207,7 @@
     copies = []
 
     def put(h, cs, acc, top, total):
-        out = (acc / total).T.astype(BF16)
+        out = (acc * (1.0 / total)).astype(BF16).T
         span = slice(cs.start // group, cs.stop // group)
         o_buf[h // 2, span, (h % 2) * group : (h % 2 + 1) * group, :] = out.reshape(span.stop - span.start, group, width)
         if h % 2 == 1 and cs.stop == rows:

time: 27.5 us -> 27.4 us (level)
  transfers between devices with their start and end apart: 8 -> 8, of which waited for: 4 -> 4; matrix products, arithmetic and copies ran while one was open for 0% -> 0% of each run, Pallas kernels for 17% -> 18%
where the time goes in v5:
time: 27.4 us; the launch traced here: 27.3 us
  starting transfers between devices  11.7 us (43%)
  Pallas kernels  8.33 us (30%)
  waiting for transfers between devices  3.6 us (13%)
  blocking collectives  3.51 us (13%)
    ppermute x4, starting transfers between devices, send(): lax.ppermute(value, 'ctx', [(i, j) for i, j in pairs if 0 <= j < ranks])  9.07 us
    all_gather x1, blocking collectives, shards(): both_d = lax.all_gather(from_d, 'tp', axis=0, tiled=True)  3.51 us
    ppermute x4, starting transfers between devices, swap(): return lax.ppermute(value, 'tp', [(0, 1), (1, 0)])  2.65 us
    pallas_call x1, Pallas kernels, last(): pl.pallas_call(functools.partial(last_kernel, count, heads, group), out_s...  2.46 us
    ppermute x4, waiting for transfers between devices, send(): lax.ppermute(value, 'ctx', [(i, j) for i, j in pairs if 0 <= j < ranks])  2.15 us
    pallas_call x1, Pallas kernels, middle(): pl.pallas_call(functools.partial(middle_kernel, heads, group), out_shape=...  1.94 us
    pallas_call x1, Pallas kernels, early(): pl.pallas_call(functools.partial(early_kernel, count, heads, group), out_...  1.56 us
    ppermute x4, waiting for transfers between devices, swap(): return lax.ppermute(value, 'tp', [(0, 1), (1, 0)])  1.45 us
  transfers between devices with their start and end apart: 8, of which 4 were waited for; matrix products, arithmetic and copies ran while one was open for 0% of the time, Pallas kernels for 18%

profile of v5, /device:TPU:9, one launch (start us, length us, event | category | flops | bytes accessed | tf_op | source)
XLA Modules:
  0.0 27.3 jit_solution(3913206267820037455)
XLA Ops:
  0.0 1.1 %pack.1.refs_2_ = bf16[1040,128]{1,0:T(8,128)(2,1)S(1)} custom-call(bf16[64,8,128]{2,1,0:T(8,128)(2,1)} %k_ref.1, bf16[64,8,128]{2,1,0:T(8,128)(2,1)} %v_ref.1, bf16[1,4]{1,0:T(2,128)(2,1)} %ks_ref.1, bf16[1,4]{1,0:T(2,128)(2,1)} %vs_ref.1), custom_call_target="tpu_custom_call" | custom-call | tf_op jit(solution)/shard_map/pack/pallas_call | solution.py:43
  1.1 1.3 %collective-permute-start = (bf16[1040,128]{1,0:T(8,128)(2,1)S(1)}, bf16[1040,128]{1,0:T(8,128)(2,1)S(1)}, u32[]{:S(2)}, u32[]{:S(2)}) collective-permute-start(bf16[1040,128]{1,0:T(8,128)(2,1)S(1)} %pack.1.refs_2_), channel_id=1, source_target_pairs={{0,8},{2,10},{4,12},{6,14},{8,16},{10,18},{12,20},{14,22},{16,24},... | collective-permute-start | bytes 798728 | tf_op jit(solution)/shard_map/ppermute | solution.py:309
  2.4 4.1 %collective-permute-start.3 = (bf16[1040,128]{1,0:T(8,128)(2,1)S(1)}, bf16[1040,128]{1,0:T(8,128)(2,1)S(1)}, u32[]{:S(2)}, u32[]{:S(2)}) collective-permute-start(bf16[1040,128]{1,0:T(8,128)(2,1)S(1)} %pack.1.refs_2_), channel_id=1, source_target_pairs={{0,6},{2,4},{4,10},{6,8},{8,14},{10,12},{12,18},{14,16},{16,22},{1... | collective-permute-start | bytes 798728 | tf_op jit(solution)/shard_map/ppermute | solution.py:309
  6.5 1.3 %collective-permute-start.1 = (bf16[1040,128]{1,0:T(8,128)(2,1)S(1)}, bf16[1040,128]{1,0:T(8,128)(2,1)S(1)}, u32[]{:S(2)}, u32[]{:S(2)}) collective-permute-start(bf16[1040,128]{1,0:T(8,128)(2,1)S(1)} %pack.1.refs_2_), channel_id=1, source_target_pairs={{0,1},{1,0},{2,3},{3,2},{4,5},{5,4},{6,7},{7,6},{8,9},{9,8},{10,11... | collective-permute-start | bytes 798728 | tf_op jit(solution)/shard_map/ppermute | solution.py:312
  7.8 1.3 %prepare.1 = (bf16[8,512,128]{2,1,0:T(8,128)(2,1)S(1)}, bf16[128,128]{1,0:T(8,128)(2,1)S(1)}, bf16[128,128]{1,0:T(8,128)(2,1)S(1)}, bf16[128,128]{1,0:T(8,128)(2...) custom-call(s32[16]{0:T(128)} %length_hbm.1, bf16[64,64,128]{2,1,0:T(8,128)(2,1)} %q_ref.1), custom_call_target="tpu_custom_call" | custom-call | tf_op jit(solution)/shard_map/prepare/pallas_call | solution.py:234
  9.1 0.0 collective-permute-done.refs_3_
  9.1 0.8 %collective-permute-start.2 = (bf16[1040,128]{1,0:T(8,128)(2,1)S(1)}, bf16[1040,128]{1,0:T(8,128)(2,1)S(1)}, u32[]{:S(2)}, u32[]{:S(2)}) collective-permute-start(bf16[1040,128]{1,0:T(8,128)(2,1)S(1)} %collective-permute-done.refs_3_), channel_id=1, source_target_pairs={{0,1},{1,0},{2,3},{3,2},{4,5},{5,4},{6,7},{7,6},{8,9},{9,8},{10,11... | collective-permute-start | bytes 798728 | tf_op jit(solution)/shard_map/ppermute | solution.py:312
  10.0 2.5 %collective-permute-start.5 = (bf16[1040,128]{1,0:T(8,128)(2,1)S(1)}, bf16[1040,128]{1,0:T(8,128)(2,1)S(1)}, u32[]{:S(2)}, u32[]{:S(2)}) collective-permute-start(bf16[1040,128]{1,0:T(8,128)(2,1)S(1)} %get-tuple-element.43), channel_id=1, source_target_pairs={{0,4},{2,6},{4,0},{6,2},{8,12},{10,14},{12,8},{14,10},{16,20},{18,... | collective-permute-start | bytes 798728 | tf_op jit(solution)/shard_map/ppermute | solution.py:309
  12.5 1.2 %collective-permute-start.4 = (bf16[1040,128]{1,0:T(8,128)(2,1)S(1)}, bf16[1040,128]{1,0:T(8,128)(2,1)S(1)}, u32[]{:S(2)}, u32[]{:S(2)}) collective-permute-start(bf16[1040,128]{1,0:T(8,128)(2,1)S(1)} %get-tuple-element.44), channel_id=1, source_target_pairs={{0,2},{2,0},{4,6},{6,4},{8,10},{10,8},{12,14},{14,12},{16,18},{18,... | collective-permute-start | bytes 798728 | tf_op jit(solution)/shard_map/ppermute | solution.py:309
  13.7 0.0 collective-permute-done.1.refs_4_
  13.7 0.0 collective-permute-done.2.refs_5_
  13.7 1.6 %early.1 = (f32[8,128,512]{2,1,0:T(8,128)S(1)}, f32[8,512]{1,0:T(8,128)S(1)}, f32[8,512]{1,0:T(8,128)S(1)}) custom-call(bf16[8,512,128]{2,1,0:T(8,128)(2,1)S(1)} %get-tuple-element.24.qh_ref, bf16[128,128]{1,0:T(8,128)(2,1)S(1)} %get-tuple-element.27.refs_0_, bf16[128,128]{1,0:T(8,128)(2,1)S(1)} %get-tuple-element.28.refs_1_, ...), custom_call_target="tpu_custom_call" | custom-call | flops 536870912 | bytes 1048576 | tf_op jit(solution)/shard_map/early/pallas_call | solution.py:256
  15.2 0.8 %collective-permute-done.3 = bf16[1040,128]{1,0:T(8,128)(2,1)S(1)} collective-permute-done((bf16[1040,128]{1,0:T(8,128)(2,1)S(1)}, bf16[1040,128]{1,0:T(8,128)(2,1)S(1)}, u32[]{:S(2)}, u32[]{:S(2)}) %collective-permute-start.3) | collective-permute-done | bytes 266272 | tf_op jit(solution)/shard_map/ppermute | solution.py:309
  16.0 3.5 %all_gather.3.both_ref = bf16[2080,128]{1,0:T(8,128)(2,1)S(1)} all-gather(bf16[1040,128]{1,0:T(8,128)(2,1)S(1)} %collective-permute-done.3), channel_id=1, replica_groups=mesh['ctx'=16,'tp'=2] {'tp'}, dimensions={0}, use_global_device_ids=true | all-gather | bytes 798720 | tf_op jit(solution)/shard_map/all_gather | solution.py:324
  19.5 1.9 %middle.1 = (f32[8,128,512]{2,1,0:T(8,128)S(1)}, f32[8,512]{1,0:T(8,128)S(1)}, f32[8,512]{1,0:T(8,128)S(1)}) custom-call(bf16[8,512,128]{2,1,0:T(8,128)(2,1)S(1)} %get-tuple-element.24.qh_ref, bf16[128,128]{1,0:T(8,128)(2,1)S(1)} %get-tuple-element.25.mask_ref, f32[8,128,512]{2,1,0:T(8,128)S(1)} %get-tuple-element.30.acc_ref, ...), custom_call_target="tpu_custom_call" | custom-call | flops 268435456 | bytes 1048576 | tf_op jit(solution)/shard_map/middle/pallas_call | solution.py:271
  21.5 1.4 %collective-permute-done.5.refs_3_ = bf16[1040,128]{1,0:T(8,128)(2,1)S(1)} collective-permute-done((bf16[1040,128]{1,0:T(8,128)(2,1)S(1)}, bf16[1040,128]{1,0:T(8,128)(2,1)S(1)}, u32[]{:S(2)}, u32[]{:S(2)}) %collective-permute-start.5) | collective-permute-done | bytes 266272 | tf_op jit(solution)/shard_map/ppermute | solution.py:309
  22.8 0.0 collective-permute-done.4.refs_2_
  22.8 0.4 %collective-permute-start.6 = (bf16[1040,128]{1,0:T(8,128)(2,1)S(1)}, bf16[1040,128]{1,0:T(8,128)(2,1)S(1)}, u32[]{:S(2)}, u32[]{:S(2)}) collective-permute-start(bf16[1040,128]{1,0:T(8,128)(2,1)S(1)} %collective-permute-done.4.refs_2_), channel_id=1, source_target_pairs={{0,1},{1,0},{2,3},{3,2},{4,5},{5,4},{6,7},{7,6},{8,9},{9,8},{10,11... | collective-permute-start | bytes 798728 | tf_op jit(solution)/shard_map/ppermute | solution.py:312
  23.3 0.1 collective-permute-start.7
  23.4 1.1 %collective-permute-done.6.refs_4_ = bf16[1040,128]{1,0:T(8,128)(2,1)S(1)} collective-permute-done((bf16[1040,128]{1,0:T(8,128)(2,1)S(1)}, bf16[1040,128]{1,0:T(8,128)(2,1)S(1)}, u32[]{:S(2)}, u32[]{:S(2)}) %collective-permute-start.6) | collective-permute-done | bytes 266272 | tf_op jit(solution)/shard_map/ppermute | solution.py:312
  24.4 0.4 %collective-permute-done.7.refs_5_ = bf16[1040,128]{1,0:T(8,128)(2,1)S(1)} collective-permute-done((bf16[1040,128]{1,0:T(8,128)(2,1)S(1)}, bf16[1040,128]{1,0:T(8,128)(2,1)S(1)}, u32[]{:S(2)}, u32[]{:S(2)}) %collective-permute-start.7) | collective-permute-done | bytes 266272 | tf_op jit(solution)/shard_map/ppermute | solution.py:312
  24.8 2.5 %last.1 = bf16[64,64,128]{2,1,0:T(8,128)(2,1)} custom-call(bf16[8,512,128]{2,1,0:T(8,128)(2,1)S(1)} %get-tuple-element.24.qh_ref, f32[8,128,512]{2,1,0:T(8,128)S(1)} %get-tuple-element.35.acc_ref, f32[8,512]{1,0:T(8,128)S(1)} %get-tuple-element.37.top_ref, f32[8,512]{1,0:T(8,128)S(1)} %get-tuple-element.38.sum_ref, ...), custom_call_target="tpu_custom_call" | custom-call | flops 536870912 | bytes 1048576 | tf_op jit(solution)/shard_map/last/pallas_call | solution.py:286
  (1 shorter events, 0.0 us)
Async XLA Ops:
  1.1 8.0 %collective-permute-start = (bf16[1040,128]{1,0:T(8,128)(2,1)S(1)}, bf16[1040,128]{1,0:T(8,128)(2,1)S(1)}, u32[]{:S(2)}, u32[]{:S(2)}) collective-permute-start(bf16[1040,128]{1,0:T(8,128)(2,1)S(1)} %pack.1.refs_2_), channel_id=1, source_target_pairs={{0,8},{2,10},{4,12},{6,14},{8,16},{10,18},{12,20},{14,22},{16,24},... | collective-permute-start | bytes 798728 | tf_op jit(solution)/shard_map/ppermute | solution.py:309
  2.4 13.6 %collective-permute-start.3 = (bf16[1040,128]{1,0:T(8,128)(2,1)S(1)}, bf16[1040,128]{1,0:T(8,128)(2,1)S(1)}, u32[]{:S(2)}, u32[]{:S(2)}) collective-permute-start(bf16[1040,128]{1,0:T(8,128)(2,1)S(1)} %pack.1.refs_2_), channel_id=1, source_target_pairs={{0,6},{2,4},{4,10},{6,8},{8,14},{10,12},{12,18},{14,16},{16,22},{1... | collective-permute-start | bytes 798728 | tf_op jit(solution)/shard_map/ppermute | solution.py:309
  6.5 7.2 %collective-permute-start.1 = (bf16[1040,128]{1,0:T(8,128)(2,1)S(1)}, bf16[1040,128]{1,0:T(8,128)(2,1)S(1)}, u32[]{:S(2)}, u32[]{:S(2)}) collective-permute-start(bf16[1040,128]{1,0:T(8,128)(2,1)S(1)} %pack.1.refs_2_), channel_id=1, source_target_pairs={{0,1},{1,0},{2,3},{3,2},{4,5},{5,4},{6,7},{7,6},{8,9},{9,8},{10,11... | collective-permute-start | bytes 798728 | tf_op jit(solution)/shard_map/ppermute | solution.py:312
  9.1 4.6 %collective-permute-start.2 = (bf16[1040,128]{1,0:T(8,128)(2,1)S(1)}, bf16[1040,128]{1,0:T(8,128)(2,1)S(1)}, u32[]{:S(2)}, u32[]{:S(2)}) collective-permute-start(bf16[1040,128]{1,0:T(8,128)(2,1)S(1)} %collective-permute-done.refs_3_), channel_id=1, source_target_pairs={{0,1},{1,0},{2,3},{3,2},{4,5},{5,4},{6,7},{7,6},{8,9},{9,8},{10,11... | collective-permute-start | bytes 798728 | tf_op jit(solution)/shard_map/ppermute | solution.py:312
  10.0 12.8 %collective-permute-start.5 = (bf16[1040,128]{1,0:T(8,128)(2,1)S(1)}, bf16[1040,128]{1,0:T(8,128)(2,1)S(1)}, u32[]{:S(2)}, u32[]{:S(2)}) collective-permute-start(bf16[1040,128]{1,0:T(8,128)(2,1)S(1)} %get-tuple-element.43), channel_id=1, source_target_pairs={{0,4},{2,6},{4,0},{6,2},{8,12},{10,14},{12,8},{14,10},{16,20},{18,... | collective-permute-start | bytes 798728 | tf_op jit(solution)/shard_map/ppermute | solution.py:309
  12.5 10.4 %collective-permute-start.4 = (bf16[1040,128]{1,0:T(8,128)(2,1)S(1)}, bf16[1040,128]{1,0:T(8,128)(2,1)S(1)}, u32[]{:S(2)}, u32[]{:S(2)}) collective-permute-start(bf16[1040,128]{1,0:T(8,128)(2,1)S(1)} %get-tuple-element.44), channel_id=1, source_target_pairs={{0,2},{2,0},{4,6},{6,4},{8,10},{10,8},{12,14},{14,12},{16,18},{18,... | collective-permute-start | bytes 798728 | tf_op jit(solution)/shard_map/ppermute | solution.py:309
  22.8 1.6 %collective-permute-start.6 = (bf16[1040,128]{1,0:T(8,128)(2,1)S(1)}, bf16[1040,128]{1,0:T(8,128)(2,1)S(1)}, u32[]{:S(2)}, u32[]{:S(2)}) collective-permute-start(bf16[1040,128]{1,0:T(8,128)(2,1)S(1)} %collective-permute-done.4.refs_2_), channel_id=1, source_target_pairs={{0,1},{1,0},{2,3},{3,2},{4,5},{5,4},{6,7},{7,6},{8,9},{9,8},{10,11... | collective-permute-start | bytes 798728 | tf_op jit(solution)/shard_map/ppermute | solution.py:312
  23.3 1.5 %collective-permute-start.7 = (bf16[1040,128]{1,0:T(8,128)(2,1)S(1)}, bf16[1040,128]{1,0:T(8,128)(2,1)S(1)}, u32[]{:S(2)}, u32[]{:S(2)}) collective-permute-start(bf16[1040,128]{1,0:T(8,128)(2,1)S(1)} %collective-permute-done.5.refs_3_), channel_id=1, source_target_pairs={{0,1},{1,0},{2,3},{3,2},{4,5},{5,4},{6,7},{7,6},{8,9},{9,8},{10,11... | collective-permute-start | bytes 798728 | tf_op jit(solution)/shard_map/ppermute | solution.py:312

commit v6 on v5

--- a/solution.py
+++ b/solution.py
@@ -323,8 +323,11 @@
     from_d, top = lax.optimization_barrier((from_d, top))
     both_d = lax.all_gather(from_d, "tp", axis=0, tiled=True)
     acc, top, total = middle((acc, top, total), qh, masks[GATHERED], both_d)
-    from_x, from_y, top = lax.optimization_barrier((from_x, from_y, top))
-    return last((acc, top, total), qh, masks[3:], [from_x, from_y], [swap(from_x), swap(from_y)])
+    from_x, top = lax.optimization_barrier((from_x, top))
+    from_y, top = lax.optimization_barrier((from_y, top))
+    size = from_x.shape[0]
+    beside_x = swap(jnp.concatenate([from_x, masks[3]], axis=0))[:size]
+    return last((acc, top, total), qh, masks[3:], [from_x, from_y], [beside_x, swap(from_y)])
 
 
 def solution(mesh):

time: 27.4 us -> 27.1 us (0.989)
  waiting for transfers between devices: 3.6 us -> 2.78 us
  starting transfers between devices: 11.7 us -> 12.1 us
    ppermute x4, waiting for transfers between devices: 2.15 us -> 1.63 us  [send(): lax.ppermute(value, 'ctx', [(i, j) for i, j in pairs if 0 <= j < ranks])]
    ppermute x4, starting transfers between devices: 2.65 us -> 3.01 us  [swap(): return lax.ppermute(value, 'tp', [(0, 1), (1, 0)])]
    ppermute x4, waiting for transfers between devices: 1.45 us -> 1.15 us  [swap(): return lax.ppermute(value, 'tp', [(0, 1), (1, 0)])]
  transfers between devices with their start and end apart: 8 -> 8, of which waited for: 4 -> 3; matrix products, arithmetic and copies ran while one was open for 0% -> 0% of each run, Pallas kernels for 18% -> 18%
where the time goes in v6:
time: 27.1 us; the launch traced here: 26.9 us
  starting transfers between devices  12.1 us (45%)
  Pallas kernels  8.34 us (31%)
  blocking collectives  3.51 us (13%)
  waiting for transfers between devices  2.78 us (10%)
    ppermute x4, starting transfers between devices, send(): lax.ppermute(value, 'ctx', [(i, j) for i, j in pairs if 0 <= j < ranks])  9.07 us
    all_gather x1, blocking collectives, shards(): both_d = lax.all_gather(from_d, 'tp', axis=0, tiled=True)  3.51 us
    ppermute x4, starting transfers between devices, swap(): return lax.ppermute(value, 'tp', [(0, 1), (1, 0)])  3.01 us
    pallas_call x1, Pallas kernels, last(): pl.pallas_call(functools.partial(last_kernel, count, heads, group), out_s...  2.46 us
    pallas_call x1, Pallas kernels, middle(): pl.pallas_call(functools.partial(middle_kernel, heads, group), out_shape=...  1.94 us
    ppermute x4, waiting for transfers between devices, send(): lax.ppermute(value, 'ctx', [(i, j) for i, j in pairs if 0 <= j < ranks])  1.63 us
    pallas_call x1, Pallas kernels, early(): pl.pallas_call(functools.partial(early_kernel, count, heads, group), out_...  1.57 us
    pallas_call x1, Pallas kernels, prepare(): pl.pallas_call(functools.partial(prepare_kernel, heads, group), out_shape...  1.29 us
  transfers between devices with their start and end apart: 8, of which 3 were waited for; matrix products, arithmetic and copies ran while one was open for 0% of the time, Pallas kernels for 18%

profile of v6, /device:TPU:9, one launch (start us, length us, event | category | flops | bytes accessed | tf_op | source)
XLA Modules:
  0.0 26.9 jit_solution(9197051352496471901)
XLA Ops:
  0.0 1.1 %pack.1.refs_2_ = bf16[1040,128]{1,0:T(8,128)(2,1)S(1)} custom-call(bf16[64,8,128]{2,1,0:T(8,128)(2,1)} %k_ref.1, bf16[64,8,128]{2,1,0:T(8,128)(2,1)} %v_ref.1, bf16[1,4]{1,0:T(2,128)(2,1)} %ks_ref.1, bf16[1,4]{1,0:T(2,128)(2,1)} %vs_ref.1), custom_call_target="tpu_custom_call" | custom-call | tf_op jit(solution)/shard_map/pack/pallas_call | solution.py:43
  1.1 1.3 %collective-permute-start = (bf16[1040,128]{1,0:T(8,128)(2,1)S(1)}, bf16[1040,128]{1,0:T(8,128)(2,1)S(1)}, u32[]{:S(2)}, u32[]{:S(2)}) collective-permute-start(bf16[1040,128]{1,0:T(8,128)(2,1)S(1)} %pack.1.refs_2_), channel_id=1, source_target_pairs={{0,8},{2,10},{4,12},{6,14},{8,16},{10,18},{12,20},{14,22},{16,24},... | collective-permute-start | bytes 798728 | tf_op jit(solution)/shard_map/ppermute | solution.py:309
  2.4 4.1 %collective-permute-start.3 = (bf16[1040,128]{1,0:T(8,128)(2,1)S(1)}, bf16[1040,128]{1,0:T(8,128)(2,1)S(1)}, u32[]{:S(2)}, u32[]{:S(2)}) collective-permute-start(bf16[1040,128]{1,0:T(8,128)(2,1)S(1)} %pack.1.refs_2_), channel_id=1, source_target_pairs={{0,6},{2,4},{4,10},{6,8},{8,14},{10,12},{12,18},{14,16},{16,22},{1... | collective-permute-start | bytes 798728 | tf_op jit(solution)/shard_map/ppermute | solution.py:309
  6.5 1.3 %collective-permute-start.1 = (bf16[1040,128]{1,0:T(8,128)(2,1)S(1)}, bf16[1040,128]{1,0:T(8,128)(2,1)S(1)}, u32[]{:S(2)}, u32[]{:S(2)}) collective-permute-start(bf16[1040,128]{1,0:T(8,128)(2,1)S(1)} %pack.1.refs_2_), channel_id=1, source_target_pairs={{0,1},{1,0},{2,3},{3,2},{4,5},{5,4},{6,7},{7,6},{8,9},{9,8},{10,11... | collective-permute-start | bytes 798728 | tf_op jit(solution)/shard_map/ppermute | solution.py:312
  7.8 1.3 %prepare.1 = (bf16[8,512,128]{2,1,0:T(8,128)(2,1)S(1)}, bf16[128,128]{1,0:T(8,128)(2,1)S(1)}, bf16[128,128]{1,0:T(8,128)(2,1)S(1)}, bf16[128,128]{1,0:T(8,128)(2...) custom-call(s32[16]{0:T(128)} %length_hbm.1, bf16[64,64,128]{2,1,0:T(8,128)(2,1)} %q_ref.1), custom_call_target="tpu_custom_call" | custom-call | tf_op jit(solution)/shard_map/prepare/pallas_call | solution.py:234
  9.1 0.0 collective-permute-done.refs_3_
  9.1 0.8 %collective-permute-start.2 = (bf16[1040,128]{1,0:T(8,128)(2,1)S(1)}, bf16[1040,128]{1,0:T(8,128)(2,1)S(1)}, u32[]{:S(2)}, u32[]{:S(2)}) collective-permute-start(bf16[1040,128]{1,0:T(8,128)(2,1)S(1)} %collective-permute-done.refs_3_), channel_id=1, source_target_pairs={{0,1},{1,0},{2,3},{3,2},{4,5},{5,4},{6,7},{7,6},{8,9},{9,8},{10,11... | collective-permute-start | bytes 798728 | tf_op jit(solution)/shard_map/ppermute | solution.py:312
  10.0 1.3 %collective-permute-start.5 = (bf16[1040,128]{1,0:T(8,128)(2,1)S(1)}, bf16[1040,128]{1,0:T(8,128)(2,1)S(1)}, u32[]{:S(2)}, u32[]{:S(2)}) collective-permute-start(bf16[1040,128]{1,0:T(8,128)(2,1)S(1)} %get-tuple-element.45), channel_id=1, source_target_pairs={{0,2},{2,0},{4,6},{6,4},{8,10},{10,8},{12,14},{14,12},{16,18},{18,... | collective-permute-start | bytes 798728 | tf_op jit(solution)/shard_map/ppermute | solution.py:309
  11.3 2.4 %collective-permute-start.4 = (bf16[1040,128]{1,0:T(8,128)(2,1)S(1)}, bf16[1040,128]{1,0:T(8,128)(2,1)S(1)}, u32[]{:S(2)}, u32[]{:S(2)}) collective-permute-start(bf16[1040,128]{1,0:T(8,128)(2,1)S(1)} %get-tuple-element.46), channel_id=1, source_target_pairs={{0,4},{2,6},{4,0},{6,2},{8,12},{10,14},{12,8},{14,10},{16,20},{18,... | collective-permute-start | bytes 798728 | tf_op jit(solution)/shard_map/ppermute | solution.py:309
  13.7 0.0 collective-permute-done.1.refs_4_
  13.7 0.0 collective-permute-done.2.refs_5_
  13.7 1.6 %early.1 = (f32[8,128,512]{2,1,0:T(8,128)S(1)}, f32[8,512]{1,0:T(8,128)S(1)}, f32[8,512]{1,0:T(8,128)S(1)}) custom-call(bf16[8,512,128]{2,1,0:T(8,128)(2,1)S(1)} %get-tuple-element.25.qh_ref, bf16[128,128]{1,0:T(8,128)(2,1)S(1)} %get-tuple-element.28.refs_0_, bf16[128,128]{1,0:T(8,128)(2,1)S(1)} %get-tuple-element.29.refs_1_, ...), custom_call_target="tpu_custom_call" | custom-call | flops 536870912 | bytes 1048576 | tf_op jit(solution)/shard_map/early/pallas_call | solution.py:256
  15.2 0.7 %collective-permute-done.3 = bf16[1040,128]{1,0:T(8,128)(2,1)S(1)} collective-permute-done((bf16[1040,128]{1,0:T(8,128)(2,1)S(1)}, bf16[1040,128]{1,0:T(8,128)(2,1)S(1)}, u32[]{:S(2)}, u32[]{:S(2)}) %collective-permute-start.3) | collective-permute-done | bytes 266272 | tf_op jit(solution)/shard_map/ppermute | solution.py:309
  16.0 3.5 %all_gather.3.both_ref = bf16[2080,128]{1,0:T(8,128)(2,1)S(1)} all-gather(bf16[1040,128]{1,0:T(8,128)(2,1)S(1)} %collective-permute-done.3), channel_id=1, replica_groups=mesh['ctx'=16,'tp'=2] {'tp'}, dimensions={0}, use_global_device_ids=true | all-gather | bytes 798720 | tf_op jit(solution)/shard_map/all_gather | solution.py:324
  19.5 1.9 %middle.1 = (f32[8,128,512]{2,1,0:T(8,128)S(1)}, f32[8,512]{1,0:T(8,128)S(1)}, f32[8,512]{1,0:T(8,128)S(1)}) custom-call(bf16[8,512,128]{2,1,0:T(8,128)(2,1)S(1)} %get-tuple-element.25.qh_ref, bf16[128,128]{1,0:T(8,128)(2,1)S(1)} %get-tuple-element.26.mask_ref, f32[8,128,512]{2,1,0:T(8,128)S(1)} %get-tuple-element.31.acc_ref, ...), custom_call_target="tpu_custom_call" | custom-call | flops 268435456 | bytes 1048576 | tf_op jit(solution)/shard_map/middle/pallas_call | solution.py:271
  21.5 0.0 collective-permute-done.5.refs_2_
  21.5 0.4 %collective-permute-start.6 = (bf16[1168,128]{1,0:T(8,128)(2,1)S(1)}, bf16[1168,128]{1,0:T(8,128)(2,1)S(1)}, u32[]{:S(2)}, u32[]{:S(2)}) collective-permute-start(bf16[1168,128]{1,0:T(8,128)(2,1)S(1)} %pad_maximum_fusion), channel_id=1, source_target_pairs={{0,1},{1,0},{2,3},{3,2},{4,5},{5,4},{6,7},{7,6},{8,9},{9,8},{10,11... | collective-permute-start | bytes 897032 | tf_op jit(solution)/shard_map/ppermute | solution.py:312
  21.9 0.9 %collective-permute-done.4.refs_3_ = bf16[1040,128]{1,0:T(8,128)(2,1)S(1)} collective-permute-done((bf16[1040,128]{1,0:T(8,128)(2,1)S(1)}, bf16[1040,128]{1,0:T(8,128)(2,1)S(1)}, u32[]{:S(2)}, u32[]{:S(2)}) %collective-permute-start.4) | collective-permute-done | bytes 266272 | tf_op jit(solution)/shard_map/ppermute | solution.py:309
  22.8 0.4 %collective-permute-start.7 = (bf16[1040,128]{1,0:T(8,128)(2,1)S(1)}, bf16[1040,128]{1,0:T(8,128)(2,1)S(1)}, u32[]{:S(2)}, u32[]{:S(2)}) collective-permute-start(bf16[1040,128]{1,0:T(8,128)(2,1)S(1)} %collective-permute-done.4.refs_3_), channel_id=1, source_target_pairs={{0,1},{1,0},{2,3},{3,2},{4,5},{5,4},{6,7},{7,6},{8,9},{9,8},{10,11... | collective-permute-start | bytes 798728 | tf_op jit(solution)/shard_map/ppermute | solution.py:312
  23.2 0.0 collective-permute-done.6
  23.3 1.1 %collective-permute-done.7.refs_5_ = bf16[1040,128]{1,0:T(8,128)(2,1)S(1)} collective-permute-done((bf16[1040,128]{1,0:T(8,128)(2,1)S(1)}, bf16[1040,128]{1,0:T(8,128)(2,1)S(1)}, u32[]{:S(2)}, u32[]{:S(2)}) %collective-permute-start.7) | collective-permute-done | bytes 266272 | tf_op jit(solution)/shard_map/ppermute | solution.py:312
  24.4 2.5 %last.1 = bf16[64,64,128]{2,1,0:T(8,128)(2,1)} custom-call(bf16[8,512,128]{2,1,0:T(8,128)(2,1)S(1)} %get-tuple-element.25.qh_ref, f32[8,128,512]{2,1,0:T(8,128)S(1)} %get-tuple-element.36.acc_ref, f32[8,512]{1,0:T(8,128)S(1)} %get-tuple-element.39.top_ref, f32[8,512]{1,0:T(8,128)S(1)} %get-tuple-element.40.sum_ref, ...), custom_call_target="tpu_custom_call" | custom-call | flops 536870912 | bytes 1048576 | tf_op jit(solution)/shard_map/last/pallas_call | solution.py:286
  (3 shorter events, 0.1 us)
Async XLA Ops:
  1.1 8.0 %collective-permute-start = (bf16[1040,128]{1,0:T(8,128)(2,1)S(1)}, bf16[1040,128]{1,0:T(8,128)(2,1)S(1)}, u32[]{:S(2)}, u32[]{:S(2)}) collective-permute-start(bf16[1040,128]{1,0:T(8,128)(2,1)S(1)} %pack.1.refs_2_), channel_id=1, source_target_pairs={{0,8},{2,10},{4,12},{6,14},{8,16},{10,18},{12,20},{14,22},{16,24},... | collective-permute-start | bytes 798728 | tf_op jit(solution)/shard_map/ppermute | solution.py:309
  2.4 13.6 %collective-permute-start.3 = (bf16[1040,128]{1,0:T(8,128)(2,1)S(1)}, bf16[1040,128]{1,0:T(8,128)(2,1)S(1)}, u32[]{:S(2)}, u32[]{:S(2)}) collective-permute-start(bf16[1040,128]{1,0:T(8,128)(2,1)S(1)} %pack.1.refs_2_), channel_id=1, source_target_pairs={{0,6},{2,4},{4,10},{6,8},{8,14},{10,12},{12,18},{14,16},{16,22},{1... | collective-permute-start | bytes 798728 | tf_op jit(solution)/shard_map/ppermute | solution.py:309
  6.5 7.2 %collective-permute-start.1 = (bf16[1040,128]{1,0:T(8,128)(2,1)S(1)}, bf16[1040,128]{1,0:T(8,128)(2,1)S(1)}, u32[]{:S(2)}, u32[]{:S(2)}) collective-permute-start(bf16[1040,128]{1,0:T(8,128)(2,1)S(1)} %pack.1.refs_2_), channel_id=1, source_target_pairs={{0,1},{1,0},{2,3},{3,2},{4,5},{5,4},{6,7},{7,6},{8,9},{9,8},{10,11... | collective-permute-start | bytes 798728 | tf_op jit(solution)/shard_map/ppermute | solution.py:312
  9.1 4.6 %collective-permute-start.2 = (bf16[1040,128]{1,0:T(8,128)(2,1)S(1)}, bf16[1040,128]{1,0:T(8,128)(2,1)S(1)}, u32[]{:S(2)}, u32[]{:S(2)}) collective-permute-start(bf16[1040,128]{1,0:T(8,128)(2,1)S(1)} %collective-permute-done.refs_3_), channel_id=1, source_target_pairs={{0,1},{1,0},{2,3},{3,2},{4,5},{5,4},{6,7},{7,6},{8,9},{9,8},{10,11... | collective-permute-start | bytes 798728 | tf_op jit(solution)/shard_map/ppermute | solution.py:312
  10.0 11.5 %collective-permute-start.5 = (bf16[1040,128]{1,0:T(8,128)(2,1)S(1)}, bf16[1040,128]{1,0:T(8,128)(2,1)S(1)}, u32[]{:S(2)}, u32[]{:S(2)}) collective-permute-start(bf16[1040,128]{1,0:T(8,128)(2,1)S(1)} %get-tuple-element.45), channel_id=1, source_target_pairs={{0,2},{2,0},{4,6},{6,4},{8,10},{10,8},{12,14},{14,12},{16,18},{18,... | collective-permute-start | bytes 798728 | tf_op jit(solution)/shard_map/ppermute | solution.py:309
  11.3 11.5 %collective-permute-start.4 = (bf16[1040,128]{1,0:T(8,128)(2,1)S(1)}, bf16[1040,128]{1,0:T(8,128)(2,1)S(1)}, u32[]{:S(2)}, u32[]{:S(2)}) collective-permute-start(bf16[1040,128]{1,0:T(8,128)(2,1)S(1)} %get-tuple-element.46), channel_id=1, source_target_pairs={{0,4},{2,6},{4,0},{6,2},{8,12},{10,14},{12,8},{14,10},{16,20},{18,... | collective-permute-start | bytes 798728 | tf_op jit(solution)/shard_map/ppermute | solution.py:309
  21.5 1.8 %collective-permute-start.6 = (bf16[1168,128]{1,0:T(8,128)(2,1)S(1)}, bf16[1168,128]{1,0:T(8,128)(2,1)S(1)}, u32[]{:S(2)}, u32[]{:S(2)}) collective-permute-start(bf16[1168,128]{1,0:T(8,128)(2,1)S(1)} %pad_maximum_fusion), channel_id=1, source_target_pairs={{0,1},{1,0},{2,3},{3,2},{4,5},{5,4},{6,7},{7,6},{8,9},{9,8},{10,11... | collective-permute-start | bytes 897032 | tf_op jit(solution)/shard_map/ppermute | solution.py:312
  22.8 1.6 %collective-permute-start.7 = (bf16[1040,128]{1,0:T(8,128)(2,1)S(1)}, bf16[1040,128]{1,0:T(8,128)(2,1)S(1)}, u32[]{:S(2)}, u32[]{:S(2)}) collective-permute-start(bf16[1040,128]{1,0:T(8,128)(2,1)S(1)} %collective-permute-done.4.refs_3_), channel_id=1, source_target_pairs={{0,1},{1,0},{2,3},{3,2},{4,5},{5,4},{6,7},{7,6},{8,9},{9,8},{10,11... | collective-permute-start | bytes 798728 | tf_op jit(solution)/shard_map/ppermute | solution.py:312

commit v7 on v6

--- a/solution.py
+++ b/solution.py
@@ -326,7 +326,7 @@
     from_x, top = lax.optimization_barrier((from_x, top))
     from_y, top = lax.optimization_barrier((from_y, top))
     size = from_x.shape[0]
-    beside_x = swap(jnp.concatenate([from_x, masks[3]], axis=0))[:size]
+    beside_x = swap(jnp.concatenate([from_x, masks[3][:SCALE_ROWS]], axis=0))[:size]
     return last((acc, top, total), qh, masks[3:], [from_x, from_y], [beside_x, swap(from_y)])
 
 

time: 27.1 us -> 27.1 us (level)
  no operation moved by 1% of the time
where the time goes in v7:
time: 27.1 us; the launch traced here: 26.9 us
  starting transfers between devices  12 us (44%)
  Pallas kernels  8.34 us (31%)
  blocking collectives  3.51 us (13%)
  waiting for transfers between devices  2.81 us (10%)
    ppermute x4, starting transfers between devices, send(): lax.ppermute(value, 'ctx', [(i, j) for i, j in pairs if 0 <= j < ranks])  9.07 us
    all_gather x1, blocking collectives, shards(): both_d = lax.all_gather(from_d, 'tp', axis=0, tiled=True)  3.51 us
    ppermute x4, starting transfers between devices, swap(): return lax.ppermute(value, 'tp', [(0, 1), (1, 0)])  2.97 us
    pallas_call x1, Pallas kernels, last(): pl.pallas_call(functools.partial(last_kernel, count, heads, group), out_s...  2.46 us
    pallas_call x1, Pallas kernels, middle(): pl.pallas_call(functools.partial(middle_kernel, heads, group), out_shape=...  1.94 us
    ppermute x4, waiting for transfers between devices, send(): lax.ppermute(value, 'ctx', [(i, j) for i, j in pairs if 0 <= j < ranks])  1.66 us
    pallas_call x1, Pallas kernels, early(): pl.pallas_call(functools.partial(early_kernel, count, heads, group), out_...  1.57 us
    pallas_call x1, Pallas kernels, prepare(): pl.pallas_call(functools.partial(prepare_kernel, heads, group), out_shape...  1.29 us
  transfers between devices with their start and end apart: 8, of which 3 were waited for; matrix products, arithmetic and copies ran while one was open for 0% of the time, Pallas kernels for 18%

profile of v7, /device:TPU:9, one launch (start us, length us, event | category | flops | bytes accessed | tf_op | source)
XLA Modules:
  0.0 26.9 jit_solution(15427700499937719192)
XLA Ops:
  0.0 1.1 %pack.1.refs_2_ = bf16[1040,128]{1,0:T(8,128)(2,1)S(1)} custom-call(bf16[64,8,128]{2,1,0:T(8,128)(2,1)} %k_ref.1, bf16[64,8,128]{2,1,0:T(8,128)(2,1)} %v_ref.1, bf16[1,4]{1,0:T(2,128)(2,1)} %ks_ref.1, bf16[1,4]{1,0:T(2,128)(2,1)} %vs_ref.1), custom_call_target="tpu_custom_call" | custom-call | tf_op jit(solution)/shard_map/pack/pallas_call | solution.py:43
  1.1 1.3 %collective-permute-start = (bf16[1040,128]{1,0:T(8,128)(2,1)S(1)}, bf16[1040,128]{1,0:T(8,128)(2,1)S(1)}, u32[]{:S(2)}, u32[]{:S(2)}) collective-permute-start(bf16[1040,128]{1,0:T(8,128)(2,1)S(1)} %pack.1.refs_2_), channel_id=1, source_target_pairs={{0,8},{2,10},{4,12},{6,14},{8,16},{10,18},{12,20},{14,22},{16,24},... | collective-permute-start | bytes 798728 | tf_op jit(solution)/shard_map/ppermute | solution.py:309
  2.4 1.0 %collective-permute-start.1 = (bf16[1040,128]{1,0:T(8,128)(2,1)S(1)}, bf16[1040,128]{1,0:T(8,128)(2,1)S(1)}, u32[]{:S(2)}, u32[]{:S(2)}) collective-permute-start(bf16[1040,128]{1,0:T(8,128)(2,1)S(1)} %pack.1.refs_2_), channel_id=1, source_target_pairs={{0,1},{1,0},{2,3},{3,2},{4,5},{5,4},{6,7},{7,6},{8,9},{9,8},{10,11... | collective-permute-start | bytes 798728 | tf_op jit(solution)/shard_map/ppermute | solution.py:312
  3.4 4.1 %collective-permute-start.3 = (bf16[1040,128]{1,0:T(8,128)(2,1)S(1)}, bf16[1040,128]{1,0:T(8,128)(2,1)S(1)}, u32[]{:S(2)}, u32[]{:S(2)}) collective-permute-start(bf16[1040,128]{1,0:T(8,128)(2,1)S(1)} %pack.1.refs_2_), channel_id=1, source_target_pairs={{0,6},{2,4},{4,10},{6,8},{8,14},{10,12},{12,18},{14,16},{16,22},{1... | collective-permute-start | bytes 798728 | tf_op jit(solution)/shard_map/ppermute | solution.py:309
  7.5 1.3 %prepare.1 = (bf16[8,512,128]{2,1,0:T(8,128)(2,1)S(1)}, bf16[128,128]{1,0:T(8,128)(2,1)S(1)}, bf16[128,128]{1,0:T(8,128)(2,1)S(1)}, bf16[128,128]{1,0:T(8,128)(2...) custom-call(s32[16]{0:T(128)} %length_hbm.1, bf16[64,64,128]{2,1,0:T(8,128)(2,1)} %q_ref.1), custom_call_target="tpu_custom_call" | custom-call | tf_op jit(solution)/shard_map/prepare/pallas_call | solution.py:234
  8.8 0.0 collective-permute-done.refs_3_
  8.8 1.1 %collective-permute-start.2 = (bf16[1040,128]{1,0:T(8,128)(2,1)S(1)}, bf16[1040,128]{1,0:T(8,128)(2,1)S(1)}, u32[]{:S(2)}, u32[]{:S(2)}) collective-permute-start(bf16[1040,128]{1,0:T(8,128)(2,1)S(1)} %collective-permute-done.refs_3_), channel_id=1, source_target_pairs={{0,1},{1,0},{2,3},{3,2},{4,5},{5,4},{6,7},{7,6},{8,9},{9,8},{10,11... | collective-permute-start | bytes 798728 | tf_op jit(solution)/shard_map/ppermute | solution.py:312
  10.0 1.3 %collective-permute-start.5 = (bf16[1040,128]{1,0:T(8,128)(2,1)S(1)}, bf16[1040,128]{1,0:T(8,128)(2,1)S(1)}, u32[]{:S(2)}, u32[]{:S(2)}) collective-permute-start(bf16[1040,128]{1,0:T(8,128)(2,1)S(1)} %get-tuple-element.45), channel_id=1, source_target_pairs={{0,2},{2,0},{4,6},{6,4},{8,10},{10,8},{12,14},{14,12},{16,18},{18,... | collective-permute-start | bytes 798728 | tf_op jit(solution)/shard_map/ppermute | solution.py:309
  11.3 2.4 %collective-permute-start.4 = (bf16[1040,128]{1,0:T(8,128)(2,1)S(1)}, bf16[1040,128]{1,0:T(8,128)(2,1)S(1)}, u32[]{:S(2)}, u32[]{:S(2)}) collective-permute-start(bf16[1040,128]{1,0:T(8,128)(2,1)S(1)} %get-tuple-element.46), channel_id=1, source_target_pairs={{0,4},{2,6},{4,0},{6,2},{8,12},{10,14},{12,8},{14,10},{16,20},{18,... | collective-permute-start | bytes 798728 | tf_op jit(solution)/shard_map/ppermute | solution.py:309
  13.7 0.0 collective-permute-done.1.refs_4_
  13.7 0.0 collective-permute-done.2.refs_5_
  13.7 1.6 %early.1 = (f32[8,128,512]{2,1,0:T(8,128)S(1)}, f32[8,512]{1,0:T(8,128)S(1)}, f32[8,512]{1,0:T(8,128)S(1)}) custom-call(bf16[8,512,128]{2,1,0:T(8,128)(2,1)S(1)} %get-tuple-element.25.qh_ref, bf16[128,128]{1,0:T(8,128)(2,1)S(1)} %get-tuple-element.28.refs_0_, bf16[128,128]{1,0:T(8,128)(2,1)S(1)} %get-tuple-element.29.refs_1_, ...), custom_call_target="tpu_custom_call" | custom-call | flops 536870912 | bytes 1048576 | tf_op jit(solution)/shard_map/early/pallas_call | solution.py:256
  15.2 0.7 %collective-permute-done.3 = bf16[1040,128]{1,0:T(8,128)(2,1)S(1)} collective-permute-done((bf16[1040,128]{1,0:T(8,128)(2,1)S(1)}, bf16[1040,128]{1,0:T(8,128)(2,1)S(1)}, u32[]{:S(2)}, u32[]{:S(2)}) %collective-permute-start.3) | collective-permute-done | bytes 266272 | tf_op jit(solution)/shard_map/ppermute | solution.py:309
  16.0 3.5 %all_gather.3.both_ref = bf16[2080,128]{1,0:T(8,128)(2,1)S(1)} all-gather(bf16[1040,128]{1,0:T(8,128)(2,1)S(1)} %collective-permute-done.3), channel_id=1, replica_groups=mesh['ctx'=16,'tp'=2] {'tp'}, dimensions={0}, use_global_device_ids=true | all-gather | bytes 798720 | tf_op jit(solution)/shard_map/all_gather | solution.py:324
  19.5 1.9 %middle.1 = (f32[8,128,512]{2,1,0:T(8,128)S(1)}, f32[8,512]{1,0:T(8,128)S(1)}, f32[8,512]{1,0:T(8,128)S(1)}) custom-call(bf16[8,512,128]{2,1,0:T(8,128)(2,1)S(1)} %get-tuple-element.25.qh_ref, bf16[128,128]{1,0:T(8,128)(2,1)S(1)} %get-tuple-element.26.mask_ref, f32[8,128,512]{2,1,0:T(8,128)S(1)} %get-tuple-element.31.acc_ref, ...), custom_call_target="tpu_custom_call" | custom-call | flops 268435456 | bytes 1048576 | tf_op jit(solution)/shard_map/middle/pallas_call | solution.py:271
  21.5 0.0 collective-permute-done.5.refs_2_
  21.5 0.4 %collective-permute-start.6 = (bf16[1056,128]{1,0:T(8,128)(2,1)S(1)}, bf16[1056,128]{1,0:T(8,128)(2,1)S(1)}, u32[]{:S(2)}, u32[]{:S(2)}) collective-permute-start(bf16[1056,128]{1,0:T(8,128)(2,1)S(1)} %pad_maximum_fusion), channel_id=1, source_target_pairs={{0,1},{1,0},{2,3},{3,2},{4,5},{5,4},{6,7},{7,6},{8,9},{9,8},{10,11... | collective-permute-start | bytes 811016 | tf_op jit(solution)/shard_map/ppermute | solution.py:312
  21.9 0.9 %collective-permute-done.4.refs_3_ = bf16[1040,128]{1,0:T(8,128)(2,1)S(1)} collective-permute-done((bf16[1040,128]{1,0:T(8,128)(2,1)S(1)}, bf16[1040,128]{1,0:T(8,128)(2,1)S(1)}, u32[]{:S(2)}, u32[]{:S(2)}) %collective-permute-start.4) | collective-permute-done | bytes 266272 | tf_op jit(solution)/shard_map/ppermute | solution.py:309
  22.8 0.4 %collective-permute-start.7 = (bf16[1040,128]{1,0:T(8,128)(2,1)S(1)}, bf16[1040,128]{1,0:T(8,128)(2,1)S(1)}, u32[]{:S(2)}, u32[]{:S(2)}) collective-permute-start(bf16[1040,128]{1,0:T(8,128)(2,1)S(1)} %collective-permute-done.4.refs_3_), channel_id=1, source_target_pairs={{0,1},{1,0},{2,3},{3,2},{4,5},{5,4},{6,7},{7,6},{8,9},{9,8},{10,11... | collective-permute-start | bytes 798728 | tf_op jit(solution)/shard_map/ppermute | solution.py:312
  23.3 0.0 collective-permute-done.6
  23.3 1.1 %collective-permute-done.7.refs_5_ = bf16[1040,128]{1,0:T(8,128)(2,1)S(1)} collective-permute-done((bf16[1040,128]{1,0:T(8,128)(2,1)S(1)}, bf16[1040,128]{1,0:T(8,128)(2,1)S(1)}, u32[]{:S(2)}, u32[]{:S(2)}) %collective-permute-start.7) | collective-permute-done | bytes 266272 | tf_op jit(solution)/shard_map/ppermute | solution.py:312
  24.4 2.5 %last.1 = bf16[64,64,128]{2,1,0:T(8,128)(2,1)} custom-call(bf16[8,512,128]{2,1,0:T(8,128)(2,1)S(1)} %get-tuple-element.25.qh_ref, f32[8,128,512]{2,1,0:T(8,128)S(1)} %get-tuple-element.36.acc_ref, f32[8,512]{1,0:T(8,128)S(1)} %get-tuple-element.39.top_ref, f32[8,512]{1,0:T(8,128)S(1)} %get-tuple-element.40.sum_ref, ...), custom_call_target="tpu_custom_call" | custom-call | flops 536870912 | bytes 1048576 | tf_op jit(solution)/shard_map/last/pallas_call | solution.py:286
  (4 shorter events, 0.1 us)
Async XLA Ops:
  1.1 7.7 %collective-permute-start = (bf16[1040,128]{1,0:T(8,128)(2,1)S(1)}, bf16[1040,128]{1,0:T(8,128)(2,1)S(1)}, u32[]{:S(2)}, u32[]{:S(2)}) collective-permute-start(bf16[1040,128]{1,0:T(8,128)(2,1)S(1)} %pack.1.refs_2_), channel_id=1, source_target_pairs={{0,8},{2,10},{4,12},{6,14},{8,16},{10,18},{12,20},{14,22},{16,24},... | collective-permute-start | bytes 798728 | tf_op jit(solution)/shard_map/ppermute | solution.py:309
  2.4 11.2 %collective-permute-start.1 = (bf16[1040,128]{1,0:T(8,128)(2,1)S(1)}, bf16[1040,128]{1,0:T(8,128)(2,1)S(1)}, u32[]{:S(2)}, u32[]{:S(2)}) collective-permute-start(bf16[1040,128]{1,0:T(8,128)(2,1)S(1)} %pack.1.refs_2_), channel_id=1, source_target_pairs={{0,1},{1,0},{2,3},{3,2},{4,5},{5,4},{6,7},{7,6},{8,9},{9,8},{10,11... | collective-permute-start | bytes 798728 | tf_op jit(solution)/shard_map/ppermute | solution.py:312
  3.4 12.6 %collective-permute-start.3 = (bf16[1040,128]{1,0:T(8,128)(2,1)S(1)}, bf16[1040,128]{1,0:T(8,128)(2,1)S(1)}, u32[]{:S(2)}, u32[]{:S(2)}) collective-permute-start(bf16[1040,128]{1,0:T(8,128)(2,1)S(1)} %pack.1.refs_2_), channel_id=1, source_target_pairs={{0,6},{2,4},{4,10},{6,8},{8,14},{10,12},{12,18},{14,16},{16,22},{1... | collective-permute-start | bytes 798728 | tf_op jit(solution)/shard_map/ppermute | solution.py:309
  8.8 4.9 %collective-permute-start.2 = (bf16[1040,128]{1,0:T(8,128)(2,1)S(1)}, bf16[1040,128]{1,0:T(8,128)(2,1)S(1)}, u32[]{:S(2)}, u32[]{:S(2)}) collective-permute-start(bf16[1040,128]{1,0:T(8,128)(2,1)S(1)} %collective-permute-done.refs_3_), channel_id=1, source_target_pairs={{0,1},{1,0},{2,3},{3,2},{4,5},{5,4},{6,7},{7,6},{8,9},{9,8},{10,11... | collective-permute-start | bytes 798728 | tf_op jit(solution)/shard_map/ppermute | solution.py:312
  10.0 11.5 %collective-permute-start.5 = (bf16[1040,128]{1,0:T(8,128)(2,1)S(1)}, bf16[1040,128]{1,0:T(8,128)(2,1)S(1)}, u32[]{:S(2)}, u32[]{:S(2)}) collective-permute-start(bf16[1040,128]{1,0:T(8,128)(2,1)S(1)} %get-tuple-element.45), channel_id=1, source_target_pairs={{0,2},{2,0},{4,6},{6,4},{8,10},{10,8},{12,14},{14,12},{16,18},{18,... | collective-permute-start | bytes 798728 | tf_op jit(solution)/shard_map/ppermute | solution.py:309
  11.3 11.6 %collective-permute-start.4 = (bf16[1040,128]{1,0:T(8,128)(2,1)S(1)}, bf16[1040,128]{1,0:T(8,128)(2,1)S(1)}, u32[]{:S(2)}, u32[]{:S(2)}) collective-permute-start(bf16[1040,128]{1,0:T(8,128)(2,1)S(1)} %get-tuple-element.46), channel_id=1, source_target_pairs={{0,4},{2,6},{4,0},{6,2},{8,12},{10,14},{12,8},{14,10},{16,20},{18,... | collective-permute-start | bytes 798728 | tf_op jit(solution)/shard_map/ppermute | solution.py:309
  21.5 1.8 %collective-permute-start.6 = (bf16[1056,128]{1,0:T(8,128)(2,1)S(1)}, bf16[1056,128]{1,0:T(8,128)(2,1)S(1)}, u32[]{:S(2)}, u32[]{:S(2)}) collective-permute-start(bf16[1056,128]{1,0:T(8,128)(2,1)S(1)} %pad_maximum_fusion), channel_id=1, source_target_pairs={{0,1},{1,0},{2,3},{3,2},{4,5},{5,4},{6,7},{7,6},{8,9},{9,8},{10,11... | collective-permute-start | bytes 811016 | tf_op jit(solution)/shard_map/ppermute | solution.py:312
  22.8 1.6 %collective-permute-start.7 = (bf16[1040,128]{1,0:T(8,128)(2,1)S(1)}, bf16[1040,128]{1,0:T(8,128)(2,1)S(1)}, u32[]{:S(2)}, u32[]{:S(2)}) collective-permute-start(bf16[1040,128]{1,0:T(8,128)(2,1)S(1)} %collective-permute-done.4.refs_3_), channel_id=1, source_target_pairs={{0,1},{1,0},{2,3},{3,2},{4,5},{5,4},{6,7},{7,6},{8,9},{9,8},{10,11... | collective-permute-start | bytes 798728 | tf_op jit(solution)/shard_map/ppermute | solution.py:312

commit v8 on v7

--- a/solution.py
+++ b/solution.py
@@ -210,9 +210,10 @@
         out = (acc * (1.0 / total)).astype(BF16).T
         span = slice(cs.start // group, cs.stop // group)
         o_buf[h // 2, span, (h % 2) * group : (h % 2 + 1) * group, :] = out.reshape(span.stop - span.start, group, width)
-        if h % 2 == 1 and cs.stop == rows:
-            g = h // 2
-            copies.append(pltpu.make_async_copy(o_buf.at[g], out_ref.at[:, pl.ds(g * pair, pair), :], o_sem.at[g]))
+        if h % 2 == 1:
+            g, at = h // 2, pl.ds(span.start, span.stop - span.start)
+            target = out_ref.at[at, pl.ds(g * pair, pair), :]
+            copies.append(pltpu.make_async_copy(o_buf.at[g, at], target, o_sem.at[len(copies)]))
             copies[-1].start()
 
     attend_blocks(
@@ -290,7 +291,7 @@
         out_specs=pl.BlockSpec(memory_space=HBM),
         scratch_shapes=[
             pltpu.VMEM((heads // 2, tokens, 2 * group, width), BF16),
-            pltpu.SemaphoreType.DMA((heads // 2,)),
+            pltpu.SemaphoreType.DMA((heads // 2 * (rows // min(CHUNK, rows)),)),
         ],
         compiler_params=pltpu.CompilerParams(vmem_limit_bytes=24 * 2**20),
         cost_estimate=cost(tokens, heads * group, width, count),

time: 27.1 us -> 27.1 us (level)
  no operation moved by 1% of the time
where the time goes in v8:
time: 27.1 us; the launch traced here: 26.9 us
  starting transfers between devices  12 us (44%)
  Pallas kernels  8.35 us (31%)
  blocking collectives  3.51 us (13%)
  waiting for transfers between devices  2.81 us (10%)
    ppermute x4, starting transfers between devices, send(): lax.ppermute(value, 'ctx', [(i, j) for i, j in pairs if 0 <= j < ranks])  9.07 us
    all_gather x1, blocking collectives, shards(): both_d = lax.all_gather(from_d, 'tp', axis=0, tiled=True)  3.51 us
    ppermute x4, starting transfers between devices, swap(): return lax.ppermute(value, 'tp', [(0, 1), (1, 0)])  2.97 us
    pallas_call x1, Pallas kernels, last(): pl.pallas_call(functools.partial(last_kernel, count, heads, group), out_s...  2.46 us
    pallas_call x1, Pallas kernels, middle(): pl.pallas_call(functools.partial(middle_kernel, heads, group), out_shape=...  1.94 us
    ppermute x4, waiting for transfers between devices, send(): lax.ppermute(value, 'ctx', [(i, j) for i, j in pairs if 0 <= j < ranks])  1.66 us
    pallas_call x1, Pallas kernels, early(): pl.pallas_call(functools.partial(early_kernel, count, heads, group), out_...  1.57 us
    pallas_call x1, Pallas kernels, prepare(): pl.pallas_call(functools.partial(prepare_kernel, heads, group), out_shape...  1.29 us
  transfers between devices with their start and end apart: 8, of which 3 were waited for; matrix products, arithmetic and copies ran while one was open for 0% of the time, Pallas kernels for 18%

profile of v8, /device:TPU:9, one launch (start us, length us, event | category | flops | bytes accessed | tf_op | source)
XLA Modules:
  0.0 26.9 jit_solution(1444770821913432003)
XLA Ops:
  0.0 1.1 %pack.1.refs_2_ = bf16[1040,128]{1,0:T(8,128)(2,1)S(1)} custom-call(bf16[64,8,128]{2,1,0:T(8,128)(2,1)} %k_ref.1, bf16[64,8,128]{2,1,0:T(8,128)(2,1)} %v_ref.1, bf16[1,4]{1,0:T(2,128)(2,1)} %ks_ref.1, bf16[1,4]{1,0:T(2,128)(2,1)} %vs_ref.1), custom_call_target="tpu_custom_call" | custom-call | tf_op jit(solution)/shard_map/pack/pallas_call | solution.py:43
  1.1 1.3 %collective-permute-start = (bf16[1040,128]{1,0:T(8,128)(2,1)S(1)}, bf16[1040,128]{1,0:T(8,128)(2,1)S(1)}, u32[]{:S(2)}, u32[]{:S(2)}) collective-permute-start(bf16[1040,128]{1,0:T(8,128)(2,1)S(1)} %pack.1.refs_2_), channel_id=1, source_target_pairs={{0,8},{2,10},{4,12},{6,14},{8,16},{10,18},{12,20},{14,22},{16,24},... | collective-permute-start | bytes 798728 | tf_op jit(solution)/shard_map/ppermute | solution.py:310
  2.4 1.0 %collective-permute-start.1 = (bf16[1040,128]{1,0:T(8,128)(2,1)S(1)}, bf16[1040,128]{1,0:T(8,128)(2,1)S(1)}, u32[]{:S(2)}, u32[]{:S(2)}) collective-permute-start(bf16[1040,128]{1,0:T(8,128)(2,1)S(1)} %pack.1.refs_2_), channel_id=1, source_target_pairs={{0,1},{1,0},{2,3},{3,2},{4,5},{5,4},{6,7},{7,6},{8,9},{9,8},{10,11... | collective-permute-start | bytes 798728 | tf_op jit(solution)/shard_map/ppermute | solution.py:313
  3.4 4.1 %collective-permute-start.3 = (bf16[1040,128]{1,0:T(8,128)(2,1)S(1)}, bf16[1040,128]{1,0:T(8,128)(2,1)S(1)}, u32[]{:S(2)}, u32[]{:S(2)}) collective-permute-start(bf16[1040,128]{1,0:T(8,128)(2,1)S(1)} %pack.1.refs_2_), channel_id=1, source_target_pairs={{0,6},{2,4},{4,10},{6,8},{8,14},{10,12},{12,18},{14,16},{16,22},{1... | collective-permute-start | bytes 798728 | tf_op jit(solution)/shard_map/ppermute | solution.py:310
  7.5 1.3 %prepare.1 = (bf16[8,512,128]{2,1,0:T(8,128)(2,1)S(1)}, bf16[128,128]{1,0:T(8,128)(2,1)S(1)}, bf16[128,128]{1,0:T(8,128)(2,1)S(1)}, bf16[128,128]{1,0:T(8,128)(2...) custom-call(s32[16]{0:T(128)} %length_hbm.1, bf16[64,64,128]{2,1,0:T(8,128)(2,1)} %q_ref.1), custom_call_target="tpu_custom_call" | custom-call | tf_op jit(solution)/shard_map/prepare/pallas_call | solution.py:235
  8.8 0.0 collective-permute-done.refs_3_
  8.8 1.1 %collective-permute-start.2 = (bf16[1040,128]{1,0:T(8,128)(2,1)S(1)}, bf16[1040,128]{1,0:T(8,128)(2,1)S(1)}, u32[]{:S(2)}, u32[]{:S(2)}) collective-permute-start(bf16[1040,128]{1,0:T(8,128)(2,1)S(1)} %collective-permute-done.refs_3_), channel_id=1, source_target_pairs={{0,1},{1,0},{2,3},{3,2},{4,5},{5,4},{6,7},{7,6},{8,9},{9,8},{10,11... | collective-permute-start | bytes 798728 | tf_op jit(solution)/shard_map/ppermute | solution.py:313
  10.0 1.3 %collective-permute-start.5 = (bf16[1040,128]{1,0:T(8,128)(2,1)S(1)}, bf16[1040,128]{1,0:T(8,128)(2,1)S(1)}, u32[]{:S(2)}, u32[]{:S(2)}) collective-permute-start(bf16[1040,128]{1,0:T(8,128)(2,1)S(1)} %get-tuple-element.45), channel_id=1, source_target_pairs={{0,2},{2,0},{4,6},{6,4},{8,10},{10,8},{12,14},{14,12},{16,18},{18,... | collective-permute-start | bytes 798728 | tf_op jit(solution)/shard_map/ppermute | solution.py:310
  11.3 2.4 %collective-permute-start.4 = (bf16[1040,128]{1,0:T(8,128)(2,1)S(1)}, bf16[1040,128]{1,0:T(8,128)(2,1)S(1)}, u32[]{:S(2)}, u32[]{:S(2)}) collective-permute-start(bf16[1040,128]{1,0:T(8,128)(2,1)S(1)} %get-tuple-element.46), channel_id=1, source_target_pairs={{0,4},{2,6},{4,0},{6,2},{8,12},{10,14},{12,8},{14,10},{16,20},{18,... | collective-permute-start | bytes 798728 | tf_op jit(solution)/shard_map/ppermute | solution.py:310
  13.7 0.0 collective-permute-done.1.refs_4_
  13.7 0.0 collective-permute-done.2.refs_5_
  13.7 1.6 %early.1 = (f32[8,128,512]{2,1,0:T(8,128)S(1)}, f32[8,512]{1,0:T(8,128)S(1)}, f32[8,512]{1,0:T(8,128)S(1)}) custom-call(bf16[8,512,128]{2,1,0:T(8,128)(2,1)S(1)} %get-tuple-element.25.qh_ref, bf16[128,128]{1,0:T(8,128)(2,1)S(1)} %get-tuple-element.28.refs_0_, bf16[128,128]{1,0:T(8,128)(2,1)S(1)} %get-tuple-element.29.refs_1_, ...), custom_call_target="tpu_custom_call" | custom-call | flops 536870912 | bytes 1048576 | tf_op jit(solution)/shard_map/early/pallas_call | solution.py:257
  15.2 0.7 %collective-permute-done.3 = bf16[1040,128]{1,0:T(8,128)(2,1)S(1)} collective-permute-done((bf16[1040,128]{1,0:T(8,128)(2,1)S(1)}, bf16[1040,128]{1,0:T(8,128)(2,1)S(1)}, u32[]{:S(2)}, u32[]{:S(2)}) %collective-permute-start.3) | collective-permute-done | bytes 266272 | tf_op jit(solution)/shard_map/ppermute | solution.py:310
  16.0 3.5 %all_gather.3.both_ref = bf16[2080,128]{1,0:T(8,128)(2,1)S(1)} all-gather(bf16[1040,128]{1,0:T(8,128)(2,1)S(1)} %collective-permute-done.3), channel_id=1, replica_groups=mesh['ctx'=16,'tp'=2] {'tp'}, dimensions={0}, use_global_device_ids=true | all-gather | bytes 798720 | tf_op jit(solution)/shard_map/all_gather | solution.py:325
  19.5 1.9 %middle.1 = (f32[8,128,512]{2,1,0:T(8,128)S(1)}, f32[8,512]{1,0:T(8,128)S(1)}, f32[8,512]{1,0:T(8,128)S(1)}) custom-call(bf16[8,512,128]{2,1,0:T(8,128)(2,1)S(1)} %get-tuple-element.25.qh_ref, bf16[128,128]{1,0:T(8,128)(2,1)S(1)} %get-tuple-element.26.mask_ref, f32[8,128,512]{2,1,0:T(8,128)S(1)} %get-tuple-element.31.acc_ref, ...), custom_call_target="tpu_custom_call" | custom-call | flops 268435456 | bytes 1048576 | tf_op jit(solution)/shard_map/middle/pallas_call | solution.py:272
  21.5 0.0 collective-permute-done.5.refs_2_
  21.5 0.4 %collective-permute-start.6 = (bf16[1056,128]{1,0:T(8,128)(2,1)S(1)}, bf16[1056,128]{1,0:T(8,128)(2,1)S(1)}, u32[]{:S(2)}, u32[]{:S(2)}) collective-permute-start(bf16[1056,128]{1,0:T(8,128)(2,1)S(1)} %pad_maximum_fusion), channel_id=1, source_target_pairs={{0,1},{1,0},{2,3},{3,2},{4,5},{5,4},{6,7},{7,6},{8,9},{9,8},{10,11... | collective-permute-start | bytes 811016 | tf_op jit(solution)/shard_map/ppermute | solution.py:313
  21.9 0.9 %collective-permute-done.4.refs_3_ = bf16[1040,128]{1,0:T(8,128)(2,1)S(1)} collective-permute-done((bf16[1040,128]{1,0:T(8,128)(2,1)S(1)}, bf16[1040,128]{1,0:T(8,128)(2,1)S(1)}, u32[]{:S(2)}, u32[]{:S(2)}) %collective-permute-start.4) | collective-permute-done | bytes 266272 | tf_op jit(solution)/shard_map/ppermute | solution.py:310
  22.8 0.4 %collective-permute-start.7 = (bf16[1040,128]{1,0:T(8,128)(2,1)S(1)}, bf16[1040,128]{1,0:T(8,128)(2,1)S(1)}, u32[]{:S(2)}, u32[]{:S(2)}) collective-permute-start(bf16[1040,128]{1,0:T(8,128)(2,1)S(1)} %collective-permute-done.4.refs_3_), channel_id=1, source_target_pairs={{0,1},{1,0},{2,3},{3,2},{4,5},{5,4},{6,7},{7,6},{8,9},{9,8},{10,11... | collective-permute-start | bytes 798728 | tf_op jit(solution)/shard_map/ppermute | solution.py:313
  23.3 0.0 collective-permute-done.6
  23.3 1.1 %collective-permute-done.7.refs_5_ = bf16[1040,128]{1,0:T(8,128)(2,1)S(1)} collective-permute-done((bf16[1040,128]{1,0:T(8,128)(2,1)S(1)}, bf16[1040,128]{1,0:T(8,128)(2,1)S(1)}, u32[]{:S(2)}, u32[]{:S(2)}) %collective-permute-start.7) | collective-permute-done | bytes 266272 | tf_op jit(solution)/shard_map/ppermute | solution.py:313
  24.4 2.5 %last.1 = bf16[64,64,128]{2,1,0:T(8,128)(2,1)} custom-call(bf16[8,512,128]{2,1,0:T(8,128)(2,1)S(1)} %get-tuple-element.25.qh_ref, f32[8,128,512]{2,1,0:T(8,128)S(1)} %get-tuple-element.36.acc_ref, f32[8,512]{1,0:T(8,128)S(1)} %get-tuple-element.39.top_ref, f32[8,512]{1,0:T(8,128)S(1)} %get-tuple-element.40.sum_ref, ...), custom_call_target="tpu_custom_call" | custom-call | flops 536870912 | bytes 1048576 | tf_op jit(solution)/shard_map/last/pallas_call | solution.py:287
  (4 shorter events, 0.1 us)
Async XLA Ops:
  1.1 7.7 %collective-permute-start = (bf16[1040,128]{1,0:T(8,128)(2,1)S(1)}, bf16[1040,128]{1,0:T(8,128)(2,1)S(1)}, u32[]{:S(2)}, u32[]{:S(2)}) collective-permute-start(bf16[1040,128]{1,0:T(8,128)(2,1)S(1)} %pack.1.refs_2_), channel_id=1, source_target_pairs={{0,8},{2,10},{4,12},{6,14},{8,16},{10,18},{12,20},{14,22},{16,24},... | collective-permute-start | bytes 798728 | tf_op jit(solution)/shard_map/ppermute | solution.py:310
  2.4 11.2 %collective-permute-start.1 = (bf16[1040,128]{1,0:T(8,128)(2,1)S(1)}, bf16[1040,128]{1,0:T(8,128)(2,1)S(1)}, u32[]{:S(2)}, u32[]{:S(2)}) collective-permute-start(bf16[1040,128]{1,0:T(8,128)(2,1)S(1)} %pack.1.refs_2_), channel_id=1, source_target_pairs={{0,1},{1,0},{2,3},{3,2},{4,5},{5,4},{6,7},{7,6},{8,9},{9,8},{10,11... | collective-permute-start | bytes 798728 | tf_op jit(solution)/shard_map/ppermute | solution.py:313
  3.4 12.6 %collective-permute-start.3 = (bf16[1040,128]{1,0:T(8,128)(2,1)S(1)}, bf16[1040,128]{1,0:T(8,128)(2,1)S(1)}, u32[]{:S(2)}, u32[]{:S(2)}) collective-permute-start(bf16[1040,128]{1,0:T(8,128)(2,1)S(1)} %pack.1.refs_2_), channel_id=1, source_target_pairs={{0,6},{2,4},{4,10},{6,8},{8,14},{10,12},{12,18},{14,16},{16,22},{1... | collective-permute-start | bytes 798728 | tf_op jit(solution)/shard_map/ppermute | solution.py:310
  8.8 4.9 %collective-permute-start.2 = (bf16[1040,128]{1,0:T(8,128)(2,1)S(1)}, bf16[1040,128]{1,0:T(8,128)(2,1)S(1)}, u32[]{:S(2)}, u32[]{:S(2)}) collective-permute-start(bf16[1040,128]{1,0:T(8,128)(2,1)S(1)} %collective-permute-done.refs_3_), channel_id=1, source_target_pairs={{0,1},{1,0},{2,3},{3,2},{4,5},{5,4},{6,7},{7,6},{8,9},{9,8},{10,11... | collective-permute-start | bytes 798728 | tf_op jit(solution)/shard_map/ppermute | solution.py:313
  10.0 11.5 %collective-permute-start.5 = (bf16[1040,128]{1,0:T(8,128)(2,1)S(1)}, bf16[1040,128]{1,0:T(8,128)(2,1)S(1)}, u32[]{:S(2)}, u32[]{:S(2)}) collective-permute-start(bf16[1040,128]{1,0:T(8,128)(2,1)S(1)} %get-tuple-element.45), channel_id=1, source_target_pairs={{0,2},{2,0},{4,6},{6,4},{8,10},{10,8},{12,14},{14,12},{16,18},{18,... | collective-permute-start | bytes 798728 | tf_op jit(solution)/shard_map/ppermute | solution.py:310
  11.3 11.6 %collective-permute-start.4 = (bf16[1040,128]{1,0:T(8,128)(2,1)S(1)}, bf16[1040,128]{1,0:T(8,128)(2,1)S(1)}, u32[]{:S(2)}, u32[]{:S(2)}) collective-permute-start(bf16[1040,128]{1,0:T(8,128)(2,1)S(1)} %get-tuple-element.46), channel_id=1, source_target_pairs={{0,4},{2,6},{4,0},{6,2},{8,12},{10,14},{12,8},{14,10},{16,20},{18,... | collective-permute-start | bytes 798728 | tf_op jit(solution)/shard_map/ppermute | solution.py:310
  21.5 1.8 %collective-permute-start.6 = (bf16[1056,128]{1,0:T(8,128)(2,1)S(1)}, bf16[1056,128]{1,0:T(8,128)(2,1)S(1)}, u32[]{:S(2)}, u32[]{:S(2)}) collective-permute-start(bf16[1056,128]{1,0:T(8,128)(2,1)S(1)} %pad_maximum_fusion), channel_id=1, source_target_pairs={{0,1},{1,0},{2,3},{3,2},{4,5},{5,4},{6,7},{7,6},{8,9},{9,8},{10,11... | collective-permute-start | bytes 811016 | tf_op jit(solution)/shard_map/ppermute | solution.py:313
  22.8 1.6 %collective-permute-start.7 = (bf16[1040,128]{1,0:T(8,128)(2,1)S(1)}, bf16[1040,128]{1,0:T(8,128)(2,1)S(1)}, u32[]{:S(2)}, u32[]{:S(2)}) collective-permute-start(bf16[1040,128]{1,0:T(8,128)(2,1)S(1)} %collective-permute-done.4.refs_3_), channel_id=1, source_target_pairs={{0,1},{1,0},{2,3},{3,2},{4,5},{5,4},{6,7},{7,6},{8,9},{9,8},{10,11... | collective-permute-start | bytes 798728 | tf_op jit(solution)/shard_map/ppermute | solution.py:313
